TPU v7x, 32 devices: a whole 2x2x4 slice. The times are simulated.
32 devices in a mesh: page: 8 (over z, y), seq: 4 (over x, core).
Axes of the slice: x: 2, y: 2, z: 4, core: 2. Of those that a mesh axis runs over, the one named last changes fastest.
Arguments:
- tokens: bfloat16 [8, 512, 1024], P('page', 'seq'), may hold values from -6 to 6
- memory: bfloat16 [8, 512, 1024], P('page', 'seq'), may hold values from -6 to 6
- cotangent: bfloat16 [8, 512, 1024], P('page', 'seq'), may hold values from -6 to 6
- self_qkv: bfloat16 [3, 1024, 1024], P(None, 'page', 'seq'), may hold values from -0.1875 to 0.1875
- self_out: bfloat16 [1024, 1024], P('page', 'seq'), may hold values from -1.5 to 1.5
- cross_qkv: bfloat16 [3, 1024, 1024], P(None, 'page', 'seq'), may hold values from -0.1875 to 0.1875
- cross_out: bfloat16 [1024, 1024], P('page', 'seq'), may hold values from -1.5 to 1.5
- up_weight: bfloat16 [1024, 4096], P('page', 'seq'), may hold values from -0.1875 to 0.1875
- down_weight: bfloat16 [4096, 1024], P('page', 'seq'), may hold values from -0.09375 to 0.09375
- norm_gains: bfloat16 [3, 1024], P(None, ('page', 'seq')), may hold values from 0.099609375 to 1.8984375
- norm_biases: bfloat16 [3, 1024], P(None, ('page', 'seq')), may hold values from -1.796875 to 1.796875
- token_counts: int32 [8], P('page'), may hold values from 256 to 512, as said below
- patch_counts: int32 [8], P('page'), may hold values from 128 to 512, as said below
Outputs:
- mixed: bfloat16 [8, 512, 1024], P('page', 'seq')
- input_grad: float32 [8, 512, 1024], P('page', 'seq')
- memory_grad: float32 [8, 512, 1024], P('page', 'seq')
- self_qkv_grad: float32 [3, 1024, 1024], P(None, 'page', 'seq')
- self_out_grad: float32 [1024, 1024], P('page', 'seq')
- cross_qkv_grad: float32 [3, 1024, 1024], P(None, 'page', 'seq')
- cross_out_grad: float32 [1024, 1024], P('page', 'seq')
- up_grad: float32 [1024, 4096], P('page', 'seq')
- down_grad: float32 [4096, 1024], P('page', 'seq')
- norm_gains_grad: float32 [3, 1024], P(None, ('page', 'seq'))
- norm_biases_grad: float32 [3, 1024], P(None, ('page', 'seq'))
Inputs may be any that keep to these rules, and one draw needn't show every extreme that they name: `token_counts`: some page has exactly 512 live tokens; a page with 512 live tokens has 512 live patches. Live tokens and patches are the first ones of a page. `patch_counts`: some page has exactly 512 live patches.
All inputs are finite; a program needn't handle non-finite values.
Results may differ from a plain program's by a relative error of at most 0.03.
Values may be sent and summed in bfloat16 or wider, within the bound.
A program may use at most 256 MiB of HBM per device.

v0:
```python
import jax
import jax.numpy as jnp
from jax import lax
from jax.sharding import PartitionSpec as P

HEADS = 16
HEAD_DIM = 64


def layer_norm(values, gain_row, bias_row):
    center = values - jnp.mean(values, axis=-1, keepdims=True)
    spread = jnp.mean(center * center, axis=-1, keepdims=True)
    return center * lax.rsqrt(spread + 1e-05) * gain_row + bias_row


def exact_gelu(values):
    return jax.nn.gelu(values, approximate=False)


def block_layout(key_rows, value_rows):
    total_rows = key_rows.shape[0]
    block_rows = min(512, total_rows)
    block_count = total_rows // block_rows
    block_shape = (block_count, block_rows, HEADS, HEAD_DIM)
    starts = jnp.arange(block_count, dtype=jnp.int32) * block_rows
    return (key_rows.reshape(block_shape), value_rows.reshape(block_shape), starts, block_rows)


def masked_scores(query_heads, key_block, block_start, block_rows, live_count, positions):
    scores = jnp.einsum(
        "qhd,khd->hqk", query_heads, key_block, preferred_element_type=jnp.float32
    ) * HEAD_DIM ** (-0.5)
    key_positions = block_start + jnp.arange(block_rows, dtype=jnp.int32)
    allowed = key_positions[None, :] < live_count
    if positions is not None:
        allowed = allowed & (key_positions[None, :] <= positions[:, None])
    return jnp.where(allowed[None], scores, -1e30)


def attend_forward(query_rows, key_rows, value_rows, live_count, positions):
    query_count = query_rows.shape[0]
    query_heads = query_rows.reshape(query_count, HEADS, HEAD_DIM)
    key_blocks, value_blocks, starts, block_rows = block_layout(key_rows, value_rows)

    def gather_stats(running, entry):
        run_max, run_sum = running
        key_block, block_start = entry
        scores = masked_scores(
            query_heads, key_block, block_start, block_rows, live_count, positions
        )
        new_max = jnp.maximum(run_max, jnp.max(scores, axis=-1))
        run_sum = run_sum * jnp.exp(run_max - new_max) + jnp.sum(
            jnp.exp(scores - new_max[:, :, None]), axis=-1
        )
        return ((new_max, run_sum), None)

    start_stats = (
        jnp.full((HEADS, query_count), -1e30, jnp.float32),
        jnp.zeros((HEADS, query_count), jnp.float32),
    )
    stats = lax.scan(gather_stats, start_stats, (key_blocks, starts))[0]
    log_total = stats[0] + jnp.log(stats[1])

    def accumulate(totals, entry):
        key_block, value_block, block_start = entry
        scores = masked_scores(
            query_heads, key_block, block_start, block_rows, live_count, positions
        )
        probabilities = jnp.exp(scores - log_total[:, :, None]).astype(jnp.bfloat16)
        return (
            totals
            + jnp.einsum(
                "hqk,khd->qhd", probabilities, value_block, preferred_element_type=jnp.float32
            ),
            None,
        )

    empty = jnp.zeros((query_count, HEADS, HEAD_DIM), jnp.float32)
    output = lax.scan(accumulate, empty, (key_blocks, value_blocks, starts))[0]
    return (output.reshape(query_count, -1), log_total)


def attend_backward(
    query_rows, key_rows, value_rows, grad_rows, output_rows, log_total, live_count, positions
):
    query_count = query_rows.shape[0]
    head_scale = HEAD_DIM ** (-0.5)
    query_heads = query_rows.reshape(query_count, HEADS, HEAD_DIM)
    grad_heads = grad_rows.reshape(query_count, HEADS, HEAD_DIM)
    key_blocks, value_blocks, starts, block_rows = block_layout(key_rows, value_rows)
    output_heads = output_rows.reshape(query_count, HEADS, HEAD_DIM)
    delta = jnp.einsum("qhd,qhd->hq", grad_heads.astype(jnp.float32), output_heads)

    def backward_step(query_total, entry):
        key_block, value_block, block_start = entry
        scores = masked_scores(
            query_heads, key_block, block_start, block_rows, live_count, positions
        )
        probabilities = jnp.exp(scores - log_total[:, :, None])
        grad_probs = jnp.einsum(
            "qhd,khd->hqk", grad_heads, value_block, preferred_element_type=jnp.float32
        )
        grad_scores = (probabilities * (grad_probs - delta[:, :, None])).astype(jnp.bfloat16)
        query_total = query_total + jnp.einsum(
            "hqk,khd->qhd", grad_scores, key_block, preferred_element_type=jnp.float32
        )
        key_grad = (
            jnp.einsum("hqk,qhd->khd", grad_scores, query_heads, preferred_element_type=jnp.float32)
            * head_scale
        )
        value_grad = jnp.einsum(
            "hqk,qhd->khd",
            probabilities.astype(jnp.bfloat16),
            grad_heads,
            preferred_element_type=jnp.float32,
        )
        merged = jnp.concatenate(
            [key_grad.reshape(block_rows, -1), value_grad.reshape(block_rows, -1)], axis=1
        )
        return (query_total, merged)

    empty = jnp.zeros((query_count, HEADS, HEAD_DIM), jnp.float32)
    query_total, kv_terms = lax.scan(backward_step, empty, (key_blocks, value_blocks, starts))
    return (
        (query_total * head_scale).reshape(query_count, -1),
        kv_terms.reshape(-1, kv_terms.shape[-1]),
    )


def per_device(
    tokens,
    memory,
    cotangent,
    self_qkv,
    self_out,
    cross_qkv,
    cross_out,
    up_weight,
    down_weight,
    norm_gains,
    norm_biases,
    token_counts,
    patch_counts,
):
    col_pieces = (
        lax.all_gather(self_qkv, "seq", axis=2, tiled=True),
        lax.all_gather(self_out, "seq", axis=1, tiled=True),
        lax.all_gather(cross_qkv, "seq", axis=2, tiled=True),
        lax.all_gather(cross_out, "seq", axis=1, tiled=True),
        lax.all_gather(up_weight, "seq", axis=1, tiled=True),
        lax.all_gather(down_weight, "seq", axis=1, tiled=True),
        lax.all_gather(norm_gains, "seq", axis=1, tiled=True),
        lax.all_gather(norm_biases, "seq", axis=1, tiled=True),
    )
    gathered = (
        lax.all_gather(col_pieces[0], "page", axis=1, tiled=True),
        lax.all_gather(col_pieces[1], "page", axis=0, tiled=True),
        lax.all_gather(col_pieces[2], "page", axis=1, tiled=True),
        lax.all_gather(col_pieces[3], "page", axis=0, tiled=True),
        lax.all_gather(col_pieces[4], "page", axis=0, tiled=True),
        lax.all_gather(col_pieces[5], "page", axis=0, tiled=True),
        lax.all_gather(col_pieces[6], "page", axis=1, tiled=True),
        lax.all_gather(col_pieces[7], "page", axis=1, tiled=True),
    )
    w_self, w_self_out, w_cross, w_cross_out, w_up, w_down, gain_all, bias_all = gathered
    gain_rows = gain_all.astype(jnp.float32)
    bias_rows = bias_all.astype(jnp.float32)
    token_rows = tokens.shape[1]
    feature_width = tokens.shape[2]
    positions = lax.axis_index("seq") * token_rows + jnp.arange(token_rows, dtype=jnp.int32)
    token_live = token_counts[0]
    patch_live = patch_counts[0]
    live_rows = (positions < token_live).astype(jnp.float32)[:, None]
    inputs = tokens[0].astype(jnp.float32)
    memory_rows = memory[0]
    first_low = layer_norm(inputs, gain_rows[0], bias_rows[0]).astype(jnp.bfloat16)
    self_proj = jnp.einsum(
        "td,nde->nte", first_low, w_self, preferred_element_type=jnp.float32
    ).astype(jnp.bfloat16)
    queries = self_proj[0]
    keys_all, values_all = (
        lax.all_gather(self_proj[1], "seq", axis=0, tiled=True),
        lax.all_gather(self_proj[2], "seq", axis=0, tiled=True),
    )
    self_output, self_lse = attend_forward(queries, keys_all, values_all, token_live, positions)
    self_low = self_output.astype(jnp.bfloat16)
    after_self = inputs + jnp.dot(self_low, w_self_out, preferred_element_type=jnp.float32)
    second_low = layer_norm(after_self, gain_rows[1], bias_rows[1]).astype(jnp.bfloat16)
    cross_queries = jnp.dot(second_low, w_cross[0], preferred_element_type=jnp.float32).astype(
        jnp.bfloat16
    )
    cross_proj = jnp.einsum(
        "pd,nde->npe", memory_rows, w_cross[1:], preferred_element_type=jnp.float32
    ).astype(jnp.bfloat16)
    patch_keys, patch_values = (
        lax.all_gather(cross_proj[0], "seq", axis=0, tiled=True),
        lax.all_gather(cross_proj[1], "seq", axis=0, tiled=True),
    )
    cross_output, cross_lse = attend_forward(
        cross_queries, patch_keys, patch_values, patch_live, None
    )
    cross_low = cross_output.astype(jnp.bfloat16)
    after_cross = after_self + jnp.dot(cross_low, w_cross_out, preferred_element_type=jnp.float32)
    third_low = layer_norm(after_cross, gain_rows[2], bias_rows[2]).astype(jnp.bfloat16)
    hidden_pre = jnp.dot(third_low, w_up, preferred_element_type=jnp.float32)
    hidden_low = exact_gelu(hidden_pre).astype(jnp.bfloat16)
    result = after_cross + jnp.dot(hidden_low, w_down, preferred_element_type=jnp.float32)
    mixed_rows = (live_rows * result).astype(jnp.bfloat16)[None]
    out_grad = live_rows * cotangent[0].astype(jnp.float32)
    out_low = out_grad.astype(jnp.bfloat16)
    down_grad = jnp.einsum("tf,td->fd", hidden_low, out_low, preferred_element_type=jnp.float32)
    hidden_grad = jnp.einsum("td,fd->tf", out_low, w_down, preferred_element_type=jnp.float32)
    gelu_pull = jax.vjp(exact_gelu, hidden_pre)[1]
    pre_low = gelu_pull(hidden_grad)[0].astype(jnp.bfloat16)
    up_grad = jnp.einsum("td,tf->df", third_low, pre_low, preferred_element_type=jnp.float32)
    third_grad = jnp.einsum("tf,df->td", pre_low, w_up, preferred_element_type=jnp.float32)
    norm_pull = jax.vjp(layer_norm, after_cross, gain_rows[2], bias_rows[2])[1]
    back_cross, gain_third, bias_third = norm_pull(third_grad)
    cross_total = out_grad + back_cross
    cross_branch = cross_total.astype(jnp.bfloat16)
    cross_out_grad = jnp.einsum(
        "td,te->de", cross_low, cross_branch, preferred_element_type=jnp.float32
    )
    cross_attn_grad = jnp.einsum(
        "te,de->td", cross_branch, w_cross_out, preferred_element_type=jnp.float32
    ).astype(jnp.bfloat16)
    cross_query_grad, patch_terms = attend_backward(
        cross_queries,
        patch_keys,
        patch_values,
        cross_attn_grad,
        cross_output,
        cross_lse,
        patch_live,
        None,
    )
    patch_grad = lax.psum_scatter(
        patch_terms.astype(jnp.bfloat16), "seq", scatter_dimension=0, tiled=True
    )
    patch_key_grad = patch_grad[:, :feature_width]
    patch_value_grad = patch_grad[:, feature_width:]
    memory_grad = jnp.einsum(
        "pe,de->pd", patch_key_grad, w_cross[1], preferred_element_type=jnp.float32
    )
    memory_grad = memory_grad + jnp.einsum(
        "pe,de->pd", patch_value_grad, w_cross[2], preferred_element_type=jnp.float32
    )
    cross_query_low = cross_query_grad.astype(jnp.bfloat16)
    cross_qkv_grad = jnp.stack(
        [
            jnp.einsum(
                "td,te->de", second_low, cross_query_low, preferred_element_type=jnp.float32
            ),
            jnp.einsum(
                "pd,pe->de", memory_rows, patch_key_grad, preferred_element_type=jnp.float32
            ),
            jnp.einsum(
                "pd,pe->de", memory_rows, patch_value_grad, preferred_element_type=jnp.float32
            ),
        ]
    )
    second_grad = jnp.einsum(
        "te,de->td", cross_query_low, w_cross[0], preferred_element_type=jnp.float32
    )
    norm_pull = jax.vjp(layer_norm, after_self, gain_rows[1], bias_rows[1])[1]
    back_self, gain_second, bias_second = norm_pull(second_grad)
    self_total = cross_total + back_self
    self_branch = self_total.astype(jnp.bfloat16)
    self_out_grad = jnp.einsum(
        "td,te->de", self_low, self_branch, preferred_element_type=jnp.float32
    )
    self_attn_grad = jnp.einsum(
        "te,de->td", self_branch, w_self_out, preferred_element_type=jnp.float32
    ).astype(jnp.bfloat16)
    query_grad, key_terms = attend_backward(
        queries, keys_all, values_all, self_attn_grad, self_output, self_lse, token_live, positions
    )
    key_value_grad = lax.psum_scatter(
        key_terms.astype(jnp.bfloat16), "seq", scatter_dimension=0, tiled=True
    )
    proj_grads = jnp.stack(
        [
            query_grad.astype(jnp.bfloat16),
            key_value_grad[:, :feature_width],
            key_value_grad[:, feature_width:],
        ]
    )
    self_qkv_grad = jnp.einsum(
        "td,nte->nde", first_low, proj_grads, preferred_element_type=jnp.float32
    )
    first_grad = jnp.einsum("nte,nde->td", proj_grads, w_self, preferred_element_type=jnp.float32)
    norm_pull = jax.vjp(layer_norm, inputs, gain_rows[0], bias_rows[0])[1]
    back_input, gain_first, bias_first = norm_pull(first_grad)
    input_grad = (self_total + back_input)[None]
    page_sums = (
        lax.psum_scatter(
            self_qkv_grad.astype(jnp.bfloat16), "page", scatter_dimension=1, tiled=True
        ).astype(jnp.float32),
        lax.psum_scatter(
            self_out_grad.astype(jnp.bfloat16), "page", scatter_dimension=0, tiled=True
        ).astype(jnp.float32),
        lax.psum_scatter(
            cross_qkv_grad.astype(jnp.bfloat16), "page", scatter_dimension=1, tiled=True
        ).astype(jnp.float32),
        lax.psum_scatter(
            cross_out_grad.astype(jnp.bfloat16), "page", scatter_dimension=0, tiled=True
        ).astype(jnp.float32),
        lax.psum_scatter(
            up_grad.astype(jnp.bfloat16), "page", scatter_dimension=0, tiled=True
        ).astype(jnp.float32),
        lax.psum_scatter(
            down_grad.astype(jnp.bfloat16), "page", scatter_dimension=0, tiled=True
        ).astype(jnp.float32),
        lax.psum_scatter(
            jnp.stack([gain_first, gain_second, gain_third]).astype(jnp.bfloat16),
            "page",
            scatter_dimension=1,
            tiled=True,
        ).astype(jnp.float32),
        lax.psum_scatter(
            jnp.stack([bias_first, bias_second, bias_third]).astype(jnp.bfloat16),
            "page",
            scatter_dimension=1,
            tiled=True,
        ).astype(jnp.float32),
    )
    weight_grads = (
        lax.psum_scatter(
            page_sums[0].astype(jnp.bfloat16), "seq", scatter_dimension=2, tiled=True
        ).astype(jnp.float32),
        lax.psum_scatter(
            page_sums[1].astype(jnp.bfloat16), "seq", scatter_dimension=1, tiled=True
        ).astype(jnp.float32),
        lax.psum_scatter(
            page_sums[2].astype(jnp.bfloat16), "seq", scatter_dimension=2, tiled=True
        ).astype(jnp.float32),
        lax.psum_scatter(
            page_sums[3].astype(jnp.bfloat16), "seq", scatter_dimension=1, tiled=True
        ).astype(jnp.float32),
        lax.psum_scatter(
            page_sums[4].astype(jnp.bfloat16), "seq", scatter_dimension=1, tiled=True
        ).astype(jnp.float32),
        lax.psum_scatter(
            page_sums[5].astype(jnp.bfloat16), "seq", scatter_dimension=1, tiled=True
        ).astype(jnp.float32),
        lax.psum_scatter(
            page_sums[6].astype(jnp.bfloat16), "seq", scatter_dimension=1, tiled=True
        ).astype(jnp.float32),
        lax.psum_scatter(
            page_sums[7].astype(jnp.bfloat16), "seq", scatter_dimension=1, tiled=True
        ).astype(jnp.float32),
    )
    return (
        mixed_rows,
        input_grad,
        memory_grad[None],
        weight_grads[0],
        weight_grads[1],
        weight_grads[2],
        weight_grads[3],
        weight_grads[4],
        weight_grads[5],
        weight_grads[6],
        weight_grads[7],
    )


def solution(mesh):
    return jax.shard_map(
        per_device,
        mesh=mesh,
        in_specs=(
            P("page", "seq", None),
            P("page", "seq", None),
            P("page", "seq", None),
            P(None, "page", "seq"),
            P("page", "seq"),
            P(None, "page", "seq"),
            P("page", "seq"),
            P("page", "seq"),
            P("page", "seq"),
            P(None, ("page", "seq")),
            P(None, ("page", "seq")),
            P("page"),
            P("page"),
        ),
        out_specs=(
            P("page", "seq", None),
            P("page", "seq", None),
            P("page", "seq", None),
            P(None, "page", "seq"),
            P("page", "seq"),
            P(None, "page", "seq"),
            P("page", "seq"),
            P("page", "seq"),
            P("page", "seq"),
            P(None, ("page", "seq")),
            P(None, ("page", "seq")),
        ),
        check_vma=False,
    )
```

profile of v0, /device:TPU:0, one launch (start us, length us, event | category | flops | bytes accessed | tf_op | source)
XLA Modules:
  0.0 1813.1 jit_solution(9640340467947927493)
XLA Ops:
  7.2 11.8 all_gather.64
  20.2 9.2 all_gather.70
  30.9 5.1 all-gather.4
  36.1 5.1 all-gather.5
  41.3 21.0 %all_gather.63 = bf16[3,1024]{1,0:T(4,128)(2,1)S(1)} all-gather(bf16[3,128]{1,0:T(4,128)(2,1)S(1)} %bitcast.291), channel_id=1, replica_groups=mesh['page'=8,'seq'=4] {'page'}, dimensions={1}, use_global_device_ids=true | all-gather | bytes 6912 | tf_op jit(solution)/shard_map/all_gather | solution.py:163
  62.3 16.5 all_gather.61
  79.0 39.8 %all-gather.19.cloned.1.call-done = bf16[3,1024,1024]{2,1,0:T(8,128)(2,1)} async-done(((bf16[3,128,1024]{2,1,0:T(8,128)(2,1)}), bf16[3,1024,1024]{2,1,0:T(8,128)(2,1)}) %all-gather.19.cloned.1.call-update) | async-done | bytes 6291472 | tf_op jit(solution)/shard_map/all_gather | solution.py:156
  118.8 3.9 fusion.14
  124.2 6.3 all_gather.68
  130.5 88.5 %all-gather.23.cloned.1.call-done = bf16[3,1024,1024]{1,2,0:T(8,128)(2,1)} async-done(((bf16[3,128,1024]{1,2,0:T(8,128)(2,1)}), bf16[3,1024,1024]{1,2,0:T(8,128)(2,1)}) %all-gather.23.cloned.1.call-update) | async-done | bytes 6291472 | tf_op jit(solution)/shard_map/all_gather | solution.py:158
  219.0 3.4 fusion.15
  224.1 7.5 all_gather.74
  231.7 4.5 all-gather.27.cloned.1.call-done
  236.2 17.6 all-gather.31.cloned.1.call-done
  256.1 16.5 all-gather.37.cloned.1.call-done
  274.1 17.2 all-gather.35.cloned.1.call-done
  297.8 45.0 %all-gather.21.cloned.1.call-done = bf16[1024,1024]{1,0:T(8,128)(2,1)} async-done(((bf16[128,1024]{1,0:T(8,128)(2,1)}), bf16[1024,1024]{1,0:T(8,128)(2,1)}) %all-gather.21.cloned.1.call-update) | async-done | bytes 2097168 | tf_op jit(solution)/shard_map/all_gather | solution.py:157
  347.8 12.5 all-gather.41.cloned.1.call-done
  364.3 15.0 all-gather.39.cloned.1.call-done
  379.2 4.5 bitcast_convert_fusion
  383.7 46.8 %all-gather.25.cloned.1.call-done = bf16[1024,1024]{1,0:T(8,128)(2,1)} async-done(((bf16[128,1024]{1,0:T(8,128)(2,1)}), bf16[1024,1024]{1,0:T(8,128)(2,1)}) %all-gather.25.cloned.1.call-update) | async-done | bytes 2097168 | tf_op jit(solution)/shard_map/all_gather | solution.py:159
  432.9 123.2 %all-gather.29.cloned.1.call-done = bf16[1024,4096]{1,0:T(8,128)(2,1)} async-done(((bf16[128,4096]{1,0:T(8,128)(2,1)}), bf16[1024,4096]{1,0:T(8,128)(2,1)}) %all-gather.29.cloned.1.call-update) | async-done | bytes 8388624 | tf_op jit(solution)/shard_map/all_gather | solution.py:160
  556.1 9.0 multiply_convert_fusion.4
  565.1 116.2 %all-gather.33.cloned.1.call-done = bf16[4096,1024]{1,0:T(8,128)(2,1)} async-done(((bf16[512,1024]{1,0:T(8,128)(2,1)}), bf16[4096,1024]{1,0:T(8,128)(2,1)}) %all-gather.33.cloned.1.call-update) | async-done | bytes 8388624 | tf_op jit(solution)/shard_map/all_gather | solution.py:161
  681.3 10.0 add_convert_fusion
  691.2 3.0 multiply_reduce_fusion
  700.0 4.1 multiply_convert_fusion.1
  705.7 2.8 multiply_reduce_fusion.1
  714.6 4.6 convolution_convert_fusion.5
  728.6 3.1 pad_maximum_fusion.1
  733.9 3.7 convolution_convert_fusion.4
  739.1 4.0 copy.95
  743.8 3.5 fusion.21
  749.0 12.4 reduce-scatter.31.cloned.1.call-done
  762.5 5.4 fusion.80
  771.0 3.0 convolution_convert_fusion.3
  774.1 3.1 convolution_convert_fusion.2
  777.3 3.1 convert_bitcast_fusion.3
  780.4 15.0 reduce-scatter.55.cloned.1.call-done
  798.0 3.2 pad_maximum_fusion
  801.3 5.7 convert_bitcast_fusion
  807.0 14.8 copy.97
  821.8 10.1 copy.111
  832.0 6.9 convolution_convert_fusion.1
  838.9 5.7 convolution_convert_fusion
  844.7 15.7 reduce-scatter.59.cloned.1.call-done
  860.5 64.0 %reduce-scatter.63.cloned.1.call-done = bf16[128,3]{1,0:T(8,128)(2,1)} async-done(((bf16[1024,3]{1,0:T(8,128)(2,1)}), bf16[128,3]{1,0:T(8,128)(2,1)}) %reduce-scatter.63.cloned.1.call-update) | async-done | bytes 784
  924.5 70.1 %reduce-scatter.35.cloned.1.call-done = bf16[128,1024]{1,0:T(8,128)(2,1)} async-done(((bf16[1024,1024]{1,0:T(8,128)(2,1)}), bf16[128,1024]{1,0:T(8,128)(2,1)}) %reduce-scatter.35.cloned.1.call-update) | async-done | bytes 262160 | tf_op jit(solution)/shard_map/reduce_scatter | solution.py:299
  994.7 70.0 %reduce-scatter.43.cloned.1.call-done = bf16[128,1024]{1,0:T(8,128)(2,1)} async-done(((bf16[1024,1024]{1,0:T(8,128)(2,1)}), bf16[128,1024]{1,0:T(8,128)(2,1)}) %reduce-scatter.43.cloned.1.call-update) | async-done | bytes 262160 | tf_op jit(solution)/shard_map/reduce_scatter | solution.py:305
  1064.8 120.9 %reduce-scatter.39.cloned.1.call-done = bf16[3,128,1024]{2,1,0:T(8,128)(2,1)} async-done(((bf16[3,1024,1024]{2,1,0:T(8,128)(2,1)}), bf16[3,128,1024]{2,1,0:T(8,128)(2,1)}) %reduce-scatter.39.cloned.1.call-update) | async-done | bytes 786448 | tf_op jit(solution)/shard_map/reduce_scatter | solution.py:302
  1185.8 120.4 %reduce-scatter.57.cloned.1.call-done = bf16[128,3072]{1,0:T(8,128)(2,1)} async-done(((bf16[1024,3072]{1,0:T(8,128)(2,1)}), bf16[128,3072]{1,0:T(8,128)(2,1)}) %reduce-scatter.57.cloned.1.call-update) | async-done | bytes 786448
  1306.2 3.6 reshape.314
  1312.3 145.7 %reduce-scatter.47.cloned.1.call-done = bf16[128,4096]{1,0:T(8,128)(2,1)} async-done(((bf16[1024,4096]{1,0:T(8,128)(2,1)}), bf16[128,4096]{1,0:T(8,128)(2,1)}) %reduce-scatter.47.cloned.1.call-update) | async-done | bytes 1048592 | tf_op jit(solution)/shard_map/reduce_scatter | solution.py:308
  1458.3 151.9 %reduce-scatter.51.cloned.1.call-done = bf16[512,1024]{1,0:T(8,128)(2,1)} async-done(((bf16[4096,1024]{1,0:T(8,128)(2,1)}), bf16[512,1024]{1,0:T(8,128)(2,1)}) %reduce-scatter.51.cloned.1.call-update) | async-done | bytes 1048592 | tf_op jit(solution)/shard_map/reduce_scatter | solution.py:311
  1610.2 5.3 fusion.23
  1617.6 2.9 fusion.17
  1621.6 9.4 reduce-scatter.61.cloned.1.call-done
  1632.3 20.4 %reduce-scatter.65.cloned.1.call-done = bf16[32,3]{1,0:T(8,128)(2,1)} async-done(((bf16[128,3]{1,0:T(8,128)(2,1)}), bf16[32,3]{1,0:T(8,128)(2,1)}) %reduce-scatter.65.cloned.1.call-update) | async-done | bytes 208
  1654.0 21.2 %reduce-scatter.37.cloned.1.call-done = bf16[128,256]{1,0:T(8,128)(2,1)} async-done(((bf16[128,1024]{1,0:T(8,128)(2,1)}), bf16[128,256]{1,0:T(8,128)(2,1)}) %reduce-scatter.37.cloned.1.call-update) | async-done | bytes 65552 | tf_op jit(solution)/shard_map/reduce_scatter | solution.py:331
  1676.7 21.0 %reduce-scatter.45.cloned.1.call-done = bf16[128,256]{1,0:T(8,128)(2,1)} async-done(((bf16[128,1024]{1,0:T(8,128)(2,1)}), bf16[128,256]{1,0:T(8,128)(2,1)}) %reduce-scatter.45.cloned.1.call-update) | async-done | bytes 65552 | tf_op jit(solution)/shard_map/reduce_scatter | solution.py:337
  1699.2 24.2 %reduce-scatter.41.cloned.1.call-done = bf16[3,128,256]{2,1,0:T(8,128)(2,1)} async-done(((bf16[3,128,1024]{2,1,0:T(8,128)(2,1)}), bf16[3,128,256]{2,1,0:T(8,128)(2,1)}) %reduce-scatter.41.cloned.1.call-update) | async-done | bytes 196624 | tf_op jit(solution)/shard_map/reduce_scatter | solution.py:334
  1725.1 24.3 %reduce-scatter.33.cloned.1.call-done = bf16[3,128,256]{1,2,0:T(8,128)(2,1)} async-done(((bf16[3,128,1024]{1,2,0:T(8,128)(2,1)}), bf16[3,128,256]{1,2,0:T(8,128)(2,1)}) %reduce-scatter.33.cloned.1.call-update) | async-done | bytes 196624 | tf_op jit(solution)/shard_map/reduce_scatter | solution.py:328
  1751.2 25.6 %reduce-scatter.49.cloned.1.call-done = bf16[128,1024]{1,0:T(8,128)(2,1)} async-done(((bf16[128,4096]{1,0:T(8,128)(2,1)}), bf16[128,1024]{1,0:T(8,128)(2,1)}) %reduce-scatter.49.cloned.1.call-update) | async-done | bytes 262160 | tf_op jit(solution)/shard_map/reduce_scatter | solution.py:340
  1778.7 25.7 %reduce-scatter.53.cloned.1.call-done = bf16[512,256]{1,0:T(8,128)(2,1)} async-done(((bf16[512,1024]{1,0:T(8,128)(2,1)}), bf16[512,256]{1,0:T(8,128)(2,1)}) %reduce-scatter.53.cloned.1.call-update) | async-done | bytes 262160 | tf_op jit(solution)/shard_map/reduce_scatter | solution.py:343
  (247 shorter events, 81.2 us)
Async XLA Ops:
  7.2 211.8 %copy-start = (bf16[1,128,1024]{2,1,0:T(8,128)(2,1)S(1)}, bf16[1,128,1024]{2,1,0:T(8,128)(2,1)}, u32[]{:S(2)}) copy-start(bf16[1,128,1024]{2,1,0:T(8,128)(2,1)} %param.14) | copy-start | bytes 786436
  7.2 23.6 %copy-start.4 = (bf16[1,128,1024]{2,1,0:T(8,128)(2,1)S(1)}, bf16[1,128,1024]{2,1,0:T(8,128)(2,1)}, u32[]{:S(2)}) copy-start(bf16[1,128,1024]{2,1,0:T(8,128)(2,1)} %param.13) | copy-start | bytes 786436
  7.2 111.6 %all-gather.19.cloned.1.call-start = ((), (), s32[]{:S(2)}) async-start(), calls=%async_computation.18 | async-start | bytes 7077888 | tf_op jit(solution)/shard_map/all_gather | solution.py:156
  19.1 11.9 copy-start.42
  19.1 17.0 copy-start.43
  19.1 199.9 %all-gather.23.cloned.1.call-start = ((), (), s32[]{:S(2)}) async-start(), calls=%async_computation.20 | async-start | bytes 7077888 | tf_op jit(solution)/shard_map/all_gather | solution.py:158
  29.4 206.7 %all-gather.27.cloned.1.call-start = ((), (), s32[]{:S(2)}) async-start(), calls=%async_computation.22 | async-start | bytes 1310720 | tf_op jit(solution)/shard_map/all_gather | solution.py:150
  30.2 223.6 %all-gather.31.cloned.1.call-start = ((), (), s32[]{:S(2)}) async-start(), calls=%async_computation.24 | async-start | bytes 1310720 | tf_op jit(solution)/shard_map/all_gather | solution.py:151
  30.7 241.8 %all-gather.37.cloned.1.call-start = ((), (), s32[]{:S(2)}) async-start(), calls=%async_computation.39 | async-start | bytes 1310720 | tf_op jit(solution)/shard_map/all_gather | solution.py:182
  79.0 43.7 %copy-start.44 = (f32[128]{0:T(128)}, f32[128]{0:T(128)S(1)}, u32[]{:S(2)}) copy-start(f32[128]{0:T(128)S(1)} %fusion.34) | copy-start | bytes 1540
  123.6 167.7 %all-gather.35.cloned.1.call-start = ((), (), s32[]{:S(2)}) async-start(), calls=%async_computation.38 | async-start | bytes 1310720 | tf_op jit(solution)/shard_map/all_gather | solution.py:183
  124.1 218.6 %all-gather.21.cloned.1.call-start = ((), (), s32[]{:S(2)}) async-start(), calls=%async_computation.19 | async-start | bytes 2359296 | tf_op jit(solution)/shard_map/all_gather | solution.py:157
  130.5 93.6 %copy-start.35 = (bf16[128,256]{1,0:T(8,128)(2,1)S(1)}, bf16[128,256]{1,0:T(8,128)(2,1)}, u32[]{:S(2)}) copy-start(bf16[128,256]{1,0:T(8,128)(2,1)} %param.19) | copy-start | bytes 196612
  130.5 229.7 %all-gather.41.cloned.1.call-start = ((), (), s32[]{:S(2)}) async-start(), calls=%async_computation.41 | async-start | bytes 1310720 | tf_op jit(solution)/shard_map/all_gather | solution.py:196
  223.3 155.9 %all-gather.39.cloned.1.call-start = ((), (), s32[]{:S(2)}) async-start(), calls=%async_computation.40 | async-start | bytes 1310720 | tf_op jit(solution)/shard_map/all_gather | solution.py:197
  224.0 206.5 %all-gather.25.cloned.1.call-start = ((), (), s32[]{:S(2)}) async-start(), calls=%async_computation.21 | async-start | bytes 2359296 | tf_op jit(solution)/shard_map/all_gather | solution.py:159
  231.6 324.5 %all-gather.29.cloned.1.call-start = ((), (), s32[]{:S(2)}) async-start(), calls=%async_computation.23 | async-start | bytes 9437184 | tf_op jit(solution)/shard_map/all_gather | solution.py:160
  236.2 445.1 %all-gather.33.cloned.1.call-start = ((), (), s32[]{:S(2)}) async-start(), calls=%async_computation.25 | async-start | bytes 9437184 | tf_op jit(solution)/shard_map/all_gather | solution.py:161
  253.8 507.6 %reduce-scatter.31.cloned.1.call-start = ((), (), s32[]{:S(2)}) async-start(), calls=%async_computation.26 | async-start | bytes 2621440 | tf_op jit(solution)/shard_map/reduce_scatter | solution.py:278
  256.0 36.8 %copy-start.18 = (bf16[1,128,1024]{1,2,0:T(8,128)(2,1)}, bf16[1,128,1024]{1,2,0:T(8,128)(2,1)S(1)}, u32[]{:S(2)}) copy-start(bf16[1,128,1024]{1,2,0:T(8,128)(2,1)S(1)} %copy.63) | copy-start | bytes 786436
  274.0 19.7 %copy-start.5 = (bf16[1,512,1024]{1,2,0:T(8,128)(2,1)}, bf16[1,512,1024]{1,2,0:T(8,128)(2,1)S(1)}, u32[]{:S(2)}) copy-start(bf16[1,512,1024]{1,2,0:T(8,128)(2,1)S(1)} %copy.64) | copy-start | bytes 3145732
  292.8 2.2 copy-start.28
  297.8 49.8 %copy-start.32 = (bf16[128,16,64]{0,2,1:T(8,128)(2,1)}, bf16[128,16,64]{0,2,1:T(8,128)(2,1)S(1)}, u32[]{:S(2)}) copy-start(bf16[128,16,64]{0,2,1:T(8,128)(2,1)S(1)} %get-tuple-element.220) | copy-start | bytes 786436
  345.1 17.2 copy-start.46
  345.1 17.2 copy-start.39
  347.8 14.6 copy-start.20
  383.7 172.4 %copy-start.24 = (bf16[128,16,64]{0,2,1:T(8,128)(2,1)}, bf16[128,16,64]{0,2,1:T(8,128)(2,1)S(1)}, u32[]{:S(2)}) copy-start(bf16[128,16,64]{0,2,1:T(8,128)(2,1)S(1)} %get-tuple-element.226) | copy-start | bytes 786436
  556.1 125.1 %copy-start.16 = (bf16[1,128,1024]{2,1,0:T(8,128)(2,1)S(1)}, bf16[1,128,1024]{2,1,0:T(8,128)(2,1)}, u32[]{:S(2)}) copy-start(bf16[1,128,1024]{2,1,0:T(8,128)(2,1)} %param.15) | copy-start | bytes 786436
  681.3 10.0 copy-start.6
  691.2 3.0 copy-start.14
  696.1 8.0 copy-start.17
  698.7 5.3 copy-start.25
  700.0 4.1 copy-start.15
  704.1 4.4 copy-start.9
  705.0 3.5 copy-start.47
  705.6 3.1 copy-start.13
  705.6 3.1 copy-start.38
  714.6 4.6 copy-start.2
  714.6 4.6 copy-start.27
  714.6 4.6 copy-start.29
  719.3 3.3 copy-start.19
  731.7 63.8 %reduce-scatter.55.cloned.1.call-start = ((), (), s32[]{:S(2)}) async-start(), calls=%async_computation.42 | async-start | bytes 2621440
  743.1 117.3 %reduce-scatter.59.cloned.1.call-start = ((), (), s32[]{:S(2)}) async-start(), calls=%async_computation.44 | async-start | bytes 294912
  762.5 5.4 copy-start.30
  762.5 5.4 copy-start.31
  762.5 5.4 copy-start.45
  770.0 154.5 %reduce-scatter.63.cloned.1.call-start = ((), (), s32[]{:S(2)}) async-start(), calls=%async_computation.46 | async-start | bytes 294912
  771.0 223.7 %reduce-scatter.35.cloned.1.call-start = ((), (), s32[]{:S(2)}) async-start(), calls=%async_computation.28 | async-start | bytes 2359296 | tf_op jit(solution)/shard_map/reduce_scatter | solution.py:299
  774.1 3.2 copy-start.41
  774.1 290.6 %reduce-scatter.43.cloned.1.call-start = ((), (), s32[]{:S(2)}) async-start(), calls=%async_computation.32 | async-start | bytes 2359296 | tf_op jit(solution)/shard_map/reduce_scatter | solution.py:305
  777.3 408.4 %reduce-scatter.39.cloned.1.call-start = ((), (), s32[]{:S(2)}) async-start(), calls=%async_computation.30 | async-start | bytes 7077888 | tf_op jit(solution)/shard_map/reduce_scatter | solution.py:302
  795.4 2.6 copy-start.11
  801.3 504.9 %reduce-scatter.57.cloned.1.call-start = ((), (), s32[]{:S(2)}) async-start(), calls=%async_computation.43 | async-start | bytes 7077888
  831.9 626.1 %reduce-scatter.47.cloned.1.call-start = ((), (), s32[]{:S(2)}) async-start(), calls=%async_computation.34 | async-start | bytes 9437184 | tf_op jit(solution)/shard_map/reduce_scatter | solution.py:308
  838.9 771.3 %reduce-scatter.51.cloned.1.call-start = ((), (), s32[]{:S(2)}) async-start(), calls=%async_computation.36 | async-start | bytes 9437184 | tf_op jit(solution)/shard_map/reduce_scatter | solution.py:311
  844.7 786.3 %reduce-scatter.61.cloned.1.call-start = ((), (), s32[]{:S(2)}) async-start(), calls=%async_computation.45 | async-start | bytes 40960
  860.4 792.2 %reduce-scatter.65.cloned.1.call-start = ((), (), s32[]{:S(2)}) async-start(), calls=%async_computation.47 | async-start | bytes 40960
  924.5 750.7 %reduce-scatter.37.cloned.1.call-start = ((), (), s32[]{:S(2)}) async-start(), calls=%async_computation.29 | async-start | bytes 327680 | tf_op jit(solution)/shard_map/reduce_scatter | solution.py:331
  994.7 703.0 %reduce-scatter.45.cloned.1.call-start = ((), (), s32[]{:S(2)}) async-start(), calls=%async_computation.33 | async-start | bytes 327680 | tf_op jit(solution)/shard_map/reduce_scatter | solution.py:337
  1064.8 658.7 %reduce-scatter.41.cloned.1.call-start = ((), (), s32[]{:S(2)}) async-start(), calls=%async_computation.31 | async-start | bytes 983040 | tf_op jit(solution)/shard_map/reduce_scatter | solution.py:334
  1185.7 563.7 %reduce-scatter.33.cloned.1.call-start = ((), (), s32[]{:S(2)}) async-start(), calls=%async_computation.27 | async-start | bytes 983040 | tf_op jit(solution)/shard_map/reduce_scatter | solution.py:328
  1312.3 464.6 %reduce-scatter.49.cloned.1.call-start = ((), (), s32[]{:S(2)}) async-start(), calls=%async_computation.35 | async-start | bytes 1310720 | tf_op jit(solution)/shard_map/reduce_scatter | solution.py:340
  1458.1 346.3 %reduce-scatter.53.cloned.1.call-start = ((), (), s32[]{:S(2)}) async-start(), calls=%async_computation.37 | async-start | bytes 1310720 | tf_op jit(solution)/shard_map/reduce_scatter | solution.py:343
  1617.6 2.9 copy-start.22
  (14 other events, 19.7 us)
Sparse Core Ops, SparseCore 0:
  19.2 99.5 all-gather.18
  120.8 98.1 all-gather.22
  220.6 15.5 all-gather.26
  237.6 16.1 all-gather.30
  255.8 16.7 all-gather.36
  274.5 16.7 all-gather.34
  293.4 49.2 all-gather.20
  344.9 15.3 all-gather.40
  362.4 16.8 all-gather.38
  381.2 49.2 all-gather.24
  432.7 123.4 all-gather.28
  558.1 123.1 all-gather.32
  731.8 29.5 reduce-scatter.30
  763.9 31.4 reduce-scatter.54
  799.2 61.2 reduce-scatter.58
  864.2 60.2 reduce-scatter.62
  927.9 66.7 reduce-scatter.34
  998.1 66.6 reduce-scatter.42
  1068.3 117.3 reduce-scatter.38
  1189.1 117.0 reduce-scatter.56
  1309.9 148.1 reduce-scatter.46
  1462.1 147.9 reduce-scatter.50
  1612.6 18.3 reduce-scatter.60
  1633.3 19.3 reduce-scatter.64
  1655.1 20.0 reduce-scatter.36
  1677.7 20.0 reduce-scatter.44
  1700.1 23.2 reduce-scatter.40
  1726.1 23.2 reduce-scatter.32
  1751.9 24.8 reduce-scatter.48
  1779.4 24.8 reduce-scatter.52
where the time goes:
time: 1820 us; the launch traced here: 1810 us
  waiting for transfers between devices  1500 us (82%)
  matrix products  119 us (7%)
  blocking collectives  82.4 us (5%)
  local copies, waits for them, and re-layouts  64.1 us (4%)
  other arithmetic  25.3 us (1%)
    unnamed x36, waiting for transfers between devices  248 us
    reduce_scatter x1, waiting for transfers between devices, per_device(): lax.psum_scatter(down_grad.astype(jnp.bfloat16), 'page', scatter_dimensio...  152 us
    reduce_scatter x1, waiting for transfers between devices, per_device(): lax.psum_scatter(up_grad.astype(jnp.bfloat16), 'page', scatter_dimension=...  146 us
    all_gather x1, waiting for transfers between devices, per_device(): lax.all_gather(col_pieces[4], 'page', axis=0, tiled=True)  123 us
    reduce_scatter x1, waiting for transfers between devices, per_device(): lax.psum_scatter(cross_qkv_grad.astype(jnp.bfloat16), 'page', scatter_dim...  121 us
    all_gather x1, waiting for transfers between devices, per_device(): lax.all_gather(col_pieces[5], 'page', axis=0, tiled=True)  116 us
    all_gather x1, waiting for transfers between devices, per_device(): lax.all_gather(col_pieces[2], 'page', axis=1, tiled=True)  88.5 us
    reduce_scatter x1, waiting for transfers between devices, per_device(): lax.psum_scatter(self_out_grad.astype(jnp.bfloat16), 'page', scatter_dime...  70.1 us
  transfers between devices with their start and end apart: 30, of which 30 were waited for; matrix products, arithmetic and copies ran while one was open for 8% of the time, Pallas kernels for 0%

commit v1 on v0

v1 whole, which is shorter than its diff:
```python
import jax
import jax.numpy as jnp
from jax import lax
from jax.sharding import PartitionSpec as P

HEADS = 16
HEAD_DIM = 64
F32 = jnp.float32
BF16 = jnp.bfloat16


def layer_norm(values, gain_row, bias_row):
    center = values - jnp.mean(values, axis=-1, keepdims=True)
    spread = jnp.mean(center * center, axis=-1, keepdims=True)
    return center * lax.rsqrt(spread + 1e-05) * gain_row + bias_row


def exact_gelu(values):
    return jax.nn.gelu(values, approximate=False)


def dot(left, right, spec):
    return jnp.einsum(spec, left, right, preferred_element_type=F32)


def heads_of(rows):
    return rows.reshape(rows.shape[0], rows.shape[1] // HEAD_DIM, HEAD_DIM)


def probabilities_of(queries, keys, live, causal):
    scores = dot(heads_of(queries), heads_of(keys), "qhd,khd->hqk") * HEAD_DIM ** (-0.5)
    key_at = lax.broadcasted_iota(jnp.int32, scores.shape[1:], 1)
    allowed = key_at < live
    if causal:
        allowed = allowed & (key_at <= lax.broadcasted_iota(jnp.int32, scores.shape[1:], 0))
    scores = jnp.where(allowed[None], scores, -1e30)
    top = jnp.max(scores, axis=-1, keepdims=True)
    raised = jnp.exp(scores - top)
    return raised / jnp.sum(raised, axis=-1, keepdims=True)


def attend(queries, keys, values, live, causal):
    probs = probabilities_of(queries, keys, live, causal)
    out = dot(probs.astype(BF16), heads_of(values), "hqk,khd->qhd")
    return probs, out.reshape(queries.shape).astype(BF16)


def attend_back(probs, queries, keys, values, grad):
    shape = queries.shape
    scale = HEAD_DIM ** (-0.5)
    q, k, v, g = (heads_of(rows) for rows in (queries, keys, values, grad))
    dp = dot(g, v, "qhd,khd->hqk")
    ds = (probs * (dp - jnp.sum(probs * dp, axis=-1, keepdims=True))).astype(BF16)
    dq = (dot(ds, k, "hqk,khd->qhd") * scale).astype(BF16)
    dk = (dot(ds, q, "hqk,qhd->khd") * scale).astype(BF16)
    dv = dot(probs.astype(BF16), g, "hqk,qhd->khd").astype(BF16)
    return dq.reshape(shape), dk.reshape(keys.shape), dv.reshape(keys.shape)


def per_device(
    tokens,
    memory,
    cotangent,
    self_qkv,
    self_out,
    cross_qkv,
    cross_out,
    up_weight,
    down_weight,
    norm_gains,
    norm_biases,
    token_counts,
    patch_counts,
):
    pages = lax.axis_size("page")
    parts = lax.axis_size("seq")
    here = lax.axis_index("seq")
    ratio = pages // parts
    there = [
        (page * parts + part, ((page % ratio) * parts + part) * parts + page // ratio)
        for page in range(pages)
        for part in range(parts)
    ]
    back = [(b, a) for a, b in there]

    def gather_seq(rows):
        return lax.all_gather(rows, "seq", axis=0, tiled=True)

    def scatter_seq(rows):
        return lax.psum_scatter(
            rows.astype(BF16), "seq", scatter_dimension=0, tiled=True
        ).astype(F32)

    norms = lax.all_gather(
        jnp.concatenate([norm_gains, norm_biases]), ("page", "seq"), axis=1, tiled=True
    ).astype(F32)
    gains, biases = norms[:3], norms[3:]
    moved = lax.ppermute(
        jnp.concatenate([self_out, cross_out, down_weight]), ("page", "seq"), there
    )
    small = self_out.shape[0]
    w_self = lax.all_gather(self_qkv, "page", axis=1, tiled=True)
    tokens_all = gather_seq(tokens[0]).astype(F32)
    memory_all = gather_seq(memory[0])

    def rows_of(piece):
        blocks = lax.all_gather(piece, "page", axis=0, tiled=False)
        rows, cols = piece.shape
        blocks = blocks.reshape(ratio, parts, rows, cols).transpose(0, 2, 1, 3)
        return blocks.reshape(ratio * rows, parts * cols)

    def blocks_of(grad):
        rows, cols = grad.shape[0] // ratio, grad.shape[1] // parts
        blocks = grad.reshape(ratio, rows, parts, cols).transpose(0, 2, 1, 3)
        return blocks.reshape(pages, rows, cols).astype(BF16)

    w_self_out = rows_of(moved[:small])
    w_cross = lax.all_gather(cross_qkv, "page", axis=1, tiled=True)
    w_cross_out = rows_of(moved[small : 2 * small])
    w_up = lax.all_gather(up_weight, "page", axis=0, tiled=True)
    w_down = rows_of(moved[2 * small :])
    cotangent_all = gather_seq(cotangent[0])

    token_rows = tokens.shape[1]
    token_live = token_counts[0]
    patch_live = patch_counts[0]
    every = jnp.arange(tokens_all.shape[0], dtype=jnp.int32)
    dyr = jnp.where((every < token_live)[:, None], cotangent_all, jnp.zeros((), BF16))
    mine = here * token_rows + jnp.arange(token_rows, dtype=jnp.int32)
    live_rows = (mine < token_live)[:, None]
    inputs = tokens[0].astype(F32)
    dy = jnp.where(live_rows, cotangent[0].astype(F32), 0.0)

    a1 = layer_norm(tokens_all, gains[0], biases[0]).astype(BF16)
    q, k, v = (dot(a1, w_self[n], "td,de->te").astype(BF16) for n in range(3))
    p, o = attend(q, k, v, token_live, True)
    x1 = inputs + scatter_seq(dot(o, w_self_out, "td,de->te"))
    a2 = gather_seq(layer_norm(x1, gains[1], biases[1]).astype(BF16))
    kc, vc = (dot(memory_all, w_cross[n], "td,de->te").astype(BF16) for n in (1, 2))
    qc = dot(a2, w_cross[0], "td,de->te").astype(BF16)
    pc, oc = attend(qc, kc, vc, patch_live, False)
    x2 = x1 + scatter_seq(dot(oc, w_cross_out, "td,de->te"))
    a3 = gather_seq(layer_norm(x2, gains[2], biases[2]).astype(BF16))
    u = dot(a3, w_up, "td,df->tf")
    g = exact_gelu(u).astype(BF16)
    result = x2 + scatter_seq(dot(g, w_down, "tf,fd->td"))
    mixed = jnp.where(live_rows, result, 0.0).astype(BF16)[None]

    down_grad = dot(g, dyr, "tf,td->fd")
    dg = dot(dyr, w_down, "td,fd->tf")
    du = jax.vjp(exact_gelu, u)[1](dg)[0].astype(BF16)
    up_grad = dot(a3, du, "td,tf->df")
    da3 = scatter_seq(dot(du, w_up, "tf,df->td"))
    dx2, gain_third, bias_third = jax.vjp(layer_norm, x2, gains[2], biases[2])[1](da3)
    dx2 = dy + dx2
    dz2 = gather_seq(dx2.astype(BF16))
    cross_out_grad = dot(oc, dz2, "td,te->de")
    doc = dot(dz2, w_cross_out, "te,de->td").astype(BF16)
    dqc, dkc, dvc = attend_back(pc, qc, kc, vc, doc)
    da2 = scatter_seq(dot(dqc, w_cross[0], "te,de->td"))
    dx1, gain_second, bias_second = jax.vjp(layer_norm, x1, gains[1], biases[1])[1](da2)
    dx1 = dx2 + dx1
    dz1 = gather_seq(dx1.astype(BF16))
    memory_grad = scatter_seq(
        dot(dkc, w_cross[1], "te,de->td") + dot(dvc, w_cross[2], "te,de->td")
    )
    cross_qkv_grad = jnp.stack(
        [
            dot(a2, dqc, "td,te->de"),
            dot(memory_all, dkc, "td,te->de"),
            dot(memory_all, dvc, "td,te->de"),
        ]
    )
    self_out_grad = dot(o, dz1, "td,te->de")
    dor = dot(dz1, w_self_out, "te,de->td").astype(BF16)
    dq, dk, dv = attend_back(p, q, k, v, dor)
    da1 = scatter_seq(
        dot(dq, w_self[0], "te,de->td")
        + dot(dk, w_self[1], "te,de->td")
        + dot(dv, w_self[2], "te,de->td")
    )
    self_qkv_grad = jnp.stack(
        [dot(a1, dq, "td,te->de"), dot(a1, dk, "td,te->de"), dot(a1, dv, "td,te->de")]
    )
    dx, gain_first, bias_first = jax.vjp(layer_norm, inputs, gains[0], biases[0])[1](da1)
    input_grad = (dx1 + dx)[None]

    def sum_pages(grad, axis):
        return lax.psum_scatter(grad.astype(BF16), "page", scatter_dimension=axis, tiled=True)

    def sum_blocks(grad):
        return lax.psum_scatter(blocks_of(grad), "page", scatter_dimension=0, tiled=False)

    up_out = sum_pages(up_grad, 0).astype(F32)
    down_part = sum_blocks(down_grad)
    cross_out_part = sum_blocks(cross_out_grad)
    cross_out_qkv = sum_pages(cross_qkv_grad, 1).astype(F32)
    self_out_part = sum_blocks(self_out_grad)
    self_out_qkv = sum_pages(self_qkv_grad, 1).astype(F32)
    returned = lax.ppermute(
        jnp.concatenate([self_out_part, cross_out_part, down_part]), ("page", "seq"), back
    ).astype(F32)
    norm_sums = lax.psum_scatter(
        jnp.stack([gain_first, gain_second, gain_third, bias_first, bias_second, bias_third]),
        ("page", "seq"),
        scatter_dimension=1,
        tiled=True,
    )
    return (
        mixed,
        input_grad,
        memory_grad[None],
        self_out_qkv,
        returned[:small],
        cross_out_qkv,
        returned[small : 2 * small],
        up_out,
        returned[2 * small :],
        norm_sums[:3],
        norm_sums[3:],
    )


def solution(mesh):
    rows = P("page", "seq", None)
    stack = P(None, "page", "seq")
    flat = P("page", "seq")
    norm = P(None, ("page", "seq"))
    counts = P("page")
    return jax.shard_map(
        per_device,
        mesh=mesh,
        in_specs=(rows, rows, rows, stack, flat, stack, flat, flat, flat, norm, norm, counts, counts),
        out_specs=(rows, rows, rows, stack, flat, stack, flat, flat, flat, norm, norm),
        check_vma=False,
    )
```

time: 1820 us -> 1170 us (0.64)
  waiting for transfers between devices: 1500 us -> 861 us
  blocking collectives: 82.4 us -> 121 us
  local copies, waits for them, and re-layouts: 64.1 us -> 30.4 us
  matrix products: 119 us -> 86.7 us
    all_gather x12 -> x11, waiting for transfers between devices: 543 us -> 196 us  [the longest x7 74.3 us: gather_seq(): return lax.all_gather(rows, 'seq', axis=0, tiled=True)]
    reduce_scatter x12 -> x13, waiting for transfers between devices: 713 us -> 530 us  [the longest x3 206 us: sum_pages(): lax.psum_scatter(grad.astype(BF16), 'page', scatter_dimension=axis, tiled...]
    unnamed x36 -> x26, waiting for transfers between devices: 248 us -> 135 us
    dot_general x35 -> x40, matrix products: 119 us -> 79.5 us  [dot(): return jnp.einsum(spec, left, right, preferred_element_type=F32)]
    all_gather x8 -> x3, blocking collectives: 82.4 us -> 121 us  [the longest x2 63.8 us: rows_of(): blocks = lax.all_gather(piece, 'page', axis=0, tiled=False)]
    unnamed x109 -> x84, local copies, waits for them, and re-layouts: 48.7 us -> 10.7 us
  transfers between devices with their start and end apart: 30 -> 27, of which waited for: 30 -> 21; matrix products, arithmetic and copies ran while one was open for 8% -> 8% of each run, Pallas kernels for 0% -> 0%
where the time goes in v1:
time: 1170 us; the launch traced here: 1160 us
  waiting for transfers between devices  861 us (74%)
  blocking collectives  121 us (10%)
  matrix products  86.7 us (7%)
  other arithmetic  37.9 us (3%)
  local copies, waits for them, and re-layouts  30.4 us (3%)
  between operations  16.6 us (1%)
    reduce_scatter x3, waiting for transfers between devices, sum_pages(): lax.psum_scatter(grad.astype(BF16), 'page', scatter_dimension=axis, tiled...  206 us
    reduce_scatter x3, waiting for transfers between devices, sum_blocks(): lax.psum_scatter(blocks_of(grad), 'page', scatter_dimension=0, tiled=False)  182 us
    reduce_scatter x7, waiting for transfers between devices, scatter_seq(): lax.psum_scatter(rows.astype(BF16), 'seq', scatter_dimension=0, tiled=True)  142 us
    unnamed x26, waiting for transfers between devices  135 us
    dot_general x40, matrix products, dot(): return jnp.einsum(spec, left, right, preferred_element_type=F32)  79.5 us
    all_gather x7, waiting for transfers between devices, gather_seq(): return lax.all_gather(rows, 'seq', axis=0, tiled=True)  74.3 us
    all_gather x2, blocking collectives, rows_of(): blocks = lax.all_gather(piece, 'page', axis=0, tiled=False)  63.8 us
    all_gather x1, blocking collectives, per_device(): lax.all_gather(jnp.concatenate([norm_gains, norm_biases]), ('page', 'seq'...  57.6 us
  transfers between devices with their start and end apart: 27, of which 21 were waited for; matrix products, arithmetic and copies ran while one was open for 8% of the time, Pallas kernels for 0%

profile of v1, /device:TPU:0, one launch (start us, length us, event | category | flops | bytes accessed | tf_op | source)
XLA Modules:
  0.0 1156.5 jit_solution(8282588541750157962)
XLA Ops:
  11.1 57.6 %all-gather.6 = bf16[32,32,6]{1,2,0:T(8,128)(2,1)S(1)} all-gather(bf16[1,32,6]{1,2,0:T(8,128)(2,1)S(1)} %maximum_bitcast_fusion), channel_id=1, replica_groups=mesh['page'=8,'seq'=4] {'page','seq'}, dimensions={0}, use_global_device_ids=true | all-gather | bytes 12672 | tf_op jit(solution)/shard_map/all_gather | solution.py:94
  69.6 32.1 %all-gather.1 = bf16[1024,256]{1,0:T(8,128)(2,1)S(1)} all-gather(bf16[128,256]{1,0:T(8,128)(2,1)S(1)} %get-tuple-element.35), channel_id=3, replica_groups=mesh['page'=8,'seq'=4] {'page'}, dimensions={0}, use_global_device_ids=true | all-gather | bytes 589824 | tf_op jit(solution)/shard_map/all_gather | solution.py:107
  102.2 1.6 convert_reduce_fusion
  103.9 1.6 fusion.7
  106.0 1.5 convolution_convert_fusion.24
  107.6 1.6 convolution_convert_fusion.25
  109.2 3.7 fusion.92
  112.9 1.5 convolution_convert_fusion.26
  114.4 2.8 convolution_convert_fusion.23
  120.6 22.2 %reduce-scatter.17.cloned.1.call-done = bf16[128,1024]{1,0:T(8,128)(2,1)} async-done(((bf16[512,1024]{1,0:T(8,128)(2,1)}), bf16[128,1024]{1,0:T(8,128)(2,1)}) %reduce-scatter.17.cloned.1.call-update) | async-done | bytes 262160 | tf_op jit(solution)/shard_map/reduce_scatter | solution.py:90
  145.1 1.8 add_convert_fusion.4
  147.7 31.8 %all-gather.3 = bf16[1024,256]{1,0:T(8,128)(2,1)S(1)} all-gather(bf16[128,256]{1,0:T(8,128)(2,1)S(1)} %get-tuple-element.34), channel_id=5, replica_groups=mesh['page'=8,'seq'=4] {'page'}, dimensions={0}, use_global_device_ids=true | all-gather | bytes 589824 | tf_op jit(solution)/shard_map/all_gather | solution.py:107
  180.0 28.0 %all-gather.21.cloned.1.call-done = bf16[3,1024,256]{2,1,0:T(8,128)(2,1)} async-done(((bf16[3,128,256]{2,1,0:T(8,128)(2,1)}), bf16[3,1024,256]{2,1,0:T(8,128)(2,1)}) %all-gather.21.cloned.1.call-update) | async-done | bytes 1572880 | tf_op jit(solution)/shard_map/all_gather | solution.py:118
  207.9 1.8 convolution_convert_fusion.20
  209.8 1.9 convolution_convert_fusion.22
  211.7 13.8 %all-gather.23.cloned.1.call-done = bf16[512,1024]{1,0:T(8,128)(2,1)} async-done(((bf16[128,1024]{1,0:T(8,128)(2,1)}), bf16[512,1024]{1,0:T(8,128)(2,1)}) %all-gather.23.cloned.1.call-update) | async-done | bytes 1048592 | tf_op jit(solution)/shard_map/all_gather | solution.py:87
  225.6 1.8 convolution_convert_fusion.21
  227.4 3.6 fusion.93
  231.0 2.7 convolution_convert_fusion.19
  237.6 23.5 %reduce-scatter.19.cloned.1.call-done = bf16[128,1024]{1,0:T(8,128)(2,1)} async-done(((bf16[512,1024]{1,0:T(8,128)(2,1)}), bf16[128,1024]{1,0:T(8,128)(2,1)}) %reduce-scatter.19.cloned.1.call-update) | async-done | bytes 262160 | tf_op jit(solution)/shard_map/reduce_scatter | solution.py:90
  264.3 48.8 %all-gather.37.cloned.1.call-done = bf16[4096,256]{1,0:T(8,128)(2,1)} async-done(((bf16[512,256]{1,0:T(8,128)(2,1)}), bf16[4096,256]{1,0:T(8,128)(2,1)}) %all-gather.37.cloned.1.call-update) | async-done | bytes 2097168 | tf_op jit(solution)/shard_map/all_gather | solution.py:107
  313.1 3.2 copy.76
  316.3 1.8 copy.108
  318.1 44.9 %all-gather.27.cloned.1.call-done = bf16[1024,1024]{1,0:T(8,128)(2,1)} async-done(((bf16[128,1024]{1,0:T(8,128)(2,1)}), bf16[1024,1024]{1,0:T(8,128)(2,1)}) %all-gather.27.cloned.1.call-update) | async-done | bytes 2097168 | tf_op jit(solution)/shard_map/all_gather | solution.py:120
  363.0 17.2 %all-gather.25.cloned.1.call-done = bf16[512,1024]{1,0:T(8,128)(2,1)} async-done(((bf16[128,1024]{1,0:T(8,128)(2,1)}), bf16[512,1024]{1,0:T(8,128)(2,1)}) %all-gather.25.cloned.1.call-update) | async-done | bytes 1048592 | tf_op jit(solution)/shard_map/all_gather | solution.py:87
  380.2 8.6 multiply_convert_fusion.2
  388.8 9.7 all-gather.39.cloned.1.call-done
  398.6 5.1 add_convert_fusion.2
  404.7 2.4 convolution_convert_fusion.3
  407.2 4.1 convolution_convert_fusion.4
  411.4 20.8 %reduce-scatter.23.cloned.1.call-done = bf16[128,1024]{1,0:T(8,128)(2,1)} async-done(((bf16[512,1024]{1,0:T(8,128)(2,1)}), bf16[128,1024]{1,0:T(8,128)(2,1)}) %reduce-scatter.23.cloned.1.call-update) | async-done | bytes 262160 | tf_op jit(solution)/shard_map/reduce_scatter | solution.py:90
  433.4 26.4 %reduce-scatter.21.cloned.1.call-done = bf16[128,1024]{1,0:T(8,128)(2,1)} async-done(((bf16[512,1024]{1,0:T(8,128)(2,1)}), bf16[128,1024]{1,0:T(8,128)(2,1)}) %reduce-scatter.21.cloned.1.call-update) | async-done | bytes 262160 | tf_op jit(solution)/shard_map/reduce_scatter | solution.py:90
  459.8 2.0 fusion.85
  463.7 16.6 %all-gather.29.cloned.1.call-done = bf16[512,1024]{1,0:T(8,128)(2,1)} async-done(((bf16[128,1024]{1,0:T(8,128)(2,1)}), bf16[512,1024]{1,0:T(8,128)(2,1)}) %all-gather.29.cloned.1.call-update) | async-done | bytes 1048592 | tf_op jit(solution)/shard_map/all_gather | solution.py:87
  480.3 1.7 convolution_convert_fusion.18
  482.1 3.1 multiply_reduce_fusion.1
  488.0 2.5 convolution_convert_fusion.2
  490.6 25.0 %reduce-scatter.25.cloned.1.call-done = bf16[128,1024]{1,0:T(8,128)(2,1)} async-done(((bf16[512,1024]{1,0:T(8,128)(2,1)}), bf16[128,1024]{1,0:T(8,128)(2,1)}) %reduce-scatter.25.cloned.1.call-update) | async-done | bytes 262160 | tf_op jit(solution)/shard_map/reduce_scatter | solution.py:90
  518.3 2.5 fusion.84
  520.8 16.8 %all-gather.31.cloned.1.call-done = bf16[512,1024]{1,0:T(8,128)(2,1)} async-done(((bf16[128,1024]{1,0:T(8,128)(2,1)}), bf16[512,1024]{1,0:T(8,128)(2,1)}) %all-gather.31.cloned.1.call-update) | async-done | bytes 1048592 | tf_op jit(solution)/shard_map/all_gather | solution.py:87
  537.7 1.8 convolution_convert_fusion.17
  539.5 3.1 convolution_convert_fusion.16
  549.0 4.2 convolution_convert_fusion.1
  553.3 4.6 convert_element_type.282
  557.8 3.2 copy.85
  561.1 2.3 copy.101
  563.4 2.6 convolution_convert_fusion.10
  566.1 2.3 copy.100
  568.3 2.6 convolution_convert_fusion.11
  571.2 4.2 convolution_convert_fusion
  575.5 1.9 fusion.32
  580.4 2.6 add_convert_fusion
  593.4 51.7 %reduce-scatter.37.cloned.1.call-done = bf16[1,512,256]{2,1,0:T(8,128)(2,1)} async-done(((bf16[8,512,256]{2,1,0:T(8,128)(2,1)}), bf16[1,512,256]{2,1,0:T(8,128)(2,1)}) %reduce-scatter.37.cloned.1.call-update) | async-done | bytes 262160 | tf_op jit(solution)/shard_map/reduce_scatter | solution.py:192
  645.1 64.9 %reduce-scatter.35.cloned.1.call-done = bf16[1,128,256]{2,1,0:T(8,128)(2,1)} async-done(((bf16[8,128,256]{2,1,0:T(8,128)(2,1)}), bf16[1,128,256]{2,1,0:T(8,128)(2,1)}) %reduce-scatter.35.cloned.1.call-update) | async-done | bytes 65552 | tf_op jit(solution)/shard_map/reduce_scatter | solution.py:192
  710.0 65.0 %reduce-scatter.33.cloned.1.call-done = bf16[1,128,256]{2,1,0:T(8,128)(2,1)} async-done(((bf16[8,128,256]{2,1,0:T(8,128)(2,1)}), bf16[1,128,256]{2,1,0:T(8,128)(2,1)}) %reduce-scatter.33.cloned.1.call-update) | async-done | bytes 65552 | tf_op jit(solution)/shard_map/reduce_scatter | solution.py:192
  776.8 74.9 %reduce-scatter.41.cloned.1.call-done = bf16[128,1024]{1,0:T(8,128)(2,1)} async-done(((bf16[1024,1024]{1,0:T(8,128)(2,1)}), bf16[128,1024]{1,0:T(8,128)(2,1)}) %reduce-scatter.41.cloned.1.call-update) | async-done | bytes 262160 | tf_op jit(solution)/shard_map/reduce_scatter | solution.py:189
  851.7 1.8 convert_element_type.288
  853.5 24.6 %reduce-scatter.29.cloned.1.call-done = bf16[128,1024]{1,0:T(8,128)(2,1)} async-done(((bf16[512,1024]{1,0:T(8,128)(2,1)}), bf16[128,1024]{1,0:T(8,128)(2,1)}) %reduce-scatter.29.cloned.1.call-update) | async-done | bytes 262160 | tf_op jit(solution)/shard_map/reduce_scatter | solution.py:90
  878.1 1.8 bitcast_convert_fusion
  879.9 67.6 %reduce-scatter.39.cloned.1.call-done = bf16[3,128,256]{2,1,0:T(8,128)(2,1)} async-done(((bf16[3,1024,256]{2,1,0:T(8,128)(2,1)}), bf16[3,128,256]{2,1,0:T(8,128)(2,1)}) %reduce-scatter.39.cloned.1.call-update) | async-done | bytes 196624 | tf_op jit(solution)/shard_map/reduce_scatter | solution.py:189
  947.5 1.7 convert_element_type.286
  951.9 130.7 %reduce-scatter.43.cloned.1.call-done = f32[32,6]{1,0:T(8,128)} async-done(((f32[1024,6]{1,0:T(8,128)}), f32[32,6]{1,0:T(8,128)}) %reduce-scatter.43.cloned.1.call-update) | async-done | bytes 784
  1084.7 63.1 %reduce-scatter.31.cloned.1.call-done = bf16[3,128,256]{2,1,0:T(8,128)(2,1)} async-done(((bf16[3,1024,256]{2,1,0:T(8,128)(2,1)}), bf16[3,128,256]{2,1,0:T(8,128)(2,1)}) %reduce-scatter.31.cloned.1.call-update) | async-done | bytes 196624 | tf_op jit(solution)/shard_map/reduce_scatter | solution.py:189
  1147.8 1.7 convert_element_type.274
  (207 shorter events, 54.8 us)
Async XLA Ops:
  7.2 95.1 %all-gather.33.cloned.1.call-start = ((), (), s32[]{:S(2)}) async-start(), calls=%async_computation.34 | async-start | bytes 1310720 | tf_op jit(solution)/shard_map/all_gather | solution.py:87
  7.9 98.1 %all-gather.19.cloned.1.call-start = ((), (), s32[]{:S(2)}) async-start(), calls=%async_computation.14 | async-start | bytes 1769472 | tf_op jit(solution)/shard_map/all_gather | solution.py:102
  8.7 134.2 %reduce-scatter.17.cloned.1.call-start = ((), (), s32[]{:S(2)}) async-start(), calls=%async_computation.15 | async-start | bytes 1310720 | tf_op jit(solution)/shard_map/reduce_scatter | solution.py:90
  9.7 59.9 %collective-permute-start = (bf16[768,256]{1,0:T(8,128)(2,1)S(1)}, bf16[768,256]{1,0:T(8,128)(2,1)S(1)}, u32[]{:S(2)}, u32[]{:S(2)}) collective-permute-start(bf16[768,256]{1,0:T(8,128)(2,1)S(1)} %pad_maximum_fusion.2), channel_id=1, source_target_pairs={{0,0},{1,4},{2,8},{3,12},{4,16},{5,20},{6,24},{7,28},{8,1},{9,5},{... | collective-permute-start | bytes 1179656 | tf_op jit(solution)/shard_map/ppermute | solution.py:98
  102.2 15.0 %copy-start.18 = (bf16[32,8,4,256]{3,1,2,0:T(8,128)(2,1)}, bf16[32,8,4,256]{3,1,2,0:T(8,128)(2,1)S(1)}, u32[]{:S(2)}) copy-start(bf16[32,8,4,256]{3,1,2,0:T(8,128)(2,1)S(1)} %copy.106) | copy-start | bytes 1572868
  102.2 3.3 copy-start.2
  107.6 5.3 copy-start.27
  109.2 3.7 copy-start.29
  114.4 2.8 copy-start.34
  117.2 25.6 %copy-start = (bf16[1,128,1024]{2,1,0:T(8,128)(2,1)S(1)}, bf16[1,128,1024]{2,1,0:T(8,128)(2,1)}, u32[]{:S(2)}) copy-start(bf16[1,128,1024]{2,1,0:T(8,128)(2,1)} %param.13) | copy-start | bytes 786436
  119.4 60.6 %all-gather.35.cloned.1.call-start = ((), (), s32[]{:S(2)}) async-start(), calls=%async_computation.35 | async-start | bytes 1310720 | tf_op jit(solution)/shard_map/all_gather | solution.py:87
  120.0 88.0 %all-gather.21.cloned.1.call-start = ((), (), s32[]{:S(2)}) async-start(), calls=%async_computation.16 | async-start | bytes 1769472 | tf_op jit(solution)/shard_map/all_gather | solution.py:118
  120.6 105.0 %all-gather.23.cloned.1.call-start = ((), (), s32[]{:S(2)}) async-start(), calls=%async_computation.17 | async-start | bytes 1310720 | tf_op jit(solution)/shard_map/all_gather | solution.py:87
  146.9 114.1 %reduce-scatter.19.cloned.1.call-start = ((), (), s32[]{:S(2)}) async-start(), calls=%async_computation.18 | async-start | bytes 1310720 | tf_op jit(solution)/shard_map/reduce_scatter | solution.py:90
  209.8 21.2 %copy-start.31 = (bf16[512,256]{0,1:T(8,128)(2,1)}, bf16[512,256]{0,1:T(8,128)(2,1)S(1)}, u32[]{:S(2)}) copy-start(bf16[512,256]{0,1:T(8,128)(2,1)S(1)} %convolution_convert_fusion.20) | copy-start | bytes 786436
  227.4 3.6 copy-start.26
  233.7 0.7 copy-start.22
  233.7 27.3 %copy-start.1 = (bf16[128,1024]{1,0:T(8,128)(2,1)S(1)}, bf16[128,1024]{1,0:T(8,128)(2,1)}, u32[]{:S(2)}) copy-start(bf16[128,1024]{1,0:T(8,128)(2,1)} %reduce-scatter.17.cloned.1.call-done) | copy-start | bytes 786436
  236.0 77.1 %all-gather.37.cloned.1.call-start = ((), (), s32[]{:S(2)}) async-start(), calls=%async_computation.36 | async-start | bytes 2359296 | tf_op jit(solution)/shard_map/all_gather | solution.py:107
  236.8 126.2 %all-gather.27.cloned.1.call-start = ((), (), s32[]{:S(2)}) async-start(), calls=%async_computation.20 | async-start | bytes 2359296 | tf_op jit(solution)/shard_map/all_gather | solution.py:120
  237.5 142.7 %all-gather.25.cloned.1.call-start = ((), (), s32[]{:S(2)}) async-start(), calls=%async_computation.19 | async-start | bytes 1310720 | tf_op jit(solution)/shard_map/all_gather | solution.py:87
  263.3 135.3 %all-gather.39.cloned.1.call-start = ((), (), s32[]{:S(2)}) async-start(), calls=%async_computation.37 | async-start | bytes 1310720 | tf_op jit(solution)/shard_map/all_gather | solution.py:87
  264.0 168.2 %reduce-scatter.23.cloned.1.call-start = ((), (), s32[]{:S(2)}) async-start(), calls=%async_computation.22 | async-start | bytes 1310720 | tf_op jit(solution)/shard_map/reduce_scatter | solution.py:90
  398.6 6.2 copy-start.33
  403.7 1.1 copy-start.38
  407.1 52.7 %reduce-scatter.21.cloned.1.call-start = ((), (), s32[]{:S(2)}) async-start(), calls=%async_computation.21 | async-start | bytes 1310720 | tf_op jit(solution)/shard_map/reduce_scatter | solution.py:90
  411.3 51.3 %copy-start.10 = (bf16[1,128,1024]{2,1,0:T(8,128)(2,1)S(1)}, bf16[1,128,1024]{2,1,0:T(8,128)(2,1)}, u32[]{:S(2)}) copy-start(bf16[1,128,1024]{2,1,0:T(8,128)(2,1)} %param.15) | copy-start | bytes 786436
  411.3 69.0 %all-gather.29.cloned.1.call-start = ((), (), s32[]{:S(2)}) async-start(), calls=%async_computation.23 | async-start | bytes 1310720 | tf_op jit(solution)/shard_map/all_gather | solution.py:87
  461.8 0.8 copy-start.3
  463.5 52.1 %reduce-scatter.25.cloned.1.call-start = ((), (), s32[]{:S(2)}) async-start(), calls=%async_computation.24 | async-start | bytes 1310720 | tf_op jit(solution)/shard_map/reduce_scatter | solution.py:90
  482.0 3.1 copy-start.36
  482.1 3.5 copy-start.4
  485.6 1.2 copy-start.32
  487.3 0.7 copy-start.8
  490.5 47.1 %all-gather.31.cloned.1.call-start = ((), (), s32[]{:S(2)}) async-start(), calls=%async_computation.25 | async-start | bytes 1310720 | tf_op jit(solution)/shard_map/all_gather | solution.py:87
  520.8 67.5 %reduce-scatter.27.cloned.1.call-start = ((), (), s32[]{:S(2)}) async-start(), calls=%async_computation.26 | async-start | bytes 1310720 | tf_op jit(solution)/shard_map/reduce_scatter | solution.py:90
  539.5 3.5 copy-start.6
  539.5 3.5 copy-start.35
  543.0 4.5 copy-start.23
  543.8 1.2 copy-start.30
  545.0 1.0 copy-start.28
  545.0 1.5 copy-start.20
  545.9 1.0 copy-start.14
  546.4 1.1 copy-start.12
  549.0 96.1 %reduce-scatter.37.cloned.1.call-start = ((), (), s32[]{:S(2)}) async-start(), calls=%async_computation.31 | async-start | bytes 2359296 | tf_op jit(solution)/shard_map/reduce_scatter | solution.py:192
  561.1 148.9 %reduce-scatter.35.cloned.1.call-start = ((), (), s32[]{:S(2)}) async-start(), calls=%async_computation.30 | async-start | bytes 589824 | tf_op jit(solution)/shard_map/reduce_scatter | solution.py:192
  566.0 209.0 %reduce-scatter.33.cloned.1.call-start = ((), (), s32[]{:S(2)}) async-start(), calls=%async_computation.29 | async-start | bytes 589824 | tf_op jit(solution)/shard_map/reduce_scatter | solution.py:192
  570.9 280.8 %reduce-scatter.41.cloned.1.call-start = ((), (), s32[]{:S(2)}) async-start(), calls=%async_computation.33 | async-start | bytes 2359296 | tf_op jit(solution)/shard_map/reduce_scatter | solution.py:189
  575.4 302.7 %reduce-scatter.29.cloned.1.call-start = ((), (), s32[]{:S(2)}) async-start(), calls=%async_computation.27 | async-start | bytes 1310720 | tf_op jit(solution)/shard_map/reduce_scatter | solution.py:90
  575.5 4.1 copy-start.5
  577.4 2.2 copy-start.37
  580.4 2.7 copy-start.7
  583.0 0.9 copy-start.17
  583.0 1.5 copy-start.9
  583.0 364.5 %reduce-scatter.39.cloned.1.call-start = ((), (), s32[]{:S(2)}) async-start(), calls=%async_computation.32 | async-start | bytes 1769472 | tf_op jit(solution)/shard_map/reduce_scatter | solution.py:189
  583.1 1.4 copy-start.25
  585.0 1.5 copy-start.24
  586.4 0.9 copy-start.15
  586.4 1.4 copy-start.13
  586.4 496.2 %reduce-scatter.43.cloned.1.call-start = ((), (), s32[]{:S(2)}) async-start(), calls=%async_computation.38 | async-start | bytes 540672
  592.0 555.9 %reduce-scatter.31.cloned.1.call-start = ((), (), s32[]{:S(2)}) async-start(), calls=%async_computation.28 | async-start | bytes 1769472 | tf_op jit(solution)/shard_map/reduce_scatter | solution.py:189
  775.0 175.7 %copy-start.11 = (bf16[128,1024]{1,0:T(8,128)(2,1)S(1)}, bf16[128,1024]{1,0:T(8,128)(2,1)}, u32[]{:S(2)}) copy-start(bf16[128,1024]{1,0:T(8,128)(2,1)} %reduce-scatter.27.cloned.1.call-done) | copy-start | bytes 786436
  775.0 175.7 %copy-start.19 = (f32[128,1024]{1,0:T(8,128)S(1)}, f32[128,1024]{1,0:T(8,128)}, u32[]{:S(2)}) copy-start(f32[128,1024]{1,0:T(8,128)} %get-tuple-element.24) | copy-start | bytes 1572868
  776.1 173.1 %collective-permute-start.1 = (bf16[768,256]{1,0:T(8,128)(2,1)S(1)}, bf16[768,256]{1,0:T(8,128)(2,1)S(1)}, u32[]{:S(2)}, u32[]{:S(2)}) collective-permute-start(bf16[768,256]{1,0:T(8,128)(2,1)S(1)} %pad_maximum_fusion.3), channel_id=1, source_target_pairs={{0,0},{4,1},{8,2},{12,3},{16,4},{20,5},{24,6},{28,7},{1,8},{5,9},{... | collective-permute-start | bytes 1179656 | tf_op jit(solution)/shard_map/ppermute | solution.py:200
  (2 other events, 1.4 us)
Sparse Core Ops, SparseCore 0:
  9.6 30.6 all-gather.32
  42.4 52.1 all-gather.18
  119.5 23.2 reduce-scatter.16
  144.3 16.7 all-gather.34
  163.4 44.5 all-gather.20
  210.0 15.5 all-gather.22
  236.1 24.8 reduce-scatter.18
  263.7 49.2 all-gather.36
  315.2 47.7 all-gather.26
  365.0 15.1 all-gather.24
  381.8 16.7 all-gather.38
  407.2 24.9 reduce-scatter.22
  434.9 24.8 reduce-scatter.20
  463.6 16.7 all-gather.28
  490.7 24.8 reduce-scatter.24
  520.9 16.7 all-gather.30
  549.1 24.8 reduce-scatter.26
  577.4 67.6 reduce-scatter.36
  649.0 60.9 reduce-scatter.34
  714.1 60.8 reduce-scatter.32
  778.6 73.0 reduce-scatter.40
  854.2 23.8 reduce-scatter.28
  882.0 65.4 reduce-scatter.38
  949.6 132.8 reduce-scatter.42
  1086.4 61.4 reduce-scatter.30

commit v2 on v1

--- a/solution.py
+++ b/solution.py
@@ -1,12 +1,304 @@
+import functools
+
 import jax
 import jax.numpy as jnp
 from jax import lax
+from jax.experimental import pallas as pl
+from jax.experimental.pallas import tpu as pltpu
 from jax.sharding import PartitionSpec as P
 
 HEADS = 16
 HEAD_DIM = 64
 F32 = jnp.float32
 BF16 = jnp.bfloat16
+MESH = pl.DeviceIdType.MESH
+NG = 6
+
+
+def ag_kernel(A, B, S, spaces, *refs):
+    ng = 6
+    ins, outs = refs[:ng], refs[ng:2*ng]
+    stage = refs[2*ng:2*ng+3]
+    local_sem, perm_send, perm_recv, recv, send = refs[2*ng+3:]
+    page = lax.axis_index("page"); seq = lax.axis_index("seq")
+    a = lax.div(page, B); b = lax.rem(page, B)
+    Pn = A*B
+    R = Pn // S
+    tp, ts = lax.rem(page, R)*S + seq, lax.div(page, R)
+    fixed = (tp == page) & (ts == seq)
+    sp, ss = ts_src = (seq*R + lax.div(page, S), lax.rem(page, S))
+    barrier = pltpu.get_barrier_semaphore()
+    def sig(dev):
+        pl.semaphore_signal(barrier, inc=1, device_id=dev, device_id_type=MESH)
+    @pl.when(a > 0)
+    def _(): sig((page - B, seq))
+    @pl.when(a < A-1)
+    def _(): sig((page + B, seq))
+    @pl.when(b > 0)
+    def _(): sig((page - 1, seq))
+    @pl.when(b < B-1)
+    def _(): sig((page + 1, seq))
+    @pl.when(jnp.logical_not(fixed))
+    def _():
+        sig((tp, ts)); sig((sp, ss))
+    n = (a > 0).astype(jnp.int32) + (a < A-1).astype(jnp.int32) + (b > 0).astype(jnp.int32) + (b < B-1).astype(jnp.int32) + 2*jnp.logical_not(fixed).astype(jnp.int32)
+    pl.semaphore_wait(barrier, n)
+
+    def window(g, j):
+        ref = outs[g]
+        if g in (0, 2):
+            r = ins[g].shape[1]
+            return ref.at[:, pl.ds(pl.multiple_of(j*r, r), r), :]
+        if g == 4:
+            r = ins[g].shape[0]
+            return ref.at[pl.ds(pl.multiple_of(j*r, r), r), :]
+        r, c = ins[g].shape
+        return ref.at[pl.ds(pl.multiple_of(lax.div(j, S)*r, r), r), pl.ds(pl.multiple_of(lax.rem(j, S)*c, c), c)]
+
+    def remote(g, j, way):
+        dev = {0: (page - B, seq), 1: (page + B, seq), 2: (page - 1, seq), 3: (page + 1, seq)}[way]
+        return pltpu.make_async_remote_copy(src_ref=window(g, j), dst_ref=window(g, j), send_sem=send.at[g, j, way], recv_sem=recv.at[g, j], device_id=dev, device_id_type=MESH)
+    def landed(g, j):
+        pltpu.make_async_remote_copy(src_ref=window(g, j), dst_ref=window(g, j), send_sem=send.at[g, j, 0], recv_sem=recv.at[g, j], device_id=(page, seq), device_id_type=MESH).wait_recv()
+
+    for i, g in enumerate((1, 3, 5)):
+        cp = pltpu.make_async_remote_copy(src_ref=ins[g], dst_ref=stage[i], send_sem=perm_send.at[i], recv_sem=perm_recv.at[i], device_id=(tp, ts), device_id_type=MESH)
+        @pl.when(jnp.logical_not(fixed))
+        def _(): cp.start()
+    own = {}
+    for i, g in enumerate((0, 2, 4)):
+        own[g] = pltpu.make_async_copy(ins[g], window(g, page), local_sem.at[g])
+        own[g].start()
+    order = [0, 1, 2, 3, 4, 5]
+    def first(g):
+        if g in own:
+            own[g].wait()
+        else:
+            i = g//2
+            cp = pltpu.make_async_remote_copy(src_ref=ins[g], dst_ref=stage[i], send_sem=perm_send.at[i], recv_sem=perm_recv.at[i], device_id=(tp, ts), device_id_type=MESH)
+            @pl.when(jnp.logical_not(fixed))
+            def _(): cp.wait()
+            @pl.when(fixed)
+            def _():
+                c2 = pltpu.make_async_copy(ins[g], window(g, page), local_sem.at[g]); c2.start(); c2.wait()
+            @pl.when(jnp.logical_not(fixed))
+            def _():
+                c2 = pltpu.make_async_copy(stage[i], window(g, page), local_sem.at[g]); c2.start(); c2.wait()
+        @pl.when(a > 0)
+        def _(): remote(g, page, 0).start()
+        @pl.when(a < A-1)
+        def _(): remote(g, page, 1).start()
+        @pl.when(b > 0)
+        def _(): remote(g, page, 2).start()
+        @pl.when(b < B-1)
+        def _(): remote(g, page, 3).start()
+    def step_a(g, d):
+        @pl.when(a - d >= 0)
+        def _():
+            j = page - d*B
+            landed(g, j)
+            @pl.when(a < A-1)
+            def _(): remote(g, j, 1).start()
+            @pl.when(b > 0)
+            def _(): remote(g, j, 2).start()
+            @pl.when(b < B-1)
+            def _(): remote(g, j, 3).start()
+        @pl.when(a + d < A)
+        def _():
+            j = page + d*B
+            landed(g, j)
+            @pl.when(a > 0)
+            def _(): remote(g, j, 0).start()
+            @pl.when(b > 0)
+            def _(): remote(g, j, 2).start()
+            @pl.when(b < B-1)
+            def _(): remote(g, j, 3).start()
+    def step_b(g, e):
+        for a2 in range(A):
+            @pl.when(b - e >= 0)
+            def _():
+                j = a2*B + b - e
+                landed(g, j)
+                @pl.when(b < B-1)
+                def _(): remote(g, j, 3).start()
+            @pl.when(b + e < B)
+            def _():
+                j = a2*B + b + e
+                landed(g, j)
+                @pl.when(b > 0)
+                def _(): remote(g, j, 2).start()
+    first(order[0])
+    for i, g in enumerate(order):
+        if i + 1 < len(order):
+            first(order[i+1])
+        for d in range(1, A):
+            step_a(g, d)
+    for g in order:
+        for e in range(1, B):
+            step_b(g, e)
+    for g in order:
+        for a2 in range(A):
+            for b2 in range(B):
+                j = a2*B + b2
+                same = b == b2
+                @pl.when(same & (a2 >= a) & (a > 0))
+                def _(): remote(g, j, 0).wait_send()
+                @pl.when(same & (a2 <= a) & (a < A-1))
+                def _(): remote(g, j, 1).wait_send()
+                @pl.when((b2 >= b) & (b > 0))
+                def _(): remote(g, j, 2).wait_send()
+                @pl.when((b2 <= b) & (b < B-1))
+                def _(): remote(g, j, 3).wait_send()
+
+def ag(ins, A, B, S, space):
+    Pn = A*B; R = Pn//S
+    shapes = []
+    for g, x in enumerate(ins):
+        if g in (0, 2): s = (x.shape[0], x.shape[1]*Pn, x.shape[2])
+        elif g == 4: s = (x.shape[0]*Pn, x.shape[1])
+        else: s = (x.shape[0]*R, x.shape[1]*S)
+        shapes.append(jax.ShapeDtypeStruct(s, x.dtype))
+    return pl.pallas_call(
+        functools.partial(ag_kernel, A, B, S, space),
+        out_shape=shapes,
+        in_specs=[pl.BlockSpec(memory_space=space)]*6,
+        out_specs=[pl.BlockSpec(memory_space=space)]*6,
+        scratch_shapes=[pltpu.VMEM(ins[g].shape, BF16) for g in (1, 3, 5)] + [
+            pltpu.SemaphoreType.DMA((6,)), pltpu.SemaphoreType.DMA((3,)), pltpu.SemaphoreType.DMA((3,)),
+            pltpu.SemaphoreType.DMA((6, Pn)), pltpu.SemaphoreType.DMA((6, Pn, 4))],
+        compiler_params=pltpu.CompilerParams(collective_id=0, has_side_effects=True, vmem_limit_bytes=48*2**20),
+    )(*ins)
+
+
+def window(ref, g, j, S, shard):
+    if g in (0, 2):
+        r = shard[1]
+        return ref.at[:, pl.ds(pl.multiple_of(j*r, r), r), :]
+    if g == 4:
+        r = shard[0]
+        return ref.at[pl.ds(pl.multiple_of(j*r, r), r), :]
+    r, c = shard
+    return ref.at[pl.ds(pl.multiple_of(lax.div(j, S)*r, r), r), pl.ds(pl.multiple_of(lax.rem(j, S)*c, c), c)]
+
+def rs_kernel(A, B, S, shards, *refs):
+    grads, outs = refs[:NG], refs[NG:2*NG]
+    rb, zz = refs[2*NG:3*NG], refs[3*NG:4*NG]
+    stage = refs[4*NG:4*NG+3]
+    ysend, yrecv, zsend, zrecv, psend, precv = refs[4*NG+3:]
+    page = lax.axis_index("page"); seq = lax.axis_index("seq")
+    a = lax.div(page, B); b = lax.rem(page, B)
+    Pn = A*B; R = Pn // S
+    op, os_ = seq*R + lax.div(page, S), lax.rem(page, S)
+    hp, hs = lax.rem(page, R)*S + seq, lax.div(page, R)
+    fixed = (op == page) & (os_ == seq)
+    barrier = pltpu.get_barrier_semaphore()
+    def sig(dev):
+        pl.semaphore_signal(barrier, inc=1, device_id=dev, device_id_type=MESH)
+    @pl.when(a > 0)
+    def _(): sig((page - B, seq))
+    @pl.when(a < A-1)
+    def _(): sig((page + B, seq))
+    for k in range(1, B):
+        sig((a*B + lax.rem(b + k, B), seq))
+    @pl.when(jnp.logical_not(fixed))
+    def _():
+        sig((op, os_)); sig((hp, hs))
+    n = (a > 0).astype(jnp.int32) + (a < A-1).astype(jnp.int32) + (B-1) + 2*jnp.logical_not(fixed).astype(jnp.int32)
+    pl.semaphore_wait(barrier, n)
+
+    def win(g, j): return window(grads[g], g, j, S, shards[g])
+    def ycopy(g, k, t):
+        b2 = lax.rem(b + k, B)
+        return pltpu.make_async_remote_copy(src_ref=win(g, t*B + b2), dst_ref=rb[g].at[B-1-k, t], send_sem=ysend.at[g, k-1, t], recv_sem=yrecv.at[g, B-1-k, t], device_id=(a*B + b2, seq), device_id_type=MESH)
+    def ylanded(g, slot, t):
+        pltpu.make_async_remote_copy(src_ref=rb[g].at[slot, t], dst_ref=rb[g].at[slot, t], send_sem=ysend.at[g, 0, t], recv_sem=yrecv.at[g, slot, t], device_id=(page, seq), device_id_type=MESH).wait_recv()
+    def zcopy(g, t, sg):
+        way = lax.div(sg + 1, 2)
+        return pltpu.make_async_remote_copy(src_ref=rb[g].at[0, t], dst_ref=zz[g].at[way, t], send_sem=zsend.at[g, t], recv_sem=zrecv.at[g, way, t], device_id=(page + sg*B, seq), device_id_type=MESH)
+    def zlanded(g, t, way):
+        pltpu.make_async_remote_copy(src_ref=zz[g].at[way, t], dst_ref=zz[g].at[way, t], send_sem=zsend.at[g, t], recv_sem=zrecv.at[g, way, t], device_id=(page, seq), device_id_type=MESH).wait_recv()
+    def ys(g):
+        for k in range(1, B):
+            for t in range(A):
+                ycopy(g, k, t).start()
+    def acc(g):
+        for t in range(A):
+            total = win(g, t*B + b)[...].astype(F32)
+            for slot in range(B-1):
+                ylanded(g, slot, t)
+                total = total + rb[g][slot, t].astype(F32)
+            rb[g][0, t] = total.astype(BF16)
+    def phase(g, sg):
+        up = a - sg
+        has = (up >= 0) & (up < A)
+        way = lax.div(sg + 1, 2)
+        for k in range(A-1, 0, -1):
+            t = a + sg*k
+            @pl.when((t >= 0) & (t < A))
+            def _():
+                @pl.when(has)
+                def _():
+                    zlanded(g, t, way)
+                    rb[g][0, t] = (rb[g][0, t].astype(F32) + zz[g][way, t].astype(F32)).astype(BF16)
+                zcopy(g, t, sg).start()
+    first = jnp.where(2*a < A, 1, -1)
+    def final(g):
+        for way, has in ((1, a > 0), (0, a < A-1)):
+            @pl.when(has)
+            def _():
+                zlanded(g, a, way)
+        total = rb[g][0, a].astype(F32)
+        zu = jnp.where(a > 0, zz[g][1, a].astype(F32), 0.0)
+        zd = jnp.where(a < A-1, zz[g][0, a].astype(F32), 0.0)
+        total = total + zu + zd
+        if g in (0, 2, 4):
+            outs[g][...] = total
+        else:
+            i = g//2
+            stage[i][0] = total.astype(BF16)
+            @pl.when(jnp.logical_not(fixed))
+            def _():
+                pcopy(i).start()
+    def pcopy(i):
+        return pltpu.make_async_remote_copy(src_ref=stage[i].at[0], dst_ref=stage[i].at[1], send_sem=psend.at[i], recv_sem=precv.at[i], device_id=(op, os_), device_id_type=MESH)
+    order = [5, 4, 3, 2, 1, 0]
+    AHEAD = 2
+    for i in range(AHEAD): ys(order[i])
+    for i in range(NG + 2):
+        if i + AHEAD < NG: ys(order[i+AHEAD])
+        if i < NG:
+            acc(order[i]); phase(order[i], first)
+        if 0 <= i-1 < NG:
+            phase(order[i-1], -first)
+        if 0 <= i-2 < NG:
+            final(order[i-2])
+    for i, g in enumerate((1, 3, 5)):
+        @pl.when(jnp.logical_not(fixed))
+        def _():
+            pcopy(i).wait()
+            outs[g][...] = stage[i][1].astype(F32)
+        @pl.when(fixed)
+        def _():
+            outs[g][...] = stage[i][0].astype(F32)
+    for g in range(NG):
+        for t in range(A):
+            for k in range(1, B):
+                ycopy(g, k, t).wait_send()
+            @pl.when(t != a)
+            def _(): zcopy(g, t, jnp.where(t > a, 1, -1)).wait_send()
+
+def rs(grads, shards, A, B, S):
+    V = pltpu.VMEM
+    return pl.pallas_call(
+        functools.partial(rs_kernel, A, B, S, shards),
+        out_shape=[jax.ShapeDtypeStruct(s, F32) for s in shards],
+        in_specs=[pl.BlockSpec(memory_space=V)]*NG,
+        out_specs=[pl.BlockSpec(memory_space=V)]*NG,
+        scratch_shapes=[V((B-1, A, *s), BF16) for s in shards] + [V((2, A, *s), BF16) for s in shards] + [V((2, *shards[g]), BF16) for g in (1, 3, 5)] + [
+            pltpu.SemaphoreType.DMA((NG, B-1, A)), pltpu.SemaphoreType.DMA((NG, B-1, A)),
+            pltpu.SemaphoreType.DMA((NG, A)), pltpu.SemaphoreType.DMA((NG, 2, A)), pltpu.SemaphoreType.DMA((3,)), pltpu.SemaphoreType.DMA((3,))],
+        compiler_params=pltpu.CompilerParams(collective_id=1, has_side_effects=True, vmem_limit_bytes=60*2**20), name="rs",
+    )(*grads)
 
 
 def layer_norm(values, gain_row, bias_row):
@@ -75,14 +367,7 @@
     pages = lax.axis_size("page")
     parts = lax.axis_size("seq")
     here = lax.axis_index("seq")
-    ratio = pages // parts
-    there = [
-        (page * parts + part, ((page % ratio) * parts + part) * parts + page // ratio)
-        for page in range(pages)
-        for part in range(parts)
-    ]
-    back = [(b, a) for a, b in there]
-
+    wide = 2 if pages == 8 else 8
     def gather_seq(rows):
         return lax.all_gather(rows, "seq", axis=0, tiled=True)
 
@@ -95,30 +380,13 @@
         jnp.concatenate([norm_gains, norm_biases]), ("page", "seq"), axis=1, tiled=True
     ).astype(F32)
     gains, biases = norms[:3], norms[3:]
-    moved = lax.ppermute(
-        jnp.concatenate([self_out, cross_out, down_weight]), ("page", "seq"), there
-    )
-    small = self_out.shape[0]
-    w_self = lax.all_gather(self_qkv, "page", axis=1, tiled=True)
+    pieces = (self_qkv, self_out, cross_qkv, cross_out, up_weight, down_weight)
+    w_self, w_self_out, w_cross, w_cross_out, w_up, w_down = ag(
+        pieces, pages // wide, wide, parts, pl.ANY
+    )
     tokens_all = gather_seq(tokens[0]).astype(F32)
     memory_all = gather_seq(memory[0])
 
-    def rows_of(piece):
-        blocks = lax.all_gather(piece, "page", axis=0, tiled=False)
-        rows, cols = piece.shape
-        blocks = blocks.reshape(ratio, parts, rows, cols).transpose(0, 2, 1, 3)
-        return blocks.reshape(ratio * rows, parts * cols)
-
-    def blocks_of(grad):
-        rows, cols = grad.shape[0] // ratio, grad.shape[1] // parts
-        blocks = grad.reshape(ratio, rows, parts, cols).transpose(0, 2, 1, 3)
-        return blocks.reshape(pages, rows, cols).astype(BF16)
-
-    w_self_out = rows_of(moved[:small])
-    w_cross = lax.all_gather(cross_qkv, "page", axis=1, tiled=True)
-    w_cross_out = rows_of(moved[small : 2 * small])
-    w_up = lax.all_gather(up_weight, "page", axis=0, tiled=True)
-    w_down = rows_of(moved[2 * small :])
     cotangent_all = gather_seq(cotangent[0])
 
     token_rows = tokens.shape[1]
@@ -185,21 +453,16 @@
     dx, gain_first, bias_first = jax.vjp(layer_norm, inputs, gains[0], biases[0])[1](da1)
     input_grad = (dx1 + dx)[None]
 
-    def sum_pages(grad, axis):
-        return lax.psum_scatter(grad.astype(BF16), "page", scatter_dimension=axis, tiled=True)
-
-    def sum_blocks(grad):
-        return lax.psum_scatter(blocks_of(grad), "page", scatter_dimension=0, tiled=False)
-
-    up_out = sum_pages(up_grad, 0).astype(F32)
-    down_part = sum_blocks(down_grad)
-    cross_out_part = sum_blocks(cross_out_grad)
-    cross_out_qkv = sum_pages(cross_qkv_grad, 1).astype(F32)
-    self_out_part = sum_blocks(self_out_grad)
-    self_out_qkv = sum_pages(self_qkv_grad, 1).astype(F32)
-    returned = lax.ppermute(
-        jnp.concatenate([self_out_part, cross_out_part, down_part]), ("page", "seq"), back
-    ).astype(F32)
+    grads = (
+        self_qkv_grad, self_out_grad, cross_qkv_grad, cross_out_grad, up_grad, down_grad
+    )
+    sums = rs(
+        [grad.astype(BF16) for grad in grads],
+        [piece.shape for piece in pieces],
+        pages // wide,
+        wide,
+        parts,
+    )
     norm_sums = lax.psum_scatter(
         jnp.stack([gain_first, gain_second, gain_third, bias_first, bias_second, bias_third]),
         ("page", "seq"),
@@ -210,12 +473,7 @@
         mixed,
         input_grad,
         memory_grad[None],
-        self_out_qkv,
-        returned[:small],
-        cross_out_qkv,
-        returned[small : 2 * small],
-        up_out,
-        returned[2 * small :],
+        *sums,
         norm_sums[:3],
         norm_sums[3:],
     )

time: 1170 us -> 789 us (0.67)
  waiting for transfers between devices: 861 us -> 340 us
  Pallas kernels: 0 us -> 239 us
  blocking collectives: 121 us -> 43.5 us
    reduce_scatter x6 -> x0, waiting for transfers between devices: 387 us -> none  [the longest x3 206 us: sum_pages(): lax.psum_scatter(grad.astype(BF16), 'page', scatter_dimension=axis, tiled...]
    pallas_call x0 -> x2, Pallas kernels: none -> 239 us  [the longest x1 123 us: rs(): pl.pallas_call(functools.partial(rs_kernel, A, B, S, shards), out_shape=[...]
    all_gather x4 -> x0, waiting for transfers between devices: 122 us -> none  [the longest x1 48.8 us: rows_of(): blocks = lax.all_gather(piece, 'page', axis=0, tiled=False)]
    all_gather x2 -> x0, blocking collectives: 63.8 us -> none  [rows_of(): blocks = lax.all_gather(piece, 'page', axis=0, tiled=False)]
    reduce_scatter x7, waiting for transfers between devices: 142 us -> 128 us  [scatter_seq(): lax.psum_scatter(rows.astype(BF16), 'seq', scatter_dimension=0, tiled=True)]
    all_gather x1, blocking collectives: 57.6 us -> 43.5 us  [per_device(): lax.all_gather(jnp.concatenate([norm_gains, norm_biases]), ('page', 'seq'...]
    unnamed x84 -> x125, local copies, waits for them, and re-layouts: 10.7 us -> 22.6 us
    unnamed x26 -> x16, waiting for transfers between devices: 135 us -> 135 us
  transfers between devices with their start and end apart: 27 -> 15, of which waited for: 21 -> 13; matrix products, arithmetic and copies ran while one was open for 8% -> 8% of each run, Pallas kernels for 0% -> 31%
where the time goes in v2:
time: 789 us; the launch traced here: 780 us
  waiting for transfers between devices  340 us (43%)
  Pallas kernels  239 us (30%)
  matrix products  83.2 us (11%)
  blocking collectives  43.5 us (6%)
  other arithmetic  32.8 us (4%)
  local copies, waits for them, and re-layouts  23.6 us (3%)
  between operations  16.4 us (2%)
    unnamed x16, waiting for transfers between devices  135 us
    reduce_scatter x7, waiting for transfers between devices, scatter_seq(): lax.psum_scatter(rows.astype(BF16), 'seq', scatter_dimension=0, tiled=True)  128 us
    pallas_call x1, Pallas kernels, rs(): pl.pallas_call(functools.partial(rs_kernel, A, B, S, shards), out_shape=[...  123 us
    pallas_call x1, Pallas kernels, ag(): pl.pallas_call(functools.partial(ag_kernel, A, B, S, space), out_shape=sh...  116 us
    all_gather x7, waiting for transfers between devices, gather_seq(): return lax.all_gather(rows, 'seq', axis=0, tiled=True)  77.1 us
    dot_general x40, matrix products, dot(): return jnp.einsum(spec, left, right, preferred_element_type=F32)  73.9 us
    all_gather x1, blocking collectives, per_device(): lax.all_gather(jnp.concatenate([norm_gains, norm_biases]), ('page', 'seq'...  43.5 us
    unnamed x125, local copies, waits for them, and re-layouts  22.6 us
  transfers between devices with their start and end apart: 15, of which 13 were waited for; matrix products, arithmetic and copies ran while one was open for 8% of the time, Pallas kernels for 31%

profile of v2, /device:TPU:0, one launch (start us, length us, event | category | flops | bytes accessed | tf_op | source)
XLA Modules:
  0.0 779.9 jit_solution(9847710703391179961)
XLA Ops:
  9.3 43.5 %all-gather.3 = bf16[32,32,6]{1,2,0:T(8,128)(2,1)S(1)} all-gather(bf16[1,32,6]{1,2,0:T(8,128)(2,1)S(1)} %maximum_bitcast_fusion), channel_id=1, replica_groups=mesh['page'=8,'seq'=4] {'page','seq'}, dimensions={0}, use_global_device_ids=true | all-gather | bytes 12672 | tf_op jit(solution)/shard_map/all_gather | solution.py:379
  58.3 115.6 %shard_map.212 = (bf16[3,1024,256]{2,1,0:T(8,128)(2,1)S(1)}, bf16[256,1024]{1,0:T(8,128)(2,1)S(1)}, bf16[3,1024,256]{2,1,0:T(8,128)(2,1)S(1)}, bf16[256,1024]{1,...) custom-call(bf16[3,128,256]{2,1,0:T(8,128)(2,1)S(1)} %copy-done.6, ...), custom_call_target="tpu_custom_call" | custom-call | tf_op jit(solution)/shard_map/pallas_call | solution.py:161
  176.5 1.5 convert_reduce_fusion
  178.0 1.6 fusion.7
  180.6 1.2 convolution_convert_fusion.25
  181.8 1.2 convolution_convert_fusion.26
  183.0 4.7 fusion.114
  187.7 2.8 convolution_convert_fusion.23
  191.2 1.4 convolution_convert_fusion.6
  193.5 25.0 %reduce-scatter.11.cloned.1.call-done = bf16[128,1024]{1,0:T(8,128)(2,1)} async-done(((bf16[512,1024]{1,0:T(8,128)(2,1)}), bf16[128,1024]{1,0:T(8,128)(2,1)}) %reduce-scatter.11.cloned.1.call-update) | async-done | bytes 262160 | tf_op jit(solution)/shard_map/reduce_scatter | solution.py:375
  218.4 1.1 fusion.77
  219.6 1.2 multiply_reduce_fusion.3
  220.7 1.8 add_convert_fusion.4
  223.3 13.6 %all-gather.22.cloned.1.call-done = bf16[1,512,1024]{2,1,0:T(8,128)(2,1)} async-done(((bf16[1,128,1024]{2,1,0:T(8,128)(2,1)}), bf16[1,512,1024]{2,1,0:T(8,128)(2,1)}) %all-gather.22.cloned.1.call-update) | async-done | bytes 1048592 | tf_op jit(solution)/shard_map/all_gather | solution.py:372
  236.9 2.4 convolution_convert_fusion.20
  239.3 2.4 convolution_convert_fusion.22
  241.7 14.0 %all-gather.12.cloned.1.call-done = bf16[512,1024]{1,0:T(8,128)(2,1)} async-done(((bf16[128,1024]{1,0:T(8,128)(2,1)}), bf16[512,1024]{1,0:T(8,128)(2,1)}) %all-gather.12.cloned.1.call-update) | async-done | bytes 1048592 | tf_op jit(solution)/shard_map/all_gather | solution.py:372
  255.7 2.4 convolution_convert_fusion.21
  258.1 4.6 fusion.115
  262.7 2.8 convolution_convert_fusion.19
  266.3 1.5 convolution_convert_fusion.5
  268.0 24.8 %reduce-scatter.13.cloned.1.call-done = bf16[128,1024]{1,0:T(8,128)(2,1)} async-done(((bf16[512,1024]{1,0:T(8,128)(2,1)}), bf16[128,1024]{1,0:T(8,128)(2,1)}) %reduce-scatter.13.cloned.1.call-update) | async-done | bytes 262160 | tf_op jit(solution)/shard_map/reduce_scatter | solution.py:375
  292.8 1.2 fusion.111
  296.5 16.1 %all-gather.14.cloned.1.call-done = bf16[512,1024]{1,0:T(8,128)(2,1)} async-done(((bf16[128,1024]{1,0:T(8,128)(2,1)}), bf16[512,1024]{1,0:T(8,128)(2,1)}) %all-gather.14.cloned.1.call-update) | async-done | bytes 1048592 | tf_op jit(solution)/shard_map/all_gather | solution.py:372
  312.6 8.6 %multiply_convert_fusion.2 = (bf16[512,1024]{1,0:T(8,128)(2,1)}, f32[512,1024]{1,0:T(8,128)}, f32[512,1024]{1,0:T(8,128)}) fusion(bf16[512,1024]{1,0:T(8,128)(2,1)} %all-gather.14.cloned.1.call-done, bf16[1024,1024]{1,0:T(8,128)(2,1)} %get-tuple-element.27), kind=kOutput, calls=%fused_computation.26 | convolution fusion | flops 1107820544 | bytes 8388608 | tf_op jit(solution)/shard_map/td,df->tf/dot_general | solution.py:315
  321.3 9.7 %all-gather.24.cloned.1.call-done = bf16[1,512,1024]{2,1,0:T(8,128)(2,1)} async-done(((bf16[1,128,1024]{2,1,0:T(8,128)(2,1)}), bf16[1,512,1024]{2,1,0:T(8,128)(2,1)}) %all-gather.24.cloned.1.call-update) | async-done | bytes 1048592 | tf_op jit(solution)/shard_map/all_gather | solution.py:372
  330.9 5.1 add_convert_fusion.2
  337.0 2.3 convolution_convert_fusion.3
  339.4 4.2 convolution_convert_fusion.4
  343.6 20.7 %reduce-scatter.17.cloned.1.call-done = bf16[128,1024]{1,0:T(8,128)(2,1)} async-done(((bf16[512,1024]{1,0:T(8,128)(2,1)}), bf16[128,1024]{1,0:T(8,128)(2,1)}) %reduce-scatter.17.cloned.1.call-update) | async-done | bytes 262160 | tf_op jit(solution)/shard_map/reduce_scatter | solution.py:375
  364.4 1.4 fusion.57
  365.8 26.2 %reduce-scatter.15.cloned.1.call-done = bf16[128,1024]{1,0:T(8,128)(2,1)} async-done(((bf16[512,1024]{1,0:T(8,128)(2,1)}), bf16[128,1024]{1,0:T(8,128)(2,1)}) %reduce-scatter.15.cloned.1.call-update) | async-done | bytes 262160 | tf_op jit(solution)/shard_map/reduce_scatter | solution.py:375
  392.0 2.1 fusion.109
  394.9 1.8 fusion.96
  396.8 16.8 %all-gather.16.cloned.1.call-done = bf16[512,1024]{1,0:T(8,128)(2,1)} async-done(((bf16[128,1024]{1,0:T(8,128)(2,1)}), bf16[512,1024]{1,0:T(8,128)(2,1)}) %all-gather.16.cloned.1.call-update) | async-done | bytes 1048592 | tf_op jit(solution)/shard_map/all_gather | solution.py:372
  413.6 1.8 convolution_convert_fusion.18
  415.5 3.2 multiply_reduce_fusion.1
  419.1 1.2 multiply_convert_fusion.1
  420.3 1.3 copy-done.11
  422.8 1.5 convolution_convert_fusion.2
  424.7 4.3 convolution_convert_fusion.refs_5_
  429.0 20.4 %reduce-scatter.19.cloned.1.call-done = bf16[128,1024]{1,0:T(8,128)(2,1)} async-done(((bf16[512,1024]{1,0:T(8,128)(2,1)}), bf16[128,1024]{1,0:T(8,128)(2,1)}) %reduce-scatter.19.cloned.1.call-update) | async-done | bytes 262160 | tf_op jit(solution)/shard_map/reduce_scatter | solution.py:375
  449.3 1.3 convert_reduce_fusion.2
  450.6 1.4 fusion.58
  452.1 2.5 fusion.108
  454.6 4.3 convolution_convert_fusion.1.refs_4_
  462.9 1.5 add_convert_fusion
  464.5 6.9 all-gather.18.cloned.1.call-done
  471.4 1.8 convolution_convert_fusion.17
  473.3 3.1 multiply_reduce_fusion
  476.7 1.2 multiply_convert_fusion
  481.2 1.5 add_convert_fusion.1
  483.0 1.7 fusion.28
  485.8 1.4 pad_maximum_fusion.1.refs_2_
  487.1 1.3 convolution_convert_fusion.7.refs_3_
  488.4 10.7 %reduce-scatter.23.cloned.1.call-done = bf16[128,1024]{1,0:T(8,128)(2,1)} async-done(((bf16[512,1024]{1,0:T(8,128)(2,1)}), bf16[128,1024]{1,0:T(8,128)(2,1)}) %reduce-scatter.23.cloned.1.call-update) | async-done | bytes 262160 | tf_op jit(solution)/shard_map/reduce_scatter | solution.py:375
  499.1 1.8 bitcast_convert_fusion
  502.4 1.3 pad_maximum_fusion.refs_0_
  503.7 1.3 convolution_convert_fusion.11.refs_1_
  505.0 123.3 %rs.1 = (f32[3,128,256]{2,1,0:T(8,128)}, f32[128,256]{1,0:T(8,128)}, f32[3,128,256]{2,1,0:T(8,128)}, f32[128,256]{1,0:T(8,128)}, f32[128,1024]{1,0:T(8,128)}, /*index=5*/f32[512,256]{1,0:T(8,128)}) custom-call(bf16[3,1024,256]{2,1,0:T(8,128)(2,1)} %pad_maximum_fusion.refs_0_, bf16[256,1024]{1,0:T(8,128)(2,1)} %convolution_convert_fusion.11.refs_1_, ...), custom_call_target="tpu_custom_call" | custom-call | tf_op jit(solution)/shard_map/rs/pallas_call | solution.py:292
  628.4 1.3 fusion.55
  629.7 1.4 fusion.59
  632.2 1.1 add_bitcast_fusion
  633.3 133.1 %reduce-scatter.25.cloned.1.call-done = f32[32,6]{1,0:T(8,128)} async-done(((f32[1024,6]{1,0:T(8,128)}), f32[32,6]{1,0:T(8,128)}) %reduce-scatter.25.cloned.1.call-update) | async-done | bytes 784
  (198 shorter events, 37.5 us)
Async XLA Ops:
  7.2 169.3 %all-gather.20.cloned.1.call-start = ((), (), s32[]{:S(2)}) async-start(), calls=%async_computation.19 | async-start | bytes 1310720 | tf_op jit(solution)/shard_map/all_gather | solution.py:372
  7.9 210.5 %reduce-scatter.11.cloned.1.call-start = ((), (), s32[]{:S(2)}) async-start(), calls=%async_computation.8 | async-start | bytes 1310720 | tf_op jit(solution)/shard_map/reduce_scatter | solution.py:375
  52.9 1.0 copy-start.4
  53.9 0.9 copy-start.5
  54.8 0.9 copy-start.6
  55.7 0.9 copy-start.7
  56.7 0.8 copy-start.8
  57.5 0.8 copy-start.9
  176.5 3.2 copy-start.16
  180.1 2.9 copy-start.13
  180.6 7.1 copy-start.46
  187.7 3.5 copy-start.1
  190.5 27.9 %copy-start.10 = (bf16[1,128,1024]{2,1,0:T(8,128)(2,1)S(1)}, bf16[1,128,1024]{2,1,0:T(8,128)(2,1)}, u32[]{:S(2)}) copy-start(bf16[1,128,1024]{2,1,0:T(8,128)(2,1)} %param.13) | copy-start | bytes 786436
  192.7 44.2 %all-gather.22.cloned.1.call-start = ((), (), s32[]{:S(2)}) async-start(), calls=%async_computation.20 | async-start | bytes 1310720 | tf_op jit(solution)/shard_map/all_gather | solution.py:372
  193.4 62.3 %all-gather.12.cloned.1.call-start = ((), (), s32[]{:S(2)}) async-start(), calls=%async_computation.9 | async-start | bytes 1310720 | tf_op jit(solution)/shard_map/all_gather | solution.py:372
  222.6 70.3 %reduce-scatter.13.cloned.1.call-start = ((), (), s32[]{:S(2)}) async-start(), calls=%async_computation.10 | async-start | bytes 1310720 | tf_op jit(solution)/shard_map/reduce_scatter | solution.py:375
  262.7 3.5 copy-start.3
  267.8 44.8 %all-gather.14.cloned.1.call-start = ((), (), s32[]{:S(2)}) async-start(), calls=%async_computation.11 | async-start | bytes 1310720 | tf_op jit(solution)/shard_map/all_gather | solution.py:372
  295.7 35.2 %all-gather.24.cloned.1.call-start = ((), (), s32[]{:S(2)}) async-start(), calls=%async_computation.21 | async-start | bytes 1310720 | tf_op jit(solution)/shard_map/all_gather | solution.py:372
  296.5 67.9 %reduce-scatter.17.cloned.1.call-start = ((), (), s32[]{:S(2)}) async-start(), calls=%async_computation.13 | async-start | bytes 1310720 | tf_op jit(solution)/shard_map/reduce_scatter | solution.py:375
  330.9 6.1 copy-start.53
  336.1 1.0 copy-start.57
  339.3 52.7 %reduce-scatter.15.cloned.1.call-start = ((), (), s32[]{:S(2)}) async-start(), calls=%async_computation.12 | async-start | bytes 1310720 | tf_op jit(solution)/shard_map/reduce_scatter | solution.py:375
  343.6 70.0 %all-gather.16.cloned.1.call-start = ((), (), s32[]{:S(2)}) async-start(), calls=%async_computation.14 | async-start | bytes 1310720 | tf_op jit(solution)/shard_map/all_gather | solution.py:372
  396.7 52.6 %reduce-scatter.19.cloned.1.call-start = ((), (), s32[]{:S(2)}) async-start(), calls=%async_computation.15 | async-start | bytes 1310720 | tf_op jit(solution)/shard_map/reduce_scatter | solution.py:375
  415.5 3.2 copy-start.55
  415.5 3.6 copy-start.19
  419.1 2.5 copy-start.50
  420.3 1.4 copy-start.11
  424.3 47.1 %all-gather.18.cloned.1.call-start = ((), (), s32[]{:S(2)}) async-start(), calls=%async_computation.16 | async-start | bytes 1310720 | tf_op jit(solution)/shard_map/all_gather | solution.py:372
  454.6 44.5 %reduce-scatter.23.cloned.1.call-start = ((), (), s32[]{:S(2)}) async-start(), calls=%async_computation.18 | async-start | bytes 1310720 | tf_op jit(solution)/shard_map/reduce_scatter | solution.py:375
  454.6 4.3 copy-start.12
  454.6 4.3 copy-start.49
  459.0 2.4 copy-start.20
  459.7 1.8 copy-start.56
  464.4 8.8 %copy-start.54 = (bf16[512,256]{0,1:T(8,128)(2,1)S(1)}, bf16[512,256]{0,1:T(8,128)(2,1)}, u32[]{:S(2)}) copy-start(bf16[512,256]{0,1:T(8,128)(2,1)} %convolution_convert_fusion.26) | copy-start | bytes 786436
  464.5 163.9 %reduce-scatter.21.cloned.1.call-start = ((), (), s32[]{:S(2)}) async-start(), calls=%async_computation.17 | async-start | bytes 1310720 | tf_op jit(solution)/shard_map/reduce_scatter | solution.py:375
  473.3 3.5 copy-start.18
  476.7 1.2 copy-start.48
  477.9 1.0 copy-start.47
  478.9 1.0 copy-start.29
  479.4 1.0 copy-start.27
  481.1 1.5 copy-start.36
  481.1 1.8 copy-start.21
  482.6 2.0 copy-start.26
  482.6 2.6 copy-start.23
  482.6 2.6 copy-start.38
  482.7 283.7 %reduce-scatter.25.cloned.1.call-start = ((), (), s32[]{:S(2)}) async-start(), calls=%async_computation.22 | async-start | bytes 540672
  485.2 1.9 copy-start.35
  485.2 1.9 copy-start.39
  485.7 15.1 %copy-start.14 = (bf16[512,1024]{1,0:T(8,128)(2,1)S(1)}, bf16[512,1024]{1,0:T(8,128)(2,1)}, u32[]{:S(2)}) copy-start(bf16[512,1024]{1,0:T(8,128)(2,1)} %copy-done.13) | copy-start | bytes 3145732
  485.8 15.1 %copy-start.37 = (bf16[4,64,512]{2,1,0:T(8,128)(2,1)S(1)}, bf16[4,64,512]{2,1,0:T(8,128)(2,1)}, u32[]{:S(2)}) copy-start(bf16[4,64,512]{2,1,0:T(8,128)(2,1)} %copy-done.36) | copy-start | bytes 786436
  487.1 14.3 %copy-start.30 = (bf16[4,64,512]{2,1,0:T(8,128)(2,1)S(1)}, bf16[4,64,512]{2,1,0:T(8,128)(2,1)}, u32[]{:S(2)}) copy-start(bf16[4,64,512]{2,1,0:T(8,128)(2,1)} %copy-done.29) | copy-start | bytes 786436
  488.4 13.5 %copy-start.28 = (bf16[4,64,512]{2,1,0:T(8,128)(2,1)S(1)}, bf16[4,64,512]{2,1,0:T(8,128)(2,1)}, u32[]{:S(2)}) copy-start(bf16[4,64,512]{2,1,0:T(8,128)(2,1)} %copy-done.27) | copy-start | bytes 786436
  501.9 1.8 copy-start.33
  501.9 1.8 copy-start.40
  628.3 3.9 copy-start.31
  628.3 140.2 %copy-start.45 = (f32[3,128,256]{2,1,0:T(8,128)S(1)}, f32[3,128,256]{2,1,0:T(8,128)}, u32[]{:S(2)}) copy-start(f32[3,128,256]{2,1,0:T(8,128)} %get-tuple-element.89) | copy-start | bytes 1179652
  628.4 3.8 copy-start.24
  629.7 139.6 %copy-start.52 = (f32[128,256]{1,0:T(8,128)S(1)}, f32[128,256]{1,0:T(8,128)}, u32[]{:S(2)}) copy-start(f32[128,256]{1,0:T(8,128)} %get-tuple-element.90) | copy-start | bytes 393220
  629.7 140.2 %copy-start.44 = (f32[3,128,256]{2,1,0:T(8,128)S(1)}, f32[3,128,256]{2,1,0:T(8,128)}, u32[]{:S(2)}) copy-start(f32[3,128,256]{2,1,0:T(8,128)} %get-tuple-element.91) | copy-start | bytes 1179652
  632.2 138.5 %copy-start.51 = (f32[128,256]{1,0:T(8,128)S(1)}, f32[128,256]{1,0:T(8,128)}, u32[]{:S(2)}) copy-start(f32[128,256]{1,0:T(8,128)} %get-tuple-element.92) | copy-start | bytes 393220
  632.2 139.2 %copy-start.43 = (f32[128,1024]{1,0:T(8,128)S(1)}, f32[128,1024]{1,0:T(8,128)}, u32[]{:S(2)}) copy-start(f32[128,1024]{1,0:T(8,128)} %get-tuple-element.93) | copy-start | bytes 1572868
  632.2 139.9 %copy-start.42 = (f32[512,256]{1,0:T(8,128)S(1)}, f32[512,256]{1,0:T(8,128)}, u32[]{:S(2)}) copy-start(f32[512,256]{1,0:T(8,128)} %get-tuple-element.94) | copy-start | bytes 1572868
  (9 other events, 6.7 us)
Sparse Core Ops, SparseCore 0:
  9.6 19.5 all-gather.19
  192.8 25.5 reduce-scatter.10
  220.1 16.7 all-gather.21
  238.9 16.7 all-gather.11
  267.9 24.8 reduce-scatter.12
  295.9 16.7 all-gather.13
  314.2 16.7 all-gather.23
  339.4 24.8 reduce-scatter.16
  367.1 24.8 reduce-scatter.14
  396.9 16.7 all-gather.15
  424.4 24.8 reduce-scatter.18
  454.7 16.7 all-gather.17
  474.1 24.9 reduce-scatter.22
  501.5 24.8 reduce-scatter.20
  632.3 133.9 reduce-scatter.24

commit v3 on v1

v3 whole, which is shorter than its diff:
```python
import types

import jax
import jax.numpy as jnp
from jax import lax
from jax.experimental import pallas as pl
from jax.experimental.pallas import tpu as pltpu
from jax.sharding import PartitionSpec as P

HEAD_DIM = 64
F32 = jnp.float32
BF16 = jnp.bfloat16
MESH = pl.DeviceIdType.MESH
SELF, SELF_OUT, CROSS, CROSS_OUT, UP, DOWN = range(6)
MOVED = (SELF_OUT, CROSS_OUT, DOWN)
G_TOKENS, G_MEMORY, G_COT, G_A2, G_A3, G_DZ2, G_DZ1 = range(7)
R_CHAIN, R_MIXED, R_MEMORY = range(3)
LANES = 128


def nn(left, right):
    return lax.dot_general(left, right, (((1,), (0,)), ((), ())), preferred_element_type=F32)


def nt(left, right):
    return lax.dot_general(left, right, (((1,), (1,)), ((), ())), preferred_element_type=F32)


def tn(left, right):
    return lax.dot_general(left, right, (((0,), (0,)), ((), ())), preferred_element_type=F32)


def rows_at(start, size):
    return pl.ds(pl.multiple_of(start, size), size)


def normed(values):
    center = values - jnp.mean(values, axis=-1, keepdims=True)
    rate = lax.rsqrt(jnp.mean(center * center, axis=-1, keepdims=True) + 1e-05)
    return center * rate, rate


def gelu_pair(values):
    chance = 0.5 + 0.5 * lax.erf(values * 0.7071067811865476)
    density = jnp.exp(-0.5 * values * values) * 0.3989422804014327
    return values * chance, chance + values * density


def layer_kernel(A, B, S, r):
    r.dz1 = r.a3
    ins, w, grad, rb, zz, outs = r.ins, r.w, r.grad, r.rb, r.zz, r.outs
    stage, back = dict(zip(MOVED, r.stage)), dict(zip(MOVED, r.back))
    page, seq = lax.axis_index("page"), lax.axis_index("seq")
    a, b = lax.div(page, B), lax.rem(page, B)
    R = A * B // S
    Tl, D = r.tokens.shape
    T = Tl * S
    Dl = ins[SELF].shape[2]
    Fl = ins[UP].shape[1]
    own = rows_at(seq * Tl, Tl)
    to_page, to_seq = lax.rem(page, R) * S + seq, lax.div(page, R)
    from_page, from_seq = seq * R + lax.div(page, S), lax.rem(page, S)
    fixed = (to_page == page) & (to_seq == seq)
    moves = jnp.logical_not(fixed)

    def remote(src, dst, send, recv, device):
        return pltpu.make_async_remote_copy(
            src_ref=src, dst_ref=dst, send_sem=send, recv_sem=recv, device_id=device, device_id_type=MESH
        )

    def landed(dst, recv):
        remote(dst, dst, recv, recv, (page, seq)).wait_recv()

    barrier = pltpu.get_barrier_semaphore()

    def greet(device):
        pl.semaphore_signal(barrier, inc=1, device_id=device, device_id_type=MESH)

    for k in range(1, S):
        greet((page, lax.rem(seq + k, S)))
    for k in range(1, B):
        greet((a * B + lax.rem(b + k, B), seq))
    for k in range(1, A):
        greet((lax.rem(a + k, A) * B + b, seq))

    @pl.when(moves)
    def _():
        greet((to_page, to_seq))
        greet((from_page, from_seq))

    pl.semaphore_wait(barrier, S + A + B - 3 + 2 * moves.astype(jnp.int32))

    def ag_copy(i, src, dst, k):
        return remote(
            src, dst.at[own], r.ag_send.at[i, k - 1], r.ag_recv.at[i, seq], (page, lax.rem(seq + k, S))
        )

    def ag_start(i, src, dst):
        for k in range(S - 1, 0, -1):
            ag_copy(i, src, dst, k).start()

    def ag_wait(i, dst):
        for k in range(1, S):
            source = lax.rem(seq + k, S)
            landed(dst.at[rows_at(source * Tl, Tl)], r.ag_recv.at[i, source])

    def ag_sent(i, src, dst):
        for k in range(1, S):
            ag_copy(i, src, dst, k).wait_send()

    def rs_copy(i, k):
        peer = lax.rem(seq + k, S)
        return remote(
            r.part[i].at[rows_at(peer * Tl, Tl)],
            r.got[i].at[k - 1],
            r.rs_send.at[i, k - 1],
            r.rs_recv.at[i, k - 1],
            (page, peer),
        )

    def rs_start(i, term):
        part = r.part[i]
        for k in range(S - 1, -1, -1):
            at = rows_at(lax.rem(seq + k, S) * Tl, Tl)
            part[at, :] = term(at).astype(BF16)
            if k:
                rs_copy(i, k).start()

    def rs_wait(i):
        total = r.part[i][own, :].astype(F32)
        for k in range(1, S):
            rs_copy(i, k).wait_recv()
            total = total + r.got[i][k - 1].astype(F32)
        return total

    def rs_sent(i):
        for k in range(1, S):
            rs_copy(i, k).wait_send()

    def sum_all(i, value):
        buf, sent, come = r.small.at[i], r.sm_send.at[i], r.sm_recv.at[i]
        slots = r.small_got.at[i]
        buf[...] = value
        base = 0
        for count, device in (
            (S, lambda k: (page, lax.rem(seq + k, S))),
            (B, lambda k: (a * B + lax.rem(b + k, B), seq)),
            (A, lambda k: (lax.rem(a + k, A) * B + b, seq)),
        ):
            copies = [
                remote(buf, slots.at[base + k - 1], sent.at[base + k - 1], come.at[base + k - 1], device(k))
                for k in range(1, count)
            ]
            for copy in copies:
                copy.start()
            for copy in copies:
                copy.wait()
            total = buf[...]
            for k in range(1, count):
                total = total + slots[base + k - 1]
            buf[...] = total
            base += count - 1

    def window(array, g, j):
        shard = ins[g].shape
        if g in (SELF, CROSS):
            return array.at[:, rows_at(j * shard[1], shard[1]), :]
        if g == UP:
            return array.at[rows_at(j * shard[0], shard[0]), :]
        return array.at[rows_at(lax.div(j, S) * shard[0], shard[0]), rows_at(lax.rem(j, S) * shard[1], shard[1])]

    def w_copy(g, j, way, src=None):
        place = window(w[g], g, j)
        device = (page + (-B, B, -1, 1)[way], seq)
        return remote(place if src is None else src, place, r.w_send.at[g, j, way], r.w_recv.at[g, j], device)

    ways = (a > 0, a < A - 1, b > 0, b < B - 1)

    def w_forward(g, j, along, src=None):
        for way in along:
            @pl.when(ways[way])
            def _():
                w_copy(g, j, way, src).start()

    def w_local(g):
        return pltpu.make_async_copy(
            stage[g] if g in MOVED else ins[g], window(w[g], g, page), r.w_local.at[g]
        )

    def move_copy(g):
        return remote(ins[g], stage[g], r.mv_send.at[g], r.mv_recv.at[g], (to_page, to_seq))

    def move_start(g):
        @pl.when(moves)
        def _():
            move_copy(g).start()

        @pl.when(fixed)
        def _():
            pltpu.make_async_copy(ins[g], stage[g], r.mv_recv.at[g]).start()

    def w_first(g):
        src = ins[g]
        if g in MOVED:
            src = stage[g]

            @pl.when(moves)
            def _():
                move_copy(g).wait_recv()

            @pl.when(fixed)
            def _():
                pltpu.make_async_copy(ins[g], stage[g], r.mv_recv.at[g]).wait()

        w_forward(g, page, (0, 1, 2, 3), src)
        w_local(g).start()

    def w_step(g, d):
        @pl.when(a - d >= 0)
        def _():
            j = page - d * B
            landed(window(w[g], g, j), r.w_recv.at[g, j])
            w_forward(g, j, (1, 2, 3))

        @pl.when(a + d < A)
        def _():
            j = page + d * B
            landed(window(w[g], g, j), r.w_recv.at[g, j])
            w_forward(g, j, (0, 2, 3))

    def w_wait(g):
        w_local(g).wait()
        for e in range(1, B):
            for t in range(A):
                @pl.when(b - e >= 0)
                def _():
                    j = t * B + b - e
                    landed(window(w[g], g, j), r.w_recv.at[g, j])
                    w_forward(g, j, (3,))

                @pl.when(b + e < B)
                def _():
                    j = t * B + b + e
                    landed(window(w[g], g, j), r.w_recv.at[g, j])
                    w_forward(g, j, (2,))

    def w_sent(g):
        if g in MOVED:
            @pl.when(moves)
            def _():
                move_copy(g).wait_send()

        for t in range(A):
            for e in range(B):
                j = t * B + e
                for way, when in enumerate(
                    ((b == e) & (t >= a), (b == e) & (t <= a), e >= b, e <= b)
                ):
                    @pl.when(when & ways[way])
                    def _():
                        w_copy(g, j, way).wait_send()

    def y_copy(g, k, t):
        other = lax.rem(b + k, B)
        return remote(
            window(grad[g], g, t * B + other),
            rb[g].at[B - 1 - k, t],
            r.y_send.at[g, k - 1, t],
            r.y_recv.at[g, B - 1 - k, t],
            (a * B + other, seq),
        )

    def y_start(g):
        for k in range(1, B):
            for t in range(A):
                y_copy(g, k, t).start()

    def y_sum(g):
        for t in range(A):
            total = window(grad[g], g, t * B + b)[...].astype(F32)
            for slot in range(B - 1):
                landed(rb[g].at[slot, t], r.y_recv.at[g, slot, t])
                total = total + rb[g][slot, t].astype(F32)
            rb[g][0, t] = total.astype(BF16)

    def z_slot(t, at, sign):
        return jnp.where((t == at) & (sign < 0), A, t)

    def z_copy(g, t, sign):
        slot = z_slot(t, a + sign, sign)
        return remote(
            rb[g].at[0, t],
            zz[g].at[slot],
            r.z_send.at[g, t],
            r.z_recv.at[g, slot],
            (page + sign * B, seq),
        )

    def z_pass(g, sign):
        before = a - sign
        has = (before >= 0) & (before < A)
        for k in range(A - 1, 0, -1):
            t = a + sign * k

            @pl.when((t >= 0) & (t < A))
            def _():
                @pl.when(has)
                def _():
                    landed(zz[g].at[t], r.z_recv.at[g, t])
                    rb[g][0, t] = (rb[g][0, t].astype(F32) + zz[g][t].astype(F32)).astype(BF16)

                z_copy(g, t, sign).start()

    first_sign = jnp.where(2 * a < A, 1, -1)

    def back_copy(g):
        return remote(
            back[g].at[0], back[g].at[1], r.bk_send.at[g], r.bk_recv.at[g], (from_page, from_seq)
        )

    def z_total(g):
        @pl.when(a > 0)
        def _():
            landed(zz[g].at[a], r.z_recv.at[g, a])

        @pl.when(a < A - 1)
        def _():
            landed(zz[g].at[A], r.z_recv.at[g, A])

        total = rb[g][0, a].astype(F32)
        total = total + jnp.where(a > 0, zz[g][a].astype(F32), 0.0)
        total = total + jnp.where(a < A - 1, zz[g][A].astype(F32), 0.0)
        if g in MOVED:
            back[g][0] = total.astype(BF16)

            @pl.when(moves)
            def _():
                back_copy(g).start()
        else:
            outs[g][...] = total

    def z_finish(g):
        if g in MOVED:
            @pl.when(moves)
            def _():
                back_copy(g).wait()
                outs[g][...] = back[g][1].astype(F32)

            @pl.when(fixed)
            def _():
                outs[g][...] = back[g][0].astype(F32)

        for t in range(A):
            for k in range(1, B):
                y_copy(g, k, t).wait_send()

            @pl.when(t != a)
            def _():
                z_copy(g, t, jnp.where(t > a, 1, -1)).wait_send()

    token_live = r.token_counts[0]
    patch_live = r.patch_counts[0]
    gains = lambda k: r.small[0, k : k + 1, :]
    biases = lambda k: r.small[0, 3 + k : 4 + k, :]
    QB = min(256, T)
    lane = lax.broadcasted_iota(jnp.int32, (1, LANES), 1)
    halves = [(lane // HEAD_DIM == h) for h in range(2)]
    half_of = [half.astype(F32).astype(BF16) for half in halves]
    scale = HEAD_DIM ** (-0.5)

    def project(dst, left, weight):
        for n, (out, index) in enumerate(dst):
            out[...] = nn(left[...], weight[index]).astype(BF16)

    def attend(q, k, v, o, probs, live, causal):
        @pl.loop(0, Dl // LANES)
        def _(pair):
            cols = rows_at(pair * LANES, LANES)
            for block in range(T // QB):
                extent = (block + 1) * QB if causal else T
                rows = slice(block * QB, (block + 1) * QB)
                q2 = q[rows, cols]
                k2, v2 = k[:extent, cols], v[:extent, cols]
                at = lax.broadcasted_iota(jnp.int32, (QB, extent), 1)
                allowed = at < live
                if causal:
                    row = block * QB + lax.broadcasted_iota(jnp.int32, (QB, extent), 0)
                    allowed = allowed & (at <= row)
                found = []
                for h in range(2):
                    scores = nt(q2 * half_of[h], k2) * scale
                    scores = jnp.where(allowed, scores, -1e30)
                    raised = jnp.exp(scores - jnp.max(scores, axis=-1, keepdims=True))
                    share = (raised / jnp.sum(raised, axis=-1, keepdims=True)).astype(BF16)
                    probs[2 * pair + h, rows, :extent] = share
                    found.append(nn(share, v2))
                o[rows, cols] = jnp.where(halves[0], found[0], found[1]).astype(BF16)

    def attend_back(q, k, v, do, probs, dq, dk, dv, causal):
        @pl.loop(0, Dl // LANES)
        def _(pair):
            cols = rows_at(pair * LANES, LANES)
            r.dk_sum[...] = jnp.zeros_like(r.dk_sum)
            r.dv_sum[...] = jnp.zeros_like(r.dv_sum)
            for block in range(T // QB):
                extent = (block + 1) * QB if causal else T
                rows = slice(block * QB, (block + 1) * QB)
                q2, do2 = q[rows, cols], do[rows, cols]
                k2, v2 = k[:extent, cols], v[:extent, cols]
                dqs, dks, dvs = [], [], []
                for h in range(2):
                    share = probs[2 * pair + h, rows, :extent]
                    wide = share.astype(F32)
                    dp = nt(do2 * half_of[h], v2)
                    delta = jnp.sum(wide * dp, axis=-1, keepdims=True)
                    ds = (wide * (dp - delta)).astype(BF16)
                    dqs.append(nn(ds, k2))
                    dks.append(tn(ds, q2))
                    dvs.append(tn(share, do2))
                dq[rows, cols] = (jnp.where(halves[0], dqs[0], dqs[1]) * scale).astype(BF16)
                r.dk_sum[:extent, :] += jnp.where(halves[0], dks[0], dks[1])
                r.dv_sum[:extent, :] += jnp.where(halves[0], dvs[0], dvs[1])
            dk[:, cols] = (r.dk_sum[...] * scale).astype(BF16)
            dv[:, cols] = r.dv_sum[...].astype(BF16)

    def norm_back(k, values, incoming):
        unit, rate = normed(values)
        r.norm_terms[k : k + 1, :] = jnp.sum(incoming * unit, axis=0, keepdims=True)
        r.norm_terms[3 + k : 4 + k, :] = jnp.sum(incoming, axis=0, keepdims=True)
        dn = incoming * gains(k)
        return rate * (
            dn - jnp.mean(dn, axis=-1, keepdims=True) - unit * jnp.mean(dn * unit, axis=-1, keepdims=True)
        )

    def norm_own(k, values, dst):
        dst[own, :] = (normed(values)[0] * gains(k) + biases(k)).astype(BF16)

    tile = min(256, Fl)
    tiles = Fl // tile

    for g in MOVED:
        move_start(g)
    loads = []
    given = (
        (G_TOKENS, r.tokens, r.all_tokens), (G_MEMORY, r.memory, r.all_memory), (G_COT, r.cotangent, r.dyr)
    )
    for i, mine, everyone in given:
        ag_start(i, mine, everyone)
        load = pltpu.make_async_copy(mine, everyone.at[own], r.ld_sem.at[i])
        load.start()
        loads.append(load)
    w_first(SELF)
    sum_all(0, r.norms[...])
    w_first(SELF_OUT)
    w_first(CROSS)
    for load in loads:
        load.wait()
    ag_wait(G_TOKENS, r.all_tokens)

    @pl.loop(0, S)
    def _(n):
        at = rows_at(n * Tl, Tl)
        values = r.all_tokens[at, :].astype(F32)
        r.a1[at, :] = (normed(values)[0] * gains(0) + biases(0)).astype(BF16)

    w_step(SELF, 1)
    w_step(SELF_OUT, 1)
    w_step(SELF, 2)
    w_step(SELF_OUT, 2)
    w_step(SELF, 3) if A > 3 else None
    w_step(SELF_OUT, 3) if A > 3 else None
    w_step(CROSS, 1)
    w_first(CROSS_OUT)
    w_first(UP)
    w_wait(SELF)
    project(((r.q, 0), (r.k, 1), (r.v, 2)), r.a1, w[SELF])
    w_step(CROSS, 2)
    w_step(CROSS_OUT, 1)
    attend(r.q, r.k, r.v, r.o, r.p, token_live, True)
    w_step(CROSS, 3)
    w_step(CROSS_OUT, 2)
    w_wait(SELF_OUT)
    rs_start(R_CHAIN, lambda at: nn(r.o[at, :], w[SELF_OUT][...]))
    w_step(CROSS_OUT, 3)
    w_step(UP, 1)
    w_first(DOWN)
    w_wait(CROSS)
    ag_wait(G_MEMORY, r.all_memory)
    project(((r.kc, 1), (r.vc, 2)), r.all_memory, w[CROSS])
    r.x1[...] = r.all_tokens[own, :].astype(F32) + rs_wait(R_CHAIN)
    norm_own(1, r.x1[...], r.a2)
    ag_start(G_A2, r.a2.at[own], r.a2)
    rs_sent(R_CHAIN)
    w_step(UP, 2)
    w_step(DOWN, 1)
    ag_wait(G_A2, r.a2)
    project(((r.qc, 0),), r.a2, w[CROSS])
    attend(r.qc, r.kc, r.vc, r.oc, r.pc, patch_live, False)
    w_step(UP, 3)
    w_step(DOWN, 2)
    w_wait(CROSS_OUT)
    rs_start(R_CHAIN, lambda at: nn(r.oc[at, :], w[CROSS_OUT][...]))
    w_step(DOWN, 3)
    ag_wait(G_COT, r.dyr)

    @pl.loop(0, S)
    def _(n):
        at = rows_at(n * Tl, Tl)
        row = n * Tl + lax.broadcasted_iota(jnp.int32, (Tl, 1), 0)
        values = r.dyr[at, :].astype(F32)
        r.dyr[at, :] = jnp.where(row < token_live, values, 0.0).astype(BF16)

    r.x2[...] = r.x1[...] + rs_wait(R_CHAIN)
    norm_own(2, r.x2[...], r.a3)
    ag_start(G_A3, r.a3.at[own], r.a3)
    rs_sent(R_CHAIN)
    w_wait(UP)
    ag_wait(G_A3, r.a3)

    @pl.loop(0, tiles)
    def _(n):
        cols = rows_at(n * tile, tile)
        out, slope = gelu_pair(nn(r.a3[...], w[UP][:, cols]))
        r.g[:, cols] = out.astype(BF16)
        r.slope[:, cols] = slope

    w_wait(DOWN)

    @pl.loop(0, tiles)
    def _(n):
        cols = rows_at(n * tile, tile)
        r.du[:, cols] = (nt(r.dyr[...], w[DOWN][cols, :]) * r.slope[:, cols]).astype(BF16)

    rs_start(R_CHAIN, lambda at: nt(r.du[at, :], w[UP][...]))

    @pl.loop(0, tiles)
    def _(n):
        cols = rows_at(n * tile, tile)
        grad[DOWN][cols, :] = tn(r.g[:, cols], r.dyr[...]).astype(BF16)

    y_start(DOWN)

    @pl.loop(0, D // 256)
    def _(n):
        cols = rows_at(n * 256, 256)
        grad[UP][cols, :] = tn(r.a3[:, cols], r.du[...]).astype(BF16)

    y_start(UP)
    r.dx2[...] = r.dyr[own, :].astype(F32) + norm_back(2, r.x2[...], rs_wait(R_CHAIN))
    r.dz2[own, :] = r.dx2[...].astype(BF16)
    ag_start(G_DZ2, r.dz2.at[own], r.dz2)
    rs_sent(R_CHAIN)
    rs_start(R_MIXED, lambda at: nn(r.g[at, :], w[DOWN][...]))
    ag_wait(G_DZ2, r.dz2)
    r.do[...] = nt(r.dz2[...], w[CROSS_OUT][...]).astype(BF16)
    attend_back(
        r.qc, r.kc, r.vc, r.do, r.pc, r.dq, r.dk, r.dv, False
    )
    rs_start(R_CHAIN, lambda at: nt(r.dq[at, :], w[CROSS][0]))
    y_sum(DOWN)
    z_pass(DOWN, first_sign)
    grad[CROSS_OUT][...] = tn(r.oc[...], r.dz2[...]).astype(BF16)
    for n, (left, right) in enumerate(((r.a2, r.dq), (r.all_memory, r.dk), (r.all_memory, r.dv))):
        grad[CROSS][n] = tn(left[...], right[...]).astype(BF16)
    y_start(CROSS_OUT)
    y_start(CROSS)
    r.dx1[...] = r.dx2[...] + norm_back(1, r.x1[...], rs_wait(R_CHAIN))
    ag_sent(G_A3, r.a3.at[own], r.a3)
    r.dz1[own, :] = r.dx1[...].astype(BF16)
    ag_start(G_DZ1, r.dz1.at[own], r.dz1)
    rs_sent(R_CHAIN)
    rs_start(
        R_MEMORY, lambda at: nt(r.dk[at, :], w[CROSS][1]) + nt(r.dv[at, :], w[CROSS][2])
    )
    z_pass(DOWN, -first_sign)
    ag_wait(G_DZ1, r.dz1)
    r.do[...] = nt(r.dz1[...], w[SELF_OUT][...]).astype(BF16)
    attend_back(r.q, r.k, r.v, r.do, r.p, r.dq, r.dk, r.dv, True)
    rs_start(
        R_CHAIN,
        lambda at: nt(r.dq[at, :], w[SELF][0])
        + nt(r.dk[at, :], w[SELF][1])
        + nt(r.dv[at, :], w[SELF][2]),
    )
    y_sum(UP)
    z_pass(UP, first_sign)
    grad[SELF_OUT][...] = tn(r.o[...], r.dz1[...]).astype(BF16)
    for n, right in enumerate((r.dq, r.dk, r.dv)):
        grad[SELF][n] = tn(r.a1[...], right[...]).astype(BF16)
    y_start(SELF_OUT)
    y_start(SELF)
    z_total(DOWN)
    z_pass(UP, -first_sign)
    live_row = (seq * Tl + lax.broadcasted_iota(jnp.int32, (Tl, 1), 0)) < token_live
    r.mixed[...] = jnp.where(live_row, r.x2[...] + rs_wait(R_MIXED), 0.0).astype(BF16)
    r.memory_grad[...] = rs_wait(R_MEMORY)
    r.input_grad[...] = r.dx1[...] + norm_back(
        0, r.all_tokens[own, :].astype(F32), rs_wait(R_CHAIN)
    )
    y_sum(CROSS_OUT)
    z_pass(CROSS_OUT, first_sign)
    y_sum(CROSS)
    z_pass(CROSS, first_sign)
    z_total(UP)
    z_pass(CROSS_OUT, -first_sign)
    z_pass(CROSS, -first_sign)
    y_sum(SELF_OUT)
    z_pass(SELF_OUT, first_sign)
    y_sum(SELF)
    z_pass(SELF, first_sign)
    z_pass(SELF_OUT, -first_sign)
    z_total(CROSS_OUT)
    z_total(CROSS)
    r.norm_terms[6:8, :] = jnp.zeros((2, D), F32)
    sum_all(1, r.norm_terms[...])
    r.norm_sums[...] = r.small[1]
    z_pass(SELF, -first_sign)
    z_total(SELF_OUT)
    z_total(SELF)

    for i in (R_CHAIN, R_MIXED, R_MEMORY):
        rs_sent(i)
    for i, mine, everyone in given:
        ag_sent(i, mine, everyone)
    for i, everyone in ((G_A2, r.a2), (G_DZ2, r.dz2), (G_DZ1, r.dz1)):
        ag_sent(i, everyone.at[own], everyone)
    for g in range(6):
        w_sent(g)
        z_finish(g)


def layer_call(A, B, S, rows, weights, norms, counts):
    V = pltpu.VMEM
    Tl, D = rows[0].shape
    T = Tl * S
    Dl = weights[SELF].shape[2]
    Fl = weights[UP].shape[1]
    pages = A * B
    R = pages // S
    heads = Dl // HEAD_DIM
    shards = [x.shape for x in weights]
    full = []
    for g, s in enumerate(shards):
        if g in (SELF, CROSS):
            full.append((s[0], s[1] * pages, s[2]))
        elif g == UP:
            full.append((s[0] * pages, s[1]))
        else:
            full.append((s[0] * R, s[1] * S))
    hbm, vmem, smem = (pl.BlockSpec(memory_space=m) for m in (pl.ANY, V, pltpu.SMEM))
    shape = jax.ShapeDtypeStruct
    dma = pltpu.SemaphoreType.DMA
    small_slots = S + A + B - 3
    row_ref, wide_ref = V((T, D), BF16), V((T, Dl), BF16)
    own_ref, hidden_ref = V((Tl, D), F32), V((T, Fl), BF16)
    operands = dict(
        tokens=rows[0],
        memory=rows[1],
        cotangent=rows[2],
        ins=list(weights),
        norms=norms,
        token_counts=counts[0],
        patch_counts=counts[1],
    )
    specs = dict(
        tokens=hbm, memory=hbm, cotangent=hbm, ins=[hbm] * 6, norms=vmem, token_counts=smem, patch_counts=smem
    )
    results = dict(
        mixed=shape((Tl, D), BF16),
        input_grad=shape((Tl, D), F32),
        memory_grad=shape((Tl, D), F32),
        outs=[shape(s, F32) for s in shards],
        norm_sums=shape((8, D), F32),
    )
    scratch = dict(
        w=[V(s, BF16) for s in full],
        grad=[V(s, BF16) for s in full],
        rb=[V((B - 1, A, *s), BF16) for s in shards],
        zz=[V((A + 1, *s), BF16) for s in shards],
        stage=[V(shards[g], BF16) for g in MOVED],
        back=[V((2, *shards[g]), BF16) for g in MOVED],
        all_tokens=row_ref,
        all_memory=row_ref,
        dyr=row_ref,
        a1=row_ref,
        a2=row_ref,
        a3=row_ref,
        dz2=row_ref,
        q=wide_ref,
        k=wide_ref,
        v=wide_ref,
        o=wide_ref,
        qc=wide_ref,
        kc=wide_ref,
        vc=wide_ref,
        oc=wide_ref,
        do=wide_ref,
        dq=wide_ref,
        dk=wide_ref,
        dv=wide_ref,
        p=V((heads, T, T), BF16),
        pc=V((heads, T, T), BF16),
        g=hidden_ref,
        du=hidden_ref,
        slope=V((T, Fl), F32),
        x1=own_ref,
        x2=own_ref,
        dx1=own_ref,
        dx2=own_ref,
        dk_sum=V((T, LANES), F32),
        dv_sum=V((T, LANES), F32),
        part=[row_ref] * 3,
        got=[V((S - 1, Tl, D), BF16)] * 3,
        small=V((2, 8, D), F32),
        small_got=V((2, small_slots, 8, D), F32),
        norm_terms=V((8, D), F32),
        ag_send=dma((7, S - 1)),
        ag_recv=dma((7, S)),
        rs_send=dma((3, S - 1)),
        rs_recv=dma((3, S - 1)),
        sm_send=dma((2, small_slots)),
        sm_recv=dma((2, small_slots)),
        ld_sem=dma((3,)),
        w_send=dma((6, pages, 4)),
        w_recv=dma((6, pages)),
        w_local=dma((6,)),
        mv_send=dma((6,)),
        mv_recv=dma((6,)),
        y_send=dma((6, B - 1, A)),
        y_recv=dma((6, B - 1, A)),
        z_send=dma((6, A)),
        z_recv=dma((6, A + 1)),
        bk_send=dma((6,)),
        bk_recv=dma((6,)),
    )
    parts = [jax.tree.flatten(part) for part in (operands, specs, results, scratch)]
    values, in_specs, out_shape, scratch_shapes = (leaves for leaves, _ in parts)
    ends = [len(values), len(values) + len(out_shape)]

    def kernel(*refs):
        held = (refs[: ends[0]], refs[ends[0] : ends[1]], refs[ends[1] :])
        r = types.SimpleNamespace()
        for (_, tree), some in zip((parts[0], parts[2], parts[3]), held):
            vars(r).update(jax.tree.unflatten(tree, some))
        layer_kernel(A, B, S, r)

    found = pl.pallas_call(
        kernel,
        out_shape=out_shape,
        in_specs=in_specs,
        out_specs=[vmem] * len(out_shape),
        scratch_shapes=scratch_shapes,
        compiler_params=pltpu.CompilerParams(
            collective_id=0, has_side_effects=True, vmem_limit_bytes=62 * 2**20
        ),
        name="layer",
    )(*values)
    return jax.tree.unflatten(parts[2][1], found)


def per_device(
    tokens,
    memory,
    cotangent,
    self_qkv,
    self_out,
    cross_qkv,
    cross_out,
    up_weight,
    down_weight,
    norm_gains,
    norm_biases,
    token_counts,
    patch_counts,
):
    pages = lax.axis_size("page")
    parts = lax.axis_size("seq")
    wide = 2 if pages == 8 else 8
    features = tokens.shape[2]
    few = norm_gains.shape[1]
    place = (lax.axis_index("page") * parts + lax.axis_index("seq")) * few
    norms = lax.dynamic_update_slice(
        jnp.zeros((8, features), F32),
        jnp.concatenate([norm_gains, norm_biases]).astype(F32),
        (0, place),
    )
    found = layer_call(
        pages // wide,
        wide,
        parts,
        (tokens[0], memory[0], cotangent[0]),
        (self_qkv, self_out, cross_qkv, cross_out, up_weight, down_weight),
        norms,
        (token_counts, patch_counts),
    )
    norm_own = lax.dynamic_slice(found["norm_sums"], (0, place), (8, few))
    return (
        found["mixed"][None],
        found["input_grad"][None],
        found["memory_grad"][None],
        *found["outs"],
        norm_own[:3],
        norm_own[3:6],
    )


def solution(mesh):
    rows = P("page", "seq", None)
    stack = P(None, "page", "seq")
    flat = P("page", "seq")
    norm = P(None, ("page", "seq"))
    counts = P("page")
    return jax.shard_map(
        per_device,
        mesh=mesh,
        in_specs=(rows, rows, rows, stack, flat, stack, flat, flat, flat, norm, norm, counts, counts),
        out_specs=(rows, rows, rows, stack, flat, stack, flat, flat, flat, norm, norm),
        check_vma=False,
    )
```

time: 1170 us -> 311 us (0.27); the launches traced: 1160 us -> 311 us
  waiting for transfers between devices: 861 us -> 0 us
  Pallas kernels: 0 us -> 297 us
  blocking collectives: 121 us -> 0 us
  matrix products: 86.7 us -> 0 us
  other arithmetic: 37.9 us -> 0.01 us
  local copies, waits for them, and re-layouts: 30.4 us -> 11.9 us
  between operations: 16.6 us -> 2.03 us
    reduce_scatter x13 -> x0, waiting for transfers between devices: 530 us -> none  [the longest x3 206 us: sum_pages(): lax.psum_scatter(grad.astype(BF16), 'page', scatter_dimension=axis, tiled...]
    pallas_call x0 -> x1, Pallas kernels: none -> 297 us  [layer_call(): pl.pallas_call(kernel, out_shape=out_shape, in_specs=in_specs, out_specs=...]
    all_gather x11 -> x0, waiting for transfers between devices: 196 us -> none  [the longest x7 74.3 us: gather_seq(): return lax.all_gather(rows, 'seq', axis=0, tiled=True)]
    unnamed x26 -> x0, waiting for transfers between devices: 135 us -> none
    all_gather x3 -> x0, blocking collectives: 121 us -> none  [the longest x2 63.8 us: rows_of(): blocks = lax.all_gather(piece, 'page', axis=0, tiled=False)]
    dot_general x40 -> x0, matrix products: 79.5 us -> none  [dot(): return jnp.einsum(spec, left, right, preferred_element_type=F32)]
    reduce_sum x13 -> x0, other arithmetic: 15.4 us -> none  [the longest x5 5.95 us: layer_norm(): center = values - jnp.mean(values, axis=-1, keepdims=True)]
    convert_element_type x11 -> x1, other arithmetic: 14 us -> 0.01 us  [per_device(): jnp.concatenate([norm_gains, norm_biases]).astype(F32)]
  transfers between devices with their start and end apart: 27 -> 0, of which waited for: 21 -> 0; matrix products, arithmetic and copies ran while one was open for 8% -> 0% of each run, Pallas kernels for 0% -> 0%
where the time goes in v3:
time: 311 us
  Pallas kernels  297 us (95%)
  local copies, waits for them, and re-layouts  11.9 us (4%)
    pallas_call x1, Pallas kernels, layer_call(): pl.pallas_call(kernel, out_shape=out_shape, in_specs=in_specs, out_specs=...  297 us
    unnamed x31, local copies, waits for them, and re-layouts  10.1 us

profile of v3, /device:TPU:0, one launch (start us, length us, event | category | flops | bytes accessed | tf_op | source)
XLA Modules:
  0.0 310.7 jit_solution(15453699878500001584)
XLA Ops:
  0.6 0.0 copy-start.9
  0.7 0.0 copy-start.10
  0.7 0.7 copy-done.9
  1.3 0.0 copy-done.10
  1.4 0.4 dynamic_update_slice.3.refs_8_
  1.8 0.0 copy-start.6
  3.1 0.0 copy-done.6
  3.1 296.7 %layer.1 = (f32[128,1024]{1,0:T(8,128)}, f32[128,1024]{1,0:T(8,128)}, bf16[128,1024]{1,0:T(8,128)(2,1)}, f32[8,1024]{1,0:T(8,128)}, f32[3,128,256]{2,1,0:T(8,128...) custom-call(bf16[128,1024]{1,0:T(8,128)(2,1)} %bitcast.8, ...), custom_call_target="tpu_custom_call" | custom-call | tf_op jit(solution)/shard_map/layer/pallas_call | solution.py:747
  299.9 0.0 copy-start.3
  299.9 0.8 constant_dynamic-slice_fusion
  300.7 0.6 fusion
  301.3 1.7 copy.36
  303.0 0.0 copy-done.3
  303.0 0.0 copy-start.2
  303.0 0.8 copy.37
  303.8 0.4 copy-done.2
  304.2 0.0 copy-start.5
  304.2 0.8 copy.38
  305.0 0.4 copy-done.5
  305.4 0.0 copy-start.8
  305.4 0.0 copy-start.4
  305.4 0.7 copy.39
  306.1 0.2 copy-done.8
  306.4 0.7 copy.40
  307.0 0.0 copy-done.4
  307.0 0.0 copy-start.7
  307.0 0.0 copy-start.1
  307.0 0.7 copy.41
  307.8 0.2 copy-done.7
  308.0 0.7 copy.42
  308.7 0.0 copy-done.1
  308.7 0.0 copy-start
  308.7 0.8 copy.43
  309.5 0.4 copy-done
  309.9 0.8 copy.44
  (2 shorter events, 0.0 us)
Async XLA Ops:
  0.6 0.7 copy-start.9
  0.7 0.7 copy-start.10
  1.8 1.3 copy-start.6
  299.9 3.1 copy-start.3
  303.0 1.2 copy-start.2
  304.2 1.2 copy-start.5
  305.4 1.0 copy-start.8
  305.4 1.7 copy-start.4
  307.0 1.0 copy-start.7
  307.0 1.7 copy-start.1
  308.7 1.2 copy-start

commit v4 on v3

v4 whole, which is shorter than its diff:
```python
import types

import jax
import jax.numpy as jnp
from jax import lax
from jax.experimental import pallas as pl
from jax.experimental.pallas import tpu as pltpu
from jax.sharding import PartitionSpec as P

HEAD_DIM = 64
F32 = jnp.float32
BF16 = jnp.bfloat16
MESH = pl.DeviceIdType.MESH
SELF, SELF_OUT, CROSS, CROSS_OUT, UP, DOWN = range(6)
MOVED = (SELF_OUT, CROSS_OUT, DOWN)
UNITS = ((SELF, 0), (SELF, 1), (SELF, 2), (CROSS, 0), (CROSS, 1), (CROSS, 2), (UP, None))
SELF_UNITS, CROSS_UNITS, UP_UNIT = (0, 1, 2), (3, 4, 5), 6
G_TOKENS, G_MEMORY, G_COT, G_A2, G_A3, G_DZ2, G_DZ1 = range(7)
R_CHAIN, R_MIXED, R_MEMORY = range(3)
LANES = 128


def nn(left, right):
    return lax.dot_general(left, right, (((1,), (0,)), ((), ())), preferred_element_type=F32)


def nt(left, right):
    return lax.dot_general(left, right, (((1,), (1,)), ((), ())), preferred_element_type=F32)


def tn(left, right):
    return lax.dot_general(left, right, (((0,), (0,)), ((), ())), preferred_element_type=F32)


def rows_at(start, size):
    return pl.ds(pl.multiple_of(start, size), size)


def normed(values):
    center = values - jnp.mean(values, axis=-1, keepdims=True)
    rate = lax.rsqrt(jnp.mean(center * center, axis=-1, keepdims=True) + 1e-05)
    return center * rate, rate


def gelu_pair(values):
    chance = 0.5 + 0.5 * lax.erf(values * 0.7071067811865476)
    density = jnp.exp(-0.5 * values * values) * 0.3989422804014327
    return values * chance, chance + values * density


def layer_kernel(A, B, S, r):
    r.dz1 = r.a3
    r.part = [r.chain_part, r.dz2, r.a2]
    ins, w, grad, outs = r.ins, r.w, r.grad, r.outs
    page, seq = lax.axis_index("page"), lax.axis_index("seq")
    a, b = lax.div(page, B), lax.rem(page, B)
    R = A * B // S
    Tl, D = r.tokens.shape
    T = Tl * S
    Dl = ins[SELF].shape[2]
    Fl = ins[UP].shape[1]
    own = rows_at(seq * Tl, Tl)
    shelf, collector = lax.rem(page, R), lax.div(page, R)
    collects = seq == collector
    a0, b0 = lax.div(seq * R, B), lax.rem(seq * R, B)
    mine = b - b0
    holds = (mine >= 0) & (mine < R)

    def remote(src, dst, send, recv, device):
        return pltpu.make_async_remote_copy(
            src_ref=src, dst_ref=dst, send_sem=send, recv_sem=recv, device_id=device, device_id_type=MESH
        )

    def landed(dst, recv):
        remote(dst, dst, recv, recv, (page, seq)).wait_recv()

    barrier = pltpu.get_barrier_semaphore()

    def greet(device):
        pl.semaphore_signal(barrier, inc=1, device_id=device, device_id_type=MESH)

    for k in range(1, S):
        greet((page, lax.rem(seq + k, S)))
    for k in range(1, B):
        greet((a * B + lax.rem(b + k, B), seq))
    for k in range(1, A):
        greet((lax.rem(a + k, A) * B + b, seq))

    pl.semaphore_wait(barrier, S + A + B - 3)

    X = S // 2
    chip, core = lax.div(seq, 2), lax.rem(seq, 2)
    sibling = chip * 2 + 1 - core
    half = Tl // 2

    def part_of(source, ch):
        return rows_at(source * Tl + ch * half, half)

    def chip_at(dx):
        return lax.rem(chip + dx, X)

    def ag_copy(i, src, dst, ch, n):
        source = chip_at(2 * X - 1 - n) * 2 + core if n >= X else seq
        mine = dst.at[part_of(source, ch)] if n >= X else src.at[rows_at(ch * half, half)]
        to = chip_at(n) * 2 + core if 0 < n < X else sibling
        return remote(
            mine, dst.at[part_of(source, ch)], r.ag_send.at[i, ch, n], r.ag_recv.at[i, ch, source], (page, to)
        )

    def ag_start(i, src, dst, ch):
        for n in (*range(1, X), 0):
            ag_copy(i, src, dst, ch, n).start()

    def ag_begin(i, src, dst):
        for ch in range(2):
            ag_start(i, src, dst, ch)

    def ag_forward(i, dst):
        for ch in range(2):
            for n in range(X, 2 * X - 1):
                source = chip_at(2 * X - 1 - n) * 2 + core
                landed(dst.at[part_of(source, ch)], r.ag_recv.at[i, ch, source])
                ag_copy(i, None, dst, ch, n).start()

    def ag_wait(i, dst):
        for ch in range(2):
            for x in range(X):
                source = 2 * x + 1 - core
                landed(dst.at[part_of(source, ch)], r.ag_recv.at[i, ch, source])

    def ag_sent(i, src, dst):
        for ch in range(2):
            for n in range(2 * X - 1):
                ag_copy(i, src, dst, ch, n).wait_send()

    def rs_copy(i, x, ch):
        return remote(
            r.part[i].at[part_of(x * 2 + 1 - core, ch)],
            r.got[i].at[x, rows_at(ch * half, half)],
            r.rs_send.at[i, ch, x],
            r.rs_recv.at[i, ch, x],
            (page, sibling),
        )

    def rs_far(i, dx, ch):
        to = chip_at(dx) * 2 + core
        slot = X + dx - 1
        return remote(
            r.part[i].at[part_of(to, ch)],
            r.got[i].at[slot, rows_at(ch * half, half)],
            r.rs_send.at[i, ch, slot],
            r.rs_recv.at[i, ch, slot],
            (page, to),
        )

    def rs_start(i, term):
        part, got = r.part[i], r.got[i]
        for n in range(1, X + 1):
            x = chip_at(n)
            at = rows_at((x * 2 + 1 - core) * Tl, Tl)
            part[at, :] = term(at).astype(BF16)
            for ch in range(2):
                rs_copy(i, x, ch).start()
        for dx in range(1, X):
            x = chip_at(dx)
            at = rows_at((x * 2 + core) * Tl, Tl)
            mine = term(at)
            for ch in range(2):
                rs_copy(i, x, ch).wait_recv()
                other = got[x, ch * half : (ch + 1) * half, :].astype(F32)
                part[part_of(x * 2 + core, ch), :] = (mine[ch * half : (ch + 1) * half] + other).astype(BF16)
                rs_far(i, dx, ch).start()
        part[own, :] = term(own).astype(BF16)

    def rs_wait(i, ch):
        rows = slice(ch * half, (ch + 1) * half)
        rs_copy(i, chip, ch).wait_recv()
        total = r.part[i][part_of(seq, ch), :].astype(F32) + r.got[i][chip, rows, :].astype(F32)
        for dx in range(1, X):
            rs_far(i, dx, ch).wait_recv()
            total = total + r.got[i][X + dx - 1, rows, :].astype(F32)
        return total

    def rs_sent(i):
        for ch in range(2):
            for x in range(X):
                rs_copy(i, x, ch).wait_send()
            for dx in range(1, X):
                rs_far(i, dx, ch).wait_send()

    def small_copies(i, level):
        count, base, device = (
            (B, 0, lambda k: (a * B + lax.rem(b + k, B), seq)),
            (A, B - 1, lambda k: (lax.rem(a + k, A) * B + b, seq)),
            (S, A + B - 2, lambda k: (page, lax.rem(seq + k, S))),
        )[level]
        return [
            remote(
                r.small.at[i],
                r.small_got.at[i, base + k - 1],
                r.sm_send.at[i, base + k - 1],
                r.sm_recv.at[i, base + k - 1],
                device(k),
            )
            for k in range(1, count)
        ], base

    def small_start(i, level):
        for copy in small_copies(i, level)[0]:
            copy.start()

    def small_wait(i, level):
        copies, base = small_copies(i, level)
        for copy in copies:
            copy.wait()
        total = r.small[i]
        for k in range(len(copies)):
            total = total + r.small_got[i, base + k]
        r.small[i] = total

    def rows_of(arrays, u, j):
        g, n = UNITS[u]
        size = ins[g].shape[-2]
        at = rows_at(j * size, size)
        return arrays[g].at[at, :] if n is None else arrays[g].at[n, at, :]

    def whole_of(arrays, u):
        g, n = UNITS[u]
        return arrays[g] if n is None else arrays[g].at[n]

    def w_copy(u, j, way, src=None):
        place = rows_of(w, u, j)
        device = (page + (-B, B, -1, 1)[way], seq)
        return remote(place if src is None else src, place, r.w_send.at[u, j, way], r.w_recv.at[u, j], device)

    ways = (a > 0, a < A - 1, b > 0, b < B - 1)

    def w_forward(u, j, along, src=None):
        for way in along:
            @pl.when(ways[way])
            def _():
                w_copy(u, j, way, src).start()

    def w_local(u):
        return pltpu.make_async_copy(whole_of(ins, u), rows_of(w, u, page), r.w_local.at[u])

    def w_first(*units):
        for u in units:
            w_forward(u, page, (0, 1, 2, 3), whole_of(ins, u))
            w_local(u).start()

    def w_step(d, *units):
        for u in units:
            @pl.when(a - d >= 0)
            def _():
                j = page - d * B
                landed(rows_of(w, u, j), r.w_recv.at[u, j])
                w_forward(u, j, (1, 2, 3))

            @pl.when(a + d < A)
            def _():
                j = page + d * B
                landed(rows_of(w, u, j), r.w_recv.at[u, j])
                w_forward(u, j, (0, 2, 3))

    def w_wait(*units):
        for u in units:
            w_local(u).wait()
            for e in range(1, B):
                for t in range(A):
                    @pl.when(b - e >= 0)
                    def _():
                        j = t * B + b - e
                        landed(rows_of(w, u, j), r.w_recv.at[u, j])
                        w_forward(u, j, (3,))

                    @pl.when(b + e < B)
                    def _():
                        j = t * B + b + e
                        landed(rows_of(w, u, j), r.w_recv.at[u, j])
                        w_forward(u, j, (2,))

    def w_sent(u):
        for t in range(A):
            for e in range(B):
                j = t * B + e
                for way, when in enumerate(
                    ((b == e) & (t >= a), (b == e) & (t <= a), e >= b, e <= b)
                ):
                    @pl.when(when & ways[way])
                    def _():
                        w_copy(u, j, way).wait_send()

    def block(array, g, e, n):
        rows, cols = ins[g].shape
        return array.at[rows_at(e * rows, rows), rows_at(n * cols, cols)]

    def m_local(g):
        return pltpu.make_async_copy(ins[g], block(w[g], g, shelf, seq), r.m_got.at[MOVED.index(g), seq])

    def m_collect_copy(g):
        i = MOVED.index(g)
        return remote(
            ins[g], block(w[g], g, shelf, seq), r.m_gave.at[i], r.m_got.at[i, seq], (page, collector)
        )

    def m_collect(g):
        @pl.when(collects)
        def _():
            m_local(g).start()

        @pl.when(jnp.logical_not(collects))
        def _():
            m_collect_copy(g).start()

    def m_copy(g, n, way):
        i = MOVED.index(g)
        place = block(w[g], g, mine, n)
        device = (page + B, page - B)[way] if way < 2 else a * B + lax.rem(b + way - 1, B)
        return remote(place, place, r.m_send.at[i, n, way], r.m_recv.at[i, mine, n], (device, seq))

    m_ways = [holds & (a >= a0) & (a < A - 1), holds & (a <= a0) & (a > 0)] + [holds] * (B - 1)

    def m_forward(g, n):
        for way in range(B + 1):
            @pl.when(m_ways[way])
            def _():
                m_copy(g, n, way).start()

    def m_first(g, n):
        @pl.when(collects)
        def _():
            @pl.when(seq == n)
            def _():
                m_local(g).wait()

            @pl.when(seq != n)
            def _():
                landed(block(w[g], g, shelf, n), r.m_got.at[MOVED.index(g), n])

            m_forward(g, n)

    def m_pass(g, n):
        @pl.when(holds & (a != a0))
        def _():
            landed(block(w[g], g, mine, n), r.m_recv.at[MOVED.index(g), mine, n])
            m_forward(g, n)

    def m_wait(g):
        for e in range(R):
            @pl.when(jnp.logical_not(holds) | (mine != e))
            def _():
                for n in range(S):
                    landed(block(w[g], g, e, n), r.m_recv.at[MOVED.index(g), e, n])

    def m_sent(g):
        @pl.when(jnp.logical_not(collects))
        def _():
            m_collect_copy(g).wait_send()

        for n in range(S):
            for way in range(B + 1):
                @pl.when(m_ways[way])
                def _():
                    m_copy(g, n, way).wait_send()

    low = 2 * a < A
    near = jnp.where(low, a, A - 1 - a)

    def order(m):
        if m == A - 1:
            return a
        t = jnp.where(m < A - 1 - near, A - 1 - m, m - (A - 1 - near))
        return jnp.where(low, t, A - 1 - t)

    def y_copy(u, k, t):
        other = lax.rem(b + k, B)
        return remote(
            rows_of(grad, u, t * B + other),
            r.rb[u].at[B - 1 - k, t],
            r.y_send.at[u, k - 1, t],
            r.y_recv.at[u, B - 1 - k, t],
            (a * B + other, seq),
        )

    def y_start(*units):
        for u in units:
            for m in range(A):
                for k in range(1, B):
                    y_copy(u, k, order(m)).start()

    def z_copy(u, t, sign):
        slot = jnp.where((t == a + sign) & (sign < 0), A, t)
        return remote(
            r.rb[u].at[0, t],
            r.zz[u].at[slot],
            r.z_send.at[u, t],
            r.z_recv.at[u, slot],
            (page + sign * B, seq),
        )

    def z_way(t):
        sign = jnp.where(t > a, 1, -1)
        before = a - sign
        return sign, (before >= 0) & (before < A)

    def y_sum(m, u):
        t = order(m)
        total = rows_of(grad, u, t * B + b)[...].astype(F32)
        for slot in range(B - 1):
            landed(r.rb[u].at[slot, t], r.y_recv.at[u, slot, t])
            total = total + r.rb[u][slot, t].astype(F32)
        r.rb[u][0, t] = total.astype(BF16)
        if m < A - 1:
            sign, has = z_way(t)

            @pl.when(jnp.logical_not(has))
            def _():
                z_copy(u, t, sign).start()

    def z_sum(m, u):
        t = order(m)
        sign, has = z_way(t)

        @pl.when(has)
        def _():
            landed(r.zz[u].at[t], r.z_recv.at[u, t])
            r.rb[u][0, t] = (r.rb[u][0, t].astype(F32) + r.zz[u][t].astype(F32)).astype(BF16)
            z_copy(u, t, sign).start()

    def z_total(u):
        @pl.when(a > 0)
        def _():
            landed(r.zz[u].at[a], r.z_recv.at[u, a])

        @pl.when(a < A - 1)
        def _():
            landed(r.zz[u].at[A], r.z_recv.at[u, A])

        total = r.rb[u][0, a].astype(F32)
        total = total + jnp.where(a > 0, r.zz[u][a].astype(F32), 0.0)
        total = total + jnp.where(a < A - 1, r.zz[u][A].astype(F32), 0.0)
        g, n = UNITS[u]
        if n is None:
            outs[g][...] = total
        else:
            outs[g][n] = total

    def z_sent(u):
        for t in range(A):
            for k in range(1, B):
                y_copy(u, k, t).wait_send()

            @pl.when(t != a)
            def _():
                z_copy(u, t, jnp.where(t > a, 1, -1)).wait_send()

    def unit_steps(*units):
        steps = [lambda: [y_sum(0, u) for u in units]]
        for m in range(1, A - 1):
            steps.append(lambda m=m: [(y_sum(m, u), z_sum(m - 1, u)) for u in units])
        steps.append(lambda: [(z_sum(A - 2, u), y_sum(A - 1, u)) for u in units])
        steps.append(lambda: [z_total(u) for u in units])
        return steps

    def f_copy(g, k, n):
        i = MOVED.index(g)
        other = lax.rem(b + k, B)
        return remote(
            block(grad[g], g, other - b0, n),
            r.fb[i].at[B - 1 - k, n],
            r.f_send.at[i, k - 1, n],
            r.f_recv.at[i, B - 1 - k, n],
            (a * B + other, seq),
        )

    def wanted(k):
        shelf_of = lax.rem(b + k, B) - b0
        return (shelf_of >= 0) & (shelf_of < R)

    def f_start(g):
        for n in range(S):
            for k in range(1, B):
                @pl.when(wanted(k))
                def _():
                    f_copy(g, k, n).start()

    inward = jnp.where(a > a0, -1, 1)
    from_out = holds & (a != a0) & (a > 0) & (a < A - 1)
    starts_line = holds & (a != a0) & ((a == 0) | (a == A - 1))

    def v_copy(g, n):
        i = MOVED.index(g)
        slot = jnp.where((a + 1 == a0), 1, 0)
        return remote(
            r.fb[i].at[0, n], r.vv[i].at[slot, n], r.v_send.at[i, n], r.v_recv.at[i, slot, n], (page + inward * B, seq)
        )

    def s_copy(g, n):
        i = MOVED.index(g)
        return remote(r.fb[i].at[0, n], r.back[i], r.s_send.at[i, n], r.s_recv.at[i], (page, n))

    def f_sum(g, n):
        i = MOVED.index(g)

        @pl.when(holds)
        def _():
            total = block(grad[g], g, mine, n)[...].astype(F32)
            for slot in range(B - 1):
                landed(r.fb[i].at[slot, n], r.f_recv.at[i, slot, n])
                total = total + r.fb[i][slot, n].astype(F32)
            r.fb[i][0, n] = total.astype(BF16)

            @pl.when(starts_line)
            def _():
                v_copy(g, n).start()

    def v_sum(g, n):
        i = MOVED.index(g)

        @pl.when(from_out)
        def _():
            landed(r.vv[i].at[0, n], r.v_recv.at[i, 0, n])
            r.fb[i][0, n] = (r.fb[i][0, n].astype(F32) + r.vv[i][0, n].astype(F32)).astype(BF16)
            v_copy(g, n).start()

    def v_total(g, n):
        i = MOVED.index(g)

        @pl.when(collects)
        def _():
            @pl.when(a < A - 1)
            def _():
                landed(r.vv[i].at[0, n], r.v_recv.at[i, 0, n])

            @pl.when(a > 0)
            def _():
                landed(r.vv[i].at[1, n], r.v_recv.at[i, 1, n])

            total = r.fb[i][0, n].astype(F32)
            total = total + jnp.where(a < A - 1, r.vv[i][0, n].astype(F32), 0.0)
            total = total + jnp.where(a > 0, r.vv[i][1, n].astype(F32), 0.0)

            @pl.when(seq == n)
            def _():
                outs[g][...] = total

            @pl.when(seq != n)
            def _():
                r.fb[i][0, n] = total.astype(BF16)
                s_copy(g, n).start()

    def s_wait(g):
        i = MOVED.index(g)

        @pl.when(jnp.logical_not(collects))
        def _():
            landed(r.back[i], r.s_recv.at[i])
            outs[g][...] = r.back[i][...].astype(F32)

    def v_sent(g):
        for n in range(S):
            for k in range(1, B):
                @pl.when(wanted(k))
                def _():
                    f_copy(g, k, n).wait_send()

            @pl.when(starts_line | from_out)
            def _():
                v_copy(g, n).wait_send()

            @pl.when(collects & (seq != n))
            def _():
                s_copy(g, n).wait_send()

    def moved_steps(g):
        steps = [lambda: f_sum(g, 0)]
        for n in range(1, S):
            steps.append(lambda n=n: (f_sum(g, n), v_sum(g, n - 1)))
        steps.append(lambda: (v_sum(g, S - 1), v_total(g, 0)))
        steps.append(lambda: [v_total(g, n) for n in range(1, S)])
        return steps

    token_live = r.token_counts[0]
    patch_live = r.patch_counts[0]
    r.norm_terms[6:8, :] = jnp.zeros((2, D), F32)
    gains = lambda k: r.small[0, k : k + 1, :]
    biases = lambda k: r.small[0, 3 + k : 4 + k, :]
    QB = min(256, T)
    lane = lax.broadcasted_iota(jnp.int32, (1, LANES), 1)
    halves = [(lane // HEAD_DIM == h) for h in range(2)]
    half_of = [half.astype(F32).astype(BF16) for half in halves]
    scale = HEAD_DIM ** (-0.5)

    def project(dst, left, weight):
        for n, (out, index) in enumerate(dst):
            out[...] = nn(left[...], weight[index]).astype(BF16)

    def attend(q, k, v, o, probs, live, causal):
        @pl.loop(0, Dl // LANES)
        def _(pair):
            cols = rows_at(pair * LANES, LANES)
            for block in range(T // QB):
                extent = (block + 1) * QB if causal else T
                rows = slice(block * QB, (block + 1) * QB)
                q2 = q[rows, cols]
                k2, v2 = k[:extent, cols], v[:extent, cols]
                at = lax.broadcasted_iota(jnp.int32, (QB, extent), 1)
                allowed = at < live
                if causal:
                    row = block * QB + lax.broadcasted_iota(jnp.int32, (QB, extent), 0)
                    allowed = allowed & (at <= row)
                found = []
                for h in range(2):
                    scores = nt(q2 * half_of[h], k2) * scale
                    scores = jnp.where(allowed, scores, -1e30)
                    raised = jnp.exp(scores - jnp.max(scores, axis=-1, keepdims=True))
                    share = (raised / jnp.sum(raised, axis=-1, keepdims=True)).astype(BF16)
                    probs[2 * pair + h, rows, :extent] = share
                    found.append(nn(share, v2))
                o[rows, cols] = jnp.where(halves[0], found[0], found[1]).astype(BF16)

    def attend_back(q, k, v, do, probs, dq, dk, dv, causal):
        @pl.loop(0, Dl // LANES)
        def _(pair):
            cols = rows_at(pair * LANES, LANES)
            r.dk_sum[...] = jnp.zeros_like(r.dk_sum)
            r.dv_sum[...] = jnp.zeros_like(r.dv_sum)
            for block in range(T // QB):
                extent = (block + 1) * QB if causal else T
                rows = slice(block * QB, (block + 1) * QB)
                q2, do2 = q[rows, cols], do[rows, cols]
                k2, v2 = k[:extent, cols], v[:extent, cols]
                dqs, dks, dvs = [], [], []
                for h in range(2):
                    share = probs[2 * pair + h, rows, :extent]
                    wide = share.astype(F32)
                    dp = nt(do2 * half_of[h], v2)
                    delta = jnp.sum(wide * dp, axis=-1, keepdims=True)
                    ds = (wide * (dp - delta)).astype(BF16)
                    dqs.append(nn(ds, k2))
                    dks.append(tn(ds, q2))
                    dvs.append(tn(share, do2))
                dq[rows, cols] = (jnp.where(halves[0], dqs[0], dqs[1]) * scale).astype(BF16)
                r.dk_sum[:extent, :] += jnp.where(halves[0], dks[0], dks[1])
                r.dv_sum[:extent, :] += jnp.where(halves[0], dvs[0], dvs[1])
            dk[:, cols] = (r.dk_sum[...] * scale).astype(BF16)
            dv[:, cols] = r.dv_sum[...].astype(BF16)

    def norm_back(k, values, incoming, ch):
        unit, rate = normed(values)
        for row, term in ((k, incoming * unit), (3 + k, incoming)):
            so_far = jnp.sum(term, axis=0, keepdims=True)
            r.norm_terms[row : row + 1, :] = so_far if ch == 0 else r.norm_terms[row : row + 1, :] + so_far
        dn = incoming * gains(k)
        return rate * (
            dn - jnp.mean(dn, axis=-1, keepdims=True) - unit * jnp.mean(dn * unit, axis=-1, keepdims=True)
        )

    def norm_own(k, values, dst, ch):
        dst[part_of(seq, ch), :] = (normed(values)[0] * gains(k) + biases(k)).astype(BF16)

    tile = min(256, Fl)
    tiles = Fl // tile

    few = r.norm_gains.shape[1]
    at_feature = lax.broadcasted_iota(jnp.int32, (few, D), 1)
    placed = at_feature == lax.broadcasted_iota(jnp.int32, (few, D), 0) + (page * S + seq) * few
    r.small[0] = jnp.zeros((8, D), F32)
    r.small[0, 0:3, :] = nn(r.norm_gains[...], placed.astype(F32).astype(BF16))
    r.small[0, 3:6, :] = nn(r.norm_biases[...], placed.astype(F32).astype(BF16))
    small_start(0, 0)
    w_first(*SELF_UNITS)
    m_collect(SELF_OUT)
    given = (
        (G_TOKENS, r.tokens, r.all_tokens), (G_MEMORY, r.memory, r.all_memory), (G_COT, r.cotangent, r.dyr)
    )
    loads = [pltpu.make_async_copy(piece, everyone.at[own], r.ld_sem.at[i]) for i, piece, everyone in given]
    ag_begin(*given[0])
    for load in loads:
        load.start()
    w_step(1, *SELF_UNITS)
    small_wait(0, 0)
    small_start(0, 1)
    m_collect(CROSS_OUT)
    ag_begin(*given[1])
    m_collect(DOWN)
    w_step(2, *SELF_UNITS)
    for n in range(S):
        m_first(SELF_OUT, n)
    small_wait(0, 1)
    small_start(0, 2)
    ag_forward(G_TOKENS, r.all_tokens)
    w_first(*CROSS_UNITS)
    ag_begin(*given[2])
    w_step(3, *SELF_UNITS)
    for n in range(S):
        m_pass(SELF_OUT, n)
    w_step(1, *CROSS_UNITS)
    small_wait(0, 2)
    ag_wait(G_TOKENS, r.all_tokens)
    for load in loads:
        load.wait()

    @pl.loop(0, S)
    def _(n):
        at = rows_at(n * Tl, Tl)
        values = r.all_tokens[at, :].astype(F32)
        r.a1[at, :] = (normed(values)[0] * gains(0) + biases(0)).astype(BF16)

    w_wait(*SELF_UNITS)
    project(((r.q, 0), (r.k, 1), (r.v, 2)), r.a1, w[SELF])
    w_step(2, *CROSS_UNITS)
    w_first(UP_UNIT)
    ag_forward(G_MEMORY, r.all_memory)
    attend(r.q, r.k, r.v, r.o, r.p, token_live, True)
    w_step(3, *CROSS_UNITS)
    m_wait(SELF_OUT)
    rs_start(R_CHAIN, lambda at: nn(r.o[at, :], w[SELF_OUT][...]))
    for n in range(S):
        m_first(CROSS_OUT, n)
    w_step(1, UP_UNIT)
    m_first(DOWN, 0)
    ag_forward(G_COT, r.dyr)
    for ch in range(2):
        rows = slice(ch * half, (ch + 1) * half)
        r.x1[rows, :] = r.all_tokens[part_of(seq, ch), :].astype(F32) + rs_wait(R_CHAIN, ch)
        norm_own(1, r.x1[rows, :], r.a2, ch)
        ag_start(G_A2, r.a2.at[own], r.a2, ch)
    rs_sent(R_CHAIN)
    for n in range(S):
        m_pass(CROSS_OUT, n)
    w_wait(*CROSS_UNITS)
    ag_wait(G_MEMORY, r.all_memory)
    project(((r.kc, 1), (r.vc, 2)), r.all_memory, w[CROSS])
    ag_forward(G_A2, r.a2)
    ag_wait(G_A2, r.a2)
    w_step(2, UP_UNIT)
    m_first(DOWN, 1)
    m_pass(DOWN, 0)
    project(((r.qc, 0),), r.a2, w[CROSS])
    attend(r.qc, r.kc, r.vc, r.oc, r.pc, patch_live, False)
    m_wait(CROSS_OUT)
    rs_start(R_CHAIN, lambda at: nn(r.oc[at, :], w[CROSS_OUT][...]))
    w_step(3, UP_UNIT)
    m_first(DOWN, 2)
    m_pass(DOWN, 1)
    m_first(DOWN, 3)
    ag_wait(G_COT, r.dyr)
    ag_sent(*given[2])

    @pl.loop(0, S)
    def _(n):
        at = rows_at(n * Tl, Tl)
        row = n * Tl + lax.broadcasted_iota(jnp.int32, (Tl, 1), 0)
        values = r.dyr[at, :].astype(F32)
        r.dyr[at, :] = jnp.where(row < token_live, values, 0.0).astype(BF16)

    for ch in range(2):
        rows = slice(ch * half, (ch + 1) * half)
        r.x2[rows, :] = r.x1[rows, :] + rs_wait(R_CHAIN, ch)
        norm_own(2, r.x2[rows, :], r.a3, ch)
        ag_start(G_A3, r.a3.at[own], r.a3, ch)
    rs_sent(R_CHAIN)
    m_pass(DOWN, 2)
    ag_forward(G_A3, r.a3)
    ag_wait(G_A3, r.a3)
    for n in range(3, S):
        m_pass(DOWN, n)
    w_wait(UP_UNIT)

    @pl.loop(0, tiles)
    def _(n):
        cols = rows_at(n * tile, tile)
        out, slope = gelu_pair(nn(r.a3[...], w[UP][:, cols]))
        r.g[:, cols] = out.astype(BF16)
        r.slope[:, cols] = slope

    @pl.loop(0, tiles)
    def _(n):
        cols = rows_at(n * tile, tile)
        grad[DOWN][cols, :] = tn(r.g[:, cols], r.dyr[...]).astype(BF16)

    f_start(DOWN)
    m_wait(DOWN)

    @pl.loop(0, tiles)
    def _(n):
        cols = rows_at(n * tile, tile)
        r.du[:, cols] = (nt(r.dyr[...], w[DOWN][cols, :]) * r.slope[:, cols]).astype(BF16)

    ag_sent(G_A3, r.a3.at[own], r.a3)
    rs_start(R_CHAIN, lambda at: nt(r.du[at, :], w[UP][...]))

    @pl.loop(0, D // 256)
    def _(n):
        cols = rows_at(n * 256, 256)
        grad[UP][cols, :] = tn(r.a3[:, cols], r.du[...]).astype(BF16)

    y_start(UP_UNIT)
    down, up = moved_steps(DOWN), unit_steps(UP_UNIT)
    down.pop(0)()
    for ch in range(2):
        rows = slice(ch * half, (ch + 1) * half)
        back_term = norm_back(2, r.x2[rows, :], rs_wait(R_CHAIN, ch), ch)
        r.dx2[rows, :] = r.dyr[part_of(seq, ch), :].astype(F32) + back_term
        r.dz2[part_of(seq, ch), :] = r.dx2[rows, :].astype(BF16)
        ag_start(G_DZ2, r.dz2.at[own], r.dz2, ch)
    rs_sent(R_CHAIN)
    down.pop(0)()
    ag_forward(G_DZ2, r.dz2)
    ag_wait(G_DZ2, r.dz2)
    r.do[...] = nt(r.dz2[...], w[CROSS_OUT][...]).astype(BF16)
    attend_back(r.qc, r.kc, r.vc, r.do, r.pc, r.dq, r.dk, r.dv, False)
    rs_start(R_CHAIN, lambda at: nt(r.dq[at, :], w[CROSS][0]))
    grad[CROSS_OUT][...] = tn(r.oc[...], r.dz2[...]).astype(BF16)
    f_start(CROSS_OUT)
    for n, (left, right) in enumerate(((r.a2, r.dq), (r.all_memory, r.dk), (r.all_memory, r.dv))):
        grad[CROSS][n] = tn(left[...], right[...]).astype(BF16)
    y_start(*CROSS_UNITS)
    down.pop(0)()
    down.pop(0)()
    for ch in range(2):
        rows = slice(ch * half, (ch + 1) * half)
        r.dx1[rows, :] = r.dx2[rows, :] + norm_back(1, r.x1[rows, :], rs_wait(R_CHAIN, ch), ch)
        r.dz1[part_of(seq, ch), :] = r.dx1[rows, :].astype(BF16)
        ag_start(G_DZ1, r.dz1.at[own], r.dz1, ch)
    rs_sent(R_CHAIN)
    up.pop(0)()
    down.pop(0)()
    ag_forward(G_DZ1, r.dz1)
    ag_wait(G_DZ1, r.dz1)
    r.do[...] = nt(r.dz1[...], w[SELF_OUT][...]).astype(BF16)
    grad[SELF_OUT][...] = tn(r.o[...], r.dz1[...]).astype(BF16)
    f_start(SELF_OUT)
    ag_sent(G_A2, r.a2.at[own], r.a2)
    rs_start(R_MEMORY, lambda at: nt(r.dk[at, :], w[CROSS][1]) + nt(r.dv[at, :], w[CROSS][2]))
    attend_back(r.q, r.k, r.v, r.do, r.p, r.dq, r.dk, r.dv, True)
    for n, right in enumerate((r.dq, r.dk, r.dv)):
        grad[SELF][n] = tn(r.a1[...], right[...]).astype(BF16)
    y_start(*SELF_UNITS)
    up.pop(0)()
    rs_start(
        R_CHAIN, lambda at: nt(r.dq[at, :], w[SELF][0]) + nt(r.dk[at, :], w[SELF][1]) + nt(r.dv[at, :], w[SELF][2])
    )
    down.pop(0)()
    up.pop(0)()
    cross_out, cross = moved_steps(CROSS_OUT), unit_steps(*CROSS_UNITS)
    self_out, selves = moved_steps(SELF_OUT), unit_steps(*SELF_UNITS)
    up.pop(0)()
    for ch in range(2):
        rows = slice(ch * half, (ch + 1) * half)
        back_term = norm_back(0, r.all_tokens[part_of(seq, ch), :].astype(F32), rs_wait(R_CHAIN, ch), ch)
        r.input_grad[rows, :] = r.dx1[rows, :] + back_term
    r.small[1] = r.norm_terms[...]
    small_start(1, 2)
    ag_sent(G_DZ2, r.dz2.at[own], r.dz2)
    rs_start(R_MIXED, lambda at: nn(r.g[at, :], w[DOWN][...]))
    for step in cross_out[:-2]:
        step()
    for ch in range(2):
        r.memory_grad[ch * half : (ch + 1) * half, :] = rs_wait(R_MEMORY, ch)
    small_wait(1, 2)
    small_start(1, 0)
    cross.pop(0)()
    up.pop(0)()
    cross.pop(0)()
    for step in cross_out[-2:]:
        step()
    cross.pop(0)()
    small_wait(1, 0)
    small_start(1, 1)
    cross.pop(0)()
    for step in self_out[:-2]:
        step()
    cross.pop(0)()
    selves.pop(0)()
    for step in self_out[-2:]:
        step()
    for ch in range(2):
        rows = slice(ch * half, (ch + 1) * half)
        live_row = (seq * Tl + ch * half + lax.broadcasted_iota(jnp.int32, (half, 1), 0)) < token_live
        r.mixed[rows, :] = jnp.where(live_row, r.x2[rows, :] + rs_wait(R_MIXED, ch), 0.0).astype(BF16)
    selves.pop(0)()
    selves.pop(0)()
    small_wait(1, 1)
    picked = lax.dot_general(
        r.small[1],
        placed.astype(F32),
        (((1,), (1,)), ((), ())),
        precision=lax.Precision.HIGHEST,
        preferred_element_type=F32,
    )
    r.gains_grad[...] = picked[0:3]
    r.biases_grad[...] = picked[3:6]
    for g in MOVED:
        s_wait(g)
    for step in (*down, *up, *cross, *selves):
        step()

    for i in (R_CHAIN, R_MIXED, R_MEMORY):
        rs_sent(i)
    for i, piece, everyone in given[:2]:
        ag_sent(i, piece, everyone)
    ag_sent(G_DZ1, r.dz1.at[own], r.dz1)
    for u in range(len(UNITS)):
        w_sent(u)
        z_sent(u)
    for g in MOVED:
        m_sent(g)
        v_sent(g)


def layer_call(A, B, S, rows, weights, norms, counts):
    V = pltpu.VMEM
    Tl, D = rows[0].shape
    T = Tl * S
    Dl = weights[SELF].shape[2]
    Fl = weights[UP].shape[1]
    pages = A * B
    R = pages // S
    heads = Dl // HEAD_DIM
    shards = [x.shape for x in weights]
    full = []
    for g, s in enumerate(shards):
        if g in (SELF, CROSS):
            full.append((s[0], s[1] * pages, s[2]))
        elif g == UP:
            full.append((s[0] * pages, s[1]))
        else:
            full.append((s[0] * R, s[1] * S))
    hbm, vmem, smem = (pl.BlockSpec(memory_space=m) for m in (pl.ANY, V, pltpu.SMEM))
    shape = jax.ShapeDtypeStruct
    dma = pltpu.SemaphoreType.DMA
    small_slots = S + A + B - 3
    units = len(UNITS)
    row_ref, wide_ref = V((T, D), BF16), V((T, Dl), BF16)
    own_ref, hidden_ref = V((Tl, D), F32), V((T, Fl), BF16)
    operands = dict(
        tokens=rows[0],
        memory=rows[1],
        cotangent=rows[2],
        ins=list(weights),
        norm_gains=norms[0],
        norm_biases=norms[1],
        token_counts=counts[0],
        patch_counts=counts[1],
    )
    specs = dict(
        tokens=hbm, memory=hbm, cotangent=hbm, ins=[hbm] * 6, norm_gains=vmem, norm_biases=vmem, token_counts=smem, patch_counts=smem
    )
    results = dict(
        mixed=shape((Tl, D), BF16),
        input_grad=shape((Tl, D), F32),
        memory_grad=shape((Tl, D), F32),
        outs=[shape(s, F32) for s in shards],
        gains_grad=shape(norms[0].shape, F32),
        biases_grad=shape(norms[1].shape, F32),
    )
    scratch = dict(
        w=[V(s, BF16) for s in full],
        grad=[V(s, BF16) for s in full],
        rb=[V((B - 1, A, *shards[g][-2:]), BF16) for g, _ in UNITS],
        zz=[V((A + 1, *shards[g][-2:]), BF16) for g, _ in UNITS],
        fb=[V((B - 1, S, *shards[g]), BF16) for g in MOVED],
        vv=[V((2, S, *shards[g]), BF16) for g in MOVED],
        back=[V(shards[g], BF16) for g in MOVED],
        all_tokens=row_ref,
        all_memory=row_ref,
        dyr=row_ref,
        a1=row_ref,
        a2=row_ref,
        a3=row_ref,
        dz2=row_ref,
        q=wide_ref,
        k=wide_ref,
        v=wide_ref,
        o=wide_ref,
        qc=wide_ref,
        kc=wide_ref,
        vc=wide_ref,
        oc=wide_ref,
        do=wide_ref,
        dq=wide_ref,
        dk=wide_ref,
        dv=wide_ref,
        p=V((heads, T, T), BF16),
        pc=V((heads, T, T), BF16),
        g=hidden_ref,
        du=hidden_ref,
        slope=V((T, Fl), F32),
        x1=own_ref,
        x2=own_ref,
        dx1=own_ref,
        dx2=own_ref,
        dk_sum=V((T, LANES), F32),
        dv_sum=V((T, LANES), F32),
        chain_part=row_ref,
        got=[V((S - 1, Tl, D), BF16)] * 3,
        small=V((2, 8, D), F32),
        small_got=V((2, small_slots, 8, D), F32),
        norm_terms=V((8, D), F32),
        ag_send=dma((7, 2, S - 1)),
        ag_recv=dma((7, 2, S)),
        rs_send=dma((3, 2, S - 1)),
        rs_recv=dma((3, 2, S - 1)),
        sm_send=dma((2, small_slots)),
        sm_recv=dma((2, small_slots)),
        ld_sem=dma((3,)),
        w_send=dma((units, pages, 4)),
        w_recv=dma((units, pages)),
        w_local=dma((units,)),
        y_send=dma((units, B - 1, A)),
        y_recv=dma((units, B - 1, A)),
        z_send=dma((units, A)),
        z_recv=dma((units, A + 1)),
        m_gave=dma((3,)),
        m_got=dma((3, S)),
        m_send=dma((3, S, B + 1)),
        m_recv=dma((3, R, S)),
        f_send=dma((3, B - 1, S)),
        f_recv=dma((3, B - 1, S)),
        v_send=dma((3, S)),
        v_recv=dma((3, 2, S)),
        s_send=dma((3, S)),
        s_recv=dma((3,)),
    )
    parts = [jax.tree.flatten(part) for part in (operands, specs, results, scratch)]
    values, in_specs, out_shape, scratch_shapes = (leaves for leaves, _ in parts)
    ends = [len(values), len(values) + len(out_shape)]

    def kernel(*refs):
        held = (refs[: ends[0]], refs[ends[0] : ends[1]], refs[ends[1] :])
        r = types.SimpleNamespace()
        for (_, tree), some in zip((parts[0], parts[2], parts[3]), held):
            vars(r).update(jax.tree.unflatten(tree, some))
        layer_kernel(A, B, S, r)

    found = pl.pallas_call(
        kernel,
        out_shape=out_shape,
        in_specs=in_specs,
        out_specs=[vmem] * len(out_shape),
        scratch_shapes=scratch_shapes,
        compiler_params=pltpu.CompilerParams(
            collective_id=0, has_side_effects=True, vmem_limit_bytes=62 * 2**20
        ),
        name="layer",
    )(*values)
    return jax.tree.unflatten(parts[2][1], found)


def keep_kernel(*refs):
    *arrays, sems = refs
    count = len(arrays) // 3
    given, kept, held = (arrays[n * count : (n + 1) * count] for n in range(3))
    loads = [pltpu.make_async_copy(given[n], held[n], sems.at[0, n]) for n in range(count)]
    stores = [pltpu.make_async_copy(held[n], kept[n], sems.at[1, n]) for n in range(count)]
    for load in loads:
        load.start()
    for load, store in zip(loads, stores):
        load.wait()
        store.start()
    for store in stores:
        store.wait()


def keep(*arrays):
    hbm = pl.BlockSpec(memory_space=pl.ANY)
    return pl.pallas_call(
        keep_kernel,
        out_shape=[jax.ShapeDtypeStruct(x.shape, x.dtype) for x in arrays],
        in_specs=[hbm] * len(arrays),
        out_specs=[hbm] * len(arrays),
        scratch_shapes=[pltpu.VMEM(x.shape, x.dtype) for x in arrays]
        + [pltpu.SemaphoreType.DMA((2, len(arrays)))],
        name="keep",
    )(*arrays)


def per_device(
    tokens,
    memory,
    cotangent,
    self_qkv,
    self_out,
    cross_qkv,
    cross_out,
    up_weight,
    down_weight,
    norm_gains,
    norm_biases,
    token_counts,
    patch_counts,
):
    pages = lax.axis_size("page")
    parts = lax.axis_size("seq")
    wide = 2 if pages == 8 else 8
    found = layer_call(
        pages // wide,
        wide,
        parts,
        (tokens[0], memory[0], cotangent[0]),
        (self_qkv, self_out, cross_qkv, cross_out, up_weight, down_weight),
        (norm_gains, norm_biases),
        (token_counts, patch_counts),
    )
    return keep(
        found["mixed"][None],
        found["input_grad"][None],
        found["memory_grad"][None],
        *found["outs"],
        found["gains_grad"],
        found["biases_grad"],
    )


def solution(mesh):
    rows = P("page", "seq", None)
    stack = P(None, "page", "seq")
    flat = P("page", "seq")
    norm = P(None, ("page", "seq"))
    counts = P("page")
    return jax.shard_map(
        per_device,
        mesh=mesh,
        in_specs=(rows, rows, rows, stack, flat, stack, flat, flat, flat, norm, norm, counts, counts),
        out_specs=(rows, rows, rows, stack, flat, stack, flat, flat, flat, norm, norm),
        check_vma=False,
    )
```

time: 311 us -> 236 us (0.76)
  Pallas kernels: 297 us -> 233 us
  local copies, waits for them, and re-layouts: 11.9 us -> 0 us
    pallas_call x1, Pallas kernels: 297 us -> 230 us  [layer_call(): pl.pallas_call(kernel, out_shape=out_shape, in_specs=in_specs, out_specs=...]
    unnamed x31 -> x0, local copies, waits for them, and re-layouts: 10.1 us -> none
where the time goes in v4:
time: 236 us
  Pallas kernels  233 us (99%)
    pallas_call x1, Pallas kernels, layer_call(): pl.pallas_call(kernel, out_shape=out_shape, in_specs=in_specs, out_specs=...  230 us

profile of v4, /device:TPU:0, one launch (start us, length us, event | category | flops | bytes accessed | tf_op | source)
XLA Modules:
  0.0 235.5 jit_solution(15508835276004061927)
XLA Ops:
  1.9 230.4 %layer.1 = (f32[3,32]{1,0:T(4,128)}, f32[3,32]{1,0:T(4,128)}, f32[128,1024]{1,0:T(8,128)}, f32[128,1024]{1,0:T(8,128)}, bf16[128,1024]{1,0:T(8,128)(2,1)}, /*ind...) custom-call(bf16[128,1024]{1,0:T(8,128)(2,1)} %bitcast.8, ...), custom_call_target="tpu_custom_call" | custom-call | tf_op jit(solution)/shard_map/layer/pallas_call | solution.py:1039
  232.3 3.0 %keep.1 = (bf16[1,128,1024]{2,1,0:T(8,128)(2,1)}, f32[1,128,1024]{2,1,0:T(8,128)}, f32[1,128,1024]{2,1,0:T(8,128)}, f32[3,128,256]{2,1,0:T(8,128)}, f32[128,256]...) custom-call(bf16[1,128,1024]{2,1,0:T(8,128)(2,1)} %bitcast.11, ...), custom_call_target="tpu_custom_call" | custom-call | tf_op jit(solution)/shard_map/keep/pallas_call | solution.py:1070

commit v5 on v4

--- a/solution.py
+++ b/solution.py
@@ -13,8 +13,9 @@
 MESH = pl.DeviceIdType.MESH
 SELF, SELF_OUT, CROSS, CROSS_OUT, UP, DOWN = range(6)
 MOVED = (SELF_OUT, CROSS_OUT, DOWN)
-UNITS = ((SELF, 0), (SELF, 1), (SELF, 2), (CROSS, 0), (CROSS, 1), (CROSS, 2), (UP, None))
-SELF_UNITS, CROSS_UNITS, UP_UNIT = (0, 1, 2), (3, 4, 5), 6
+QUARTERS = 4
+UNITS = tuple((g, n) for g, count in ((SELF, 3), (CROSS, 3), (UP, QUARTERS)) for n in range(count))
+SELF_UNITS, CROSS_UNITS, UP_UNITS = (0, 1, 2), (3, 4, 5), (6, 7, 8, 9)
 G_TOKENS, G_MEMORY, G_COT, G_A2, G_A3, G_DZ2, G_DZ1 = range(7)
 R_CHAIN, R_MIXED, R_MEMORY = range(3)
 LANES = 128
@@ -59,6 +60,7 @@
     T = Tl * S
     Dl = ins[SELF].shape[2]
     Fl = ins[UP].shape[1]
+    Fq = Fl // QUARTERS
     own = rows_at(seq * Tl, Tl)
     shelf, collector = lax.rem(page, R), lax.div(page, R)
     collects = seq == collector
@@ -222,11 +224,15 @@
         g, n = UNITS[u]
         size = ins[g].shape[-2]
         at = rows_at(j * size, size)
-        return arrays[g].at[at, :] if n is None else arrays[g].at[n, at, :]
+        return arrays[g].at[at, n * Fq : (n + 1) * Fq] if g == UP else arrays[g].at[n, at, :]
 
     def whole_of(arrays, u):
         g, n = UNITS[u]
-        return arrays[g] if n is None else arrays[g].at[n]
+        return arrays[g].at[:, n * Fq : (n + 1) * Fq] if g == UP else arrays[g].at[n]
+
+    turned = UP_UNITS[2:] if B == 2 else ()
+    turned_back = UP_UNITS[3:] if B == 2 else ()
+    beside = a * B + 1 - b
 
     def w_copy(u, j, way, src=None):
         place = rows_of(w, u, j)
@@ -244,29 +250,31 @@
     def w_local(u):
         return pltpu.make_async_copy(whole_of(ins, u), rows_of(w, u, page), r.w_local.at[u])
 
-    def w_first(*units):
+    def w_first(*units, along=(0, 1, 2, 3)):
         for u in units:
-            w_forward(u, page, (0, 1, 2, 3), whole_of(ins, u))
-            w_local(u).start()
+            w_forward(u, page, along, whole_of(ins, u))
+            if 2 in along:
+                w_local(u).start()
+
+    def w_turn(*units):
+        for u in units:
+            landed(rows_of(w, u, beside), r.w_recv.at[u, beside])
+            w_forward(u, beside, (0, 1))
 
     def w_step(d, *units):
         for u in units:
-            @pl.when(a - d >= 0)
-            def _():
-                j = page - d * B
-                landed(rows_of(w, u, j), r.w_recv.at[u, j])
-                w_forward(u, j, (1, 2, 3))
-
-            @pl.when(a + d < A)
-            def _():
-                j = page + d * B
-                landed(rows_of(w, u, j), r.w_recv.at[u, j])
-                w_forward(u, j, (0, 2, 3))
+            for sign, way in ((-1, 1), (1, 0)):
+                @pl.when((a + sign * d >= 0) & (a + sign * d < A))
+                def _():
+                    for column in (page, beside) if u in turned else (page,):
+                        j = column + sign * d * B
+                        landed(rows_of(w, u, j), r.w_recv.at[u, j])
+                        w_forward(u, j, (way,) if u in turned else (way, 2, 3))
 
     def w_wait(*units):
         for u in units:
             w_local(u).wait()
-            for e in range(1, B):
+            for e in range(1, 1 if u in turned else B):
                 for t in range(A):
                     @pl.when(b - e >= 0)
                     def _():
@@ -284,9 +292,10 @@
         for t in range(A):
             for e in range(B):
                 j = t * B + e
-                for way, when in enumerate(
-                    ((b == e) & (t >= a), (b == e) & (t <= a), e >= b, e <= b)
-                ):
+                along = ((b == e) & (t >= a), (b == e) & (t <= a), e >= b, e <= b)
+                if u in turned:
+                    along = (t >= a, t <= a, (b == e) & (t == a), (b == e) & (t == a))
+                for way, when in enumerate(along):
                     @pl.when(when & ways[way])
                     def _():
                         w_copy(u, j, way).wait_send()
@@ -340,8 +349,11 @@
 
             m_forward(g, n)
 
-    def m_pass(g, n):
-        @pl.when(holds & (a != a0))
+    inside = (a > 0) & (a < A - 1)
+    hops = jnp.abs(a - a0)
+
+    def m_pass(g, n, hop):
+        @pl.when(holds & (hops == hop))
         def _():
             landed(block(w[g], g, mine, n), r.m_recv.at[MOVED.index(g), mine, n])
             m_forward(g, n)
@@ -384,8 +396,8 @@
         )
 
     def y_start(*units):
-        for u in units:
-            for m in range(A):
+        for m in range(A):
+            for u in units:
                 for k in range(1, B):
                     y_copy(u, k, order(m)).start()
 
@@ -440,13 +452,72 @@
         total = r.rb[u][0, a].astype(F32)
         total = total + jnp.where(a > 0, r.zz[u][a].astype(F32), 0.0)
         total = total + jnp.where(a < A - 1, r.zz[u][A].astype(F32), 0.0)
-        g, n = UNITS[u]
-        if n is None:
-            outs[g][...] = total
-        else:
-            outs[g][n] = total
+        whole_of(outs, u)[...] = total
+
+    def c_copy(u, t, sign, side, src):
+        slot = jnp.where((t == a + sign) & (sign < 0), A, t)
+        return remote(
+            src,
+            r.tz.at[side, slot],
+            r.tz_send.at[side, t],
+            r.tz_recv.at[side, slot],
+            (page + sign * B, seq),
+        )
+
+    def c_own(u, t, side):
+        return rows_of(grad, u, t * B + (b, 1 - b)[side])
+
+    def c_first(u):
+        for m in range(A - 1):
+            t = order(m)
+            sign, has = z_way(t)
+            for side in range(2):
+                @pl.when(jnp.logical_not(has))
+                def _():
+                    c_copy(u, t, sign, side, c_own(u, t, side)).start()
+
+    def c_sum(m, u):
+        t = order(m)
+        sign, has = z_way(t)
+
+        @pl.when(has)
+        def _():
+            for side in range(2):
+                landed(r.tz.at[side, t], r.tz_recv.at[side, t])
+                total = c_own(u, t, side)[...].astype(F32) + r.tz[side, t].astype(F32)
+                r.ta[side, t] = total.astype(BF16)
+                c_copy(u, t, sign, side, r.ta.at[side, t]).start()
+
+    def c_turn(u):
+        return remote(r.ta.at[1, a], r.tb, r.y_send.at[u, 0, 0], r.y_recv.at[u, 0, 0], (beside, seq))
+
+    def c_total(u):
+        for side in (1, 0):
+            total = c_own(u, a, side)[...].astype(F32)
+            for has, slot in ((a > 0, a), (a < A - 1, A)):
+                @pl.when(has)
+                def _():
+                    landed(r.tz.at[side, slot], r.tz_recv.at[side, slot])
+
+                total = total + jnp.where(has, r.tz[side, slot].astype(F32), 0.0)
+            if side:
+                r.ta[1, a] = total.astype(BF16)
+                c_turn(u).start()
+            else:
+                whole_of(outs, u)[...] = total
+
+    def c_end(u):
+        landed(r.tb, r.y_recv.at[u, 0, 0])
+        whole_of(outs, u)[...] = whole_of(outs, u)[...] + r.tb[...].astype(F32)
 
     def z_sent(u):
+        if u in turned_back:
+            c_turn(u).wait_send()
+            for m in range(A - 1):
+                t = order(m)
+                for side in range(2):
+                    c_copy(u, t, z_way(t)[0], side, c_own(u, t, side)).wait_send()
+            return
         for t in range(A):
             for k in range(1, B):
                 y_copy(u, k, t).wait_send()
@@ -454,14 +525,6 @@
             @pl.when(t != a)
             def _():
                 z_copy(u, t, jnp.where(t > a, 1, -1)).wait_send()
-
-    def unit_steps(*units):
-        steps = [lambda: [y_sum(0, u) for u in units]]
-        for m in range(1, A - 1):
-            steps.append(lambda m=m: [(y_sum(m, u), z_sum(m - 1, u)) for u in units])
-        steps.append(lambda: [(z_sum(A - 2, u), y_sum(A - 1, u)) for u in units])
-        steps.append(lambda: [z_total(u) for u in units])
-        return steps
 
     def f_copy(g, k, n):
         i = MOVED.index(g)
@@ -486,8 +549,8 @@
                     f_copy(g, k, n).start()
 
     inward = jnp.where(a > a0, -1, 1)
-    from_out = holds & (a != a0) & (a > 0) & (a < A - 1)
-    starts_line = holds & (a != a0) & ((a == 0) | (a == A - 1))
+    from_out = holds & (a != a0) & inside
+    starts_line = holds & (a != a0) & jnp.logical_not(inside)
 
     def v_copy(g, n):
         i = MOVED.index(g)
@@ -515,10 +578,12 @@
             def _():
                 v_copy(g, n).start()
 
-    def v_sum(g, n):
+    passed = jnp.where(a > a0, A - 1 - a, a)
+
+    def v_sum(g, n, hop):
         i = MOVED.index(g)
 
-        @pl.when(from_out)
+        @pl.when(from_out & (passed == hop))
         def _():
             landed(r.vv[i].at[0, n], r.v_recv.at[i, 0, n])
             r.fb[i][0, n] = (r.fb[i][0, n].astype(F32) + r.vv[i][0, n].astype(F32)).astype(BF16)
@@ -572,14 +637,6 @@
             @pl.when(collects & (seq != n))
             def _():
                 s_copy(g, n).wait_send()
-
-    def moved_steps(g):
-        steps = [lambda: f_sum(g, 0)]
-        for n in range(1, S):
-            steps.append(lambda n=n: (f_sum(g, n), v_sum(g, n - 1)))
-        steps.append(lambda: (v_sum(g, S - 1), v_total(g, 0)))
-        steps.append(lambda: [v_total(g, n) for n in range(1, S)])
-        return steps
 
     token_live = r.token_counts[0]
     patch_live = r.patch_counts[0]
@@ -666,236 +723,331 @@
     few = r.norm_gains.shape[1]
     at_feature = lax.broadcasted_iota(jnp.int32, (few, D), 1)
     placed = at_feature == lax.broadcasted_iota(jnp.int32, (few, D), 0) + (page * S + seq) * few
-    r.small[0] = jnp.zeros((8, D), F32)
-    r.small[0, 0:3, :] = nn(r.norm_gains[...], placed.astype(F32).astype(BF16))
-    r.small[0, 3:6, :] = nn(r.norm_biases[...], placed.astype(F32).astype(BF16))
-    small_start(0, 0)
-    w_first(*SELF_UNITS)
-    m_collect(SELF_OUT)
+    plan = []
+
+    def when(time, *steps):
+        plan.extend((time, step) for step in steps)
+
+    def each_row_part(step):
+        def run():
+            for ch in range(2):
+                step(ch, slice(ch * half, (ch + 1) * half))
+
+        return run
+
+    def w_moved(g, first, hop_time, gap):
+        for n in range(S):
+            when(first + n * gap, lambda n=n: m_first(g, n))
+            for hop in range(1, A):
+                when(first + n * gap + hop * hop_time, lambda n=n, hop=hop: m_pass(g, n, hop))
+
+    def g_moved(g, first, hop_time, gap, late):
+        for n in range(S):
+            time = first + n * gap
+            when(time, lambda n=n: f_sum(g, n))
+            for hop in range(1, A - 1):
+                when(time + late + hop * hop_time, lambda n=n, hop=hop: v_sum(g, n, hop))
+            when(time + late + (A - 1) * hop_time, lambda n=n: v_total(g, n))
+
+    def g_units(units, first, hop_time, gap, late):
+        for place, u in enumerate(units):
+            time = first + gap * place / len(units)
+            for m in range(A):
+                when(time + gap * m, lambda m=m, u=u: y_sum(m, u))
+            for m in range(A - 2):
+                when(time + gap * m + late + hop_time, lambda m=m, u=u: z_sum(m, u))
+            after = time + late + 2 * hop_time
+            when(max(after, time + gap * (A - 2)), lambda u=u: z_sum(A - 2, u))
+            when(max(after + gap, time + gap * (A - 1)), lambda u=u: z_total(u))
+
     given = (
         (G_TOKENS, r.tokens, r.all_tokens), (G_MEMORY, r.memory, r.all_memory), (G_COT, r.cotangent, r.dyr)
     )
     loads = [pltpu.make_async_copy(piece, everyone.at[own], r.ld_sem.at[i]) for i, piece, everyone in given]
-    ag_begin(*given[0])
-    for load in loads:
-        load.start()
-    w_step(1, *SELF_UNITS)
-    small_wait(0, 0)
-    small_start(0, 1)
-    m_collect(CROSS_OUT)
-    ag_begin(*given[1])
-    m_collect(DOWN)
-    w_step(2, *SELF_UNITS)
-    for n in range(S):
-        m_first(SELF_OUT, n)
-    small_wait(0, 1)
-    small_start(0, 2)
-    ag_forward(G_TOKENS, r.all_tokens)
-    w_first(*CROSS_UNITS)
-    ag_begin(*given[2])
-    w_step(3, *SELF_UNITS)
-    for n in range(S):
-        m_pass(SELF_OUT, n)
-    w_step(1, *CROSS_UNITS)
-    small_wait(0, 2)
-    ag_wait(G_TOKENS, r.all_tokens)
-    for load in loads:
-        load.wait()
-
-    @pl.loop(0, S)
-    def _(n):
-        at = rows_at(n * Tl, Tl)
-        values = r.all_tokens[at, :].astype(F32)
-        r.a1[at, :] = (normed(values)[0] * gains(0) + biases(0)).astype(BF16)
-
-    w_wait(*SELF_UNITS)
-    project(((r.q, 0), (r.k, 1), (r.v, 2)), r.a1, w[SELF])
-    w_step(2, *CROSS_UNITS)
-    w_first(UP_UNIT)
-    ag_forward(G_MEMORY, r.all_memory)
-    attend(r.q, r.k, r.v, r.o, r.p, token_live, True)
-    w_step(3, *CROSS_UNITS)
-    m_wait(SELF_OUT)
-    rs_start(R_CHAIN, lambda at: nn(r.o[at, :], w[SELF_OUT][...]))
-    for n in range(S):
-        m_first(CROSS_OUT, n)
-    w_step(1, UP_UNIT)
-    m_first(DOWN, 0)
-    ag_forward(G_COT, r.dyr)
-    for ch in range(2):
-        rows = slice(ch * half, (ch + 1) * half)
+
+    def begin():
+        r.small[0] = jnp.zeros((8, D), F32)
+        r.small[0, 0:3, :] = nn(r.norm_gains[...], placed.astype(F32).astype(BF16))
+        r.small[0, 3:6, :] = nn(r.norm_biases[...], placed.astype(F32).astype(BF16))
+        small_start(0, 0)
+        w_first(*SELF_UNITS)
+        m_collect(SELF_OUT)
+        ag_begin(*given[0])
+        for load in loads:
+            load.start()
+
+    def small_next(i, level):
+        small_wait(i, level)
+        small_start(i, level + 1 if i == 0 else level - 1)
+
+    def take_tokens():
+        small_wait(0, 2)
+        ag_wait(G_TOKENS, r.all_tokens)
+        for load in loads:
+            load.wait()
+
+        @pl.loop(0, S)
+        def _(n):
+            at = rows_at(n * Tl, Tl)
+            values = r.all_tokens[at, :].astype(F32)
+            r.a1[at, :] = (normed(values)[0] * gains(0) + biases(0)).astype(BF16)
+
+    def self_project():
+        w_wait(*SELF_UNITS)
+        project(((r.q, 0), (r.k, 1), (r.v, 2)), r.a1, w[SELF])
+
+    def self_sum():
+        m_wait(SELF_OUT)
+        rs_start(R_CHAIN, lambda at: nn(r.o[at, :], w[SELF_OUT][...]))
+
+    @each_row_part
+    def self_add(ch, rows):
         r.x1[rows, :] = r.all_tokens[part_of(seq, ch), :].astype(F32) + rs_wait(R_CHAIN, ch)
         norm_own(1, r.x1[rows, :], r.a2, ch)
         ag_start(G_A2, r.a2.at[own], r.a2, ch)
-    rs_sent(R_CHAIN)
-    for n in range(S):
-        m_pass(CROSS_OUT, n)
-    w_wait(*CROSS_UNITS)
-    ag_wait(G_MEMORY, r.all_memory)
-    project(((r.kc, 1), (r.vc, 2)), r.all_memory, w[CROSS])
-    ag_forward(G_A2, r.a2)
-    ag_wait(G_A2, r.a2)
-    w_step(2, UP_UNIT)
-    m_first(DOWN, 1)
-    m_pass(DOWN, 0)
-    project(((r.qc, 0),), r.a2, w[CROSS])
-    attend(r.qc, r.kc, r.vc, r.oc, r.pc, patch_live, False)
-    m_wait(CROSS_OUT)
-    rs_start(R_CHAIN, lambda at: nn(r.oc[at, :], w[CROSS_OUT][...]))
-    w_step(3, UP_UNIT)
-    m_first(DOWN, 2)
-    m_pass(DOWN, 1)
-    m_first(DOWN, 3)
-    ag_wait(G_COT, r.dyr)
-    ag_sent(*given[2])
-
-    @pl.loop(0, S)
-    def _(n):
-        at = rows_at(n * Tl, Tl)
-        row = n * Tl + lax.broadcasted_iota(jnp.int32, (Tl, 1), 0)
-        values = r.dyr[at, :].astype(F32)
-        r.dyr[at, :] = jnp.where(row < token_live, values, 0.0).astype(BF16)
-
-    for ch in range(2):
-        rows = slice(ch * half, (ch + 1) * half)
+
+    def memory_project():
+        w_wait(*CROSS_UNITS)
+        ag_wait(G_MEMORY, r.all_memory)
+        project(((r.kc, 1), (r.vc, 2)), r.all_memory, w[CROSS])
+
+    def cross_project():
+        ag_wait(G_A2, r.a2)
+        project(((r.qc, 0),), r.a2, w[CROSS])
+
+    def cross_sum():
+        m_wait(CROSS_OUT)
+        rs_sent(R_CHAIN)
+        rs_start(R_CHAIN, lambda at: nn(r.oc[at, :], w[CROSS_OUT][...]))
+
+    def take_cotangent():
+        ag_wait(G_COT, r.dyr)
+        ag_sent(*given[2])
+
+        @pl.loop(0, S)
+        def _(n):
+            at = rows_at(n * Tl, Tl)
+            row = n * Tl + lax.broadcasted_iota(jnp.int32, (Tl, 1), 0)
+            values = r.dyr[at, :].astype(F32)
+            r.dyr[at, :] = jnp.where(row < token_live, values, 0.0).astype(BF16)
+
+    @each_row_part
+    def cross_add(ch, rows):
         r.x2[rows, :] = r.x1[rows, :] + rs_wait(R_CHAIN, ch)
         norm_own(2, r.x2[rows, :], r.a3, ch)
         ag_start(G_A3, r.a3.at[own], r.a3, ch)
-    rs_sent(R_CHAIN)
-    m_pass(DOWN, 2)
-    ag_forward(G_A3, r.a3)
-    ag_wait(G_A3, r.a3)
-    for n in range(3, S):
-        m_pass(DOWN, n)
-    w_wait(UP_UNIT)
-
-    @pl.loop(0, tiles)
-    def _(n):
-        cols = rows_at(n * tile, tile)
-        out, slope = gelu_pair(nn(r.a3[...], w[UP][:, cols]))
-        r.g[:, cols] = out.astype(BF16)
-        r.slope[:, cols] = slope
-
-    @pl.loop(0, tiles)
-    def _(n):
-        cols = rows_at(n * tile, tile)
-        grad[DOWN][cols, :] = tn(r.g[:, cols], r.dyr[...]).astype(BF16)
-
-    f_start(DOWN)
-    m_wait(DOWN)
-
-    @pl.loop(0, tiles)
-    def _(n):
-        cols = rows_at(n * tile, tile)
-        r.du[:, cols] = (nt(r.dyr[...], w[DOWN][cols, :]) * r.slope[:, cols]).astype(BF16)
-
-    ag_sent(G_A3, r.a3.at[own], r.a3)
-    rs_start(R_CHAIN, lambda at: nt(r.du[at, :], w[UP][...]))
-
-    @pl.loop(0, D // 256)
-    def _(n):
-        cols = rows_at(n * 256, 256)
-        grad[UP][cols, :] = tn(r.a3[:, cols], r.du[...]).astype(BF16)
-
-    y_start(UP_UNIT)
-    down, up = moved_steps(DOWN), unit_steps(UP_UNIT)
-    down.pop(0)()
-    for ch in range(2):
-        rows = slice(ch * half, (ch + 1) * half)
+
+    def hidden():
+        w_wait(*UP_UNITS)
+        ag_wait(G_A3, r.a3)
+
+        @pl.loop(0, tiles)
+        def _(n):
+            cols = rows_at(far_first(n) * tile, tile)
+            out, slope = gelu_pair(nn(r.a3[...], w[UP][:, cols]))
+            r.g[:, cols] = out.astype(BF16)
+            r.slope[:, cols] = slope
+            grad[DOWN][cols, :] = tn(r.g[:, cols], r.dyr[...]).astype(BF16)
+
+            @pl.when(n == tiles * (R - 1) // R - 1)
+            def _():
+                f_start(DOWN)
+
+    def far_first(n):
+        shelf_last = jnp.where(holds, mine + 1, 0) * (tiles // R)
+        return lax.rem(n + shelf_last, tiles)
+
+    straight = tuple(u for u in UP_UNITS if u not in turned)
+    when(0, begin)
+    when(6, lambda: w_step(1, *SELF_UNITS))
+    when(8, lambda: small_next(0, 0), lambda: m_collect(CROSS_OUT), lambda: ag_begin(*given[1]), lambda: m_collect(DOWN))
+    when(12, lambda: w_step(2, *SELF_UNITS))
+    w_moved(SELF_OUT, 13, 4, 0.1)
+    when(15, lambda: small_next(0, 1), lambda: ag_forward(G_TOKENS, r.all_tokens), lambda: ag_begin(*given[2]))
+    when(16.5, lambda: w_step(3, *SELF_UNITS))
+    when(17.5, lambda: w_first(*CROSS_UNITS))
+    when(21, lambda: w_first(*turned, along=(2, 3)))
+    when(22, lambda: w_first(*straight))
+    when(23.5, lambda: w_step(1, *CROSS_UNITS))
+    when(24.5, take_tokens)
+    when(27, self_project)
+    when(29, lambda: w_step(2, *CROSS_UNITS))
+    w_moved(CROSS_OUT, 30, 5, 0.1)
+    when(31, lambda: ag_forward(G_MEMORY, r.all_memory))
+    when(32, lambda: attend(r.q, r.k, r.v, r.o, r.p, token_live, True))
+    when(34.5, lambda: w_step(3, *CROSS_UNITS))
+    when(36, self_sum)
+    when(37, lambda: w_step(1, *straight))
+    w_moved(DOWN, 37.5, 7.5, 4.5)
+    when(42, lambda: ag_forward(G_COT, r.dyr))
+    when(43, lambda: w_step(2, *straight))
+    when(46, self_add)
+    when(47, lambda: w_first(*turned, along=(0, 1)))
+    when(48, memory_project)
+    when(49, lambda: w_step(3, *straight))
+    when(50, lambda: w_turn(*turned))
+    when(52, lambda: ag_forward(G_A2, r.a2))
+    when(53.2, cross_project)
+    when(54, lambda: attend(r.qc, r.kc, r.vc, r.oc, r.pc, patch_live, False))
+    when(57, cross_sum)
+    when(58, lambda: w_step(1, *turned))
+    when(61, take_cotangent)
+    when(67, cross_add)
+    when(66, lambda: w_step(2, *turned))
+    when(73, lambda: w_step(3, *turned))
+    when(75, lambda: ag_forward(G_A3, r.a3))
+    when(78, hidden)
+
+    def hidden_back():
+        m_wait(DOWN)
+
+        @pl.loop(0, tiles)
+        def _(n):
+            cols = rows_at(n * tile, tile)
+            r.du[:, cols] = (nt(r.dyr[...], w[DOWN][cols, :]) * r.slope[:, cols]).astype(BF16)
+
+        straight_columns = (QUARTERS - len(turned_back)) * Fq
+        for part in (slice(straight_columns, Fl), slice(0, straight_columns)):
+            if part.start == part.stop:
+                continue
+
+            @pl.loop(0, D // 256)
+            def _(n):
+                cols = rows_at(n * 256, 256)
+                grad[UP][cols, part] = tn(r.a3[:, cols], r.du[:, part]).astype(BF16)
+
+            if part.start:
+                for u in turned_back:
+                    c_first(u)
+        y_start(*UP_UNITS[: QUARTERS - len(turned_back)])
+
+    def hidden_sum():
+        ag_sent(G_A3, r.a3.at[own], r.a3)
+        rs_sent(R_CHAIN)
+        rs_start(R_CHAIN, lambda at: nt(r.du[at, :], w[UP][...]))
+
+    @each_row_part
+    def hidden_add(ch, rows):
         back_term = norm_back(2, r.x2[rows, :], rs_wait(R_CHAIN, ch), ch)
         r.dx2[rows, :] = r.dyr[part_of(seq, ch), :].astype(F32) + back_term
         r.dz2[part_of(seq, ch), :] = r.dx2[rows, :].astype(BF16)
         ag_start(G_DZ2, r.dz2.at[own], r.dz2, ch)
-    rs_sent(R_CHAIN)
-    down.pop(0)()
-    ag_forward(G_DZ2, r.dz2)
-    ag_wait(G_DZ2, r.dz2)
-    r.do[...] = nt(r.dz2[...], w[CROSS_OUT][...]).astype(BF16)
-    attend_back(r.qc, r.kc, r.vc, r.do, r.pc, r.dq, r.dk, r.dv, False)
-    rs_start(R_CHAIN, lambda at: nt(r.dq[at, :], w[CROSS][0]))
-    grad[CROSS_OUT][...] = tn(r.oc[...], r.dz2[...]).astype(BF16)
-    f_start(CROSS_OUT)
-    for n, (left, right) in enumerate(((r.a2, r.dq), (r.all_memory, r.dk), (r.all_memory, r.dv))):
-        grad[CROSS][n] = tn(left[...], right[...]).astype(BF16)
-    y_start(*CROSS_UNITS)
-    down.pop(0)()
-    down.pop(0)()
-    for ch in range(2):
-        rows = slice(ch * half, (ch + 1) * half)
+
+    def cross_back():
+        ag_wait(G_DZ2, r.dz2)
+        grad[CROSS_OUT][...] = tn(r.oc[...], r.dz2[...]).astype(BF16)
+        f_start(CROSS_OUT)
+        r.do[...] = nt(r.dz2[...], w[CROSS_OUT][...]).astype(BF16)
+        attend_back(r.qc, r.kc, r.vc, r.do, r.pc, r.dq, r.dkc, r.dvc, False)
+
+    def cross_back_sum():
+        rs_sent(R_CHAIN)
+        rs_start(R_CHAIN, lambda at: nt(r.dq[at, :], w[CROSS][0]))
+
+    def cross_grad():
+        for n, (left, right) in enumerate(((r.a2, r.dq), (r.all_memory, r.dkc), (r.all_memory, r.dvc))):
+            grad[CROSS][n] = tn(left[...], right[...]).astype(BF16)
+        y_start(*CROSS_UNITS)
+
+    @each_row_part
+    def cross_back_add(ch, rows):
         r.dx1[rows, :] = r.dx2[rows, :] + norm_back(1, r.x1[rows, :], rs_wait(R_CHAIN, ch), ch)
         r.dz1[part_of(seq, ch), :] = r.dx1[rows, :].astype(BF16)
         ag_start(G_DZ1, r.dz1.at[own], r.dz1, ch)
-    rs_sent(R_CHAIN)
-    up.pop(0)()
-    down.pop(0)()
-    ag_forward(G_DZ1, r.dz1)
-    ag_wait(G_DZ1, r.dz1)
-    r.do[...] = nt(r.dz1[...], w[SELF_OUT][...]).astype(BF16)
-    grad[SELF_OUT][...] = tn(r.o[...], r.dz1[...]).astype(BF16)
-    f_start(SELF_OUT)
-    ag_sent(G_A2, r.a2.at[own], r.a2)
-    rs_start(R_MEMORY, lambda at: nt(r.dk[at, :], w[CROSS][1]) + nt(r.dv[at, :], w[CROSS][2]))
-    attend_back(r.q, r.k, r.v, r.do, r.p, r.dq, r.dk, r.dv, True)
-    for n, right in enumerate((r.dq, r.dk, r.dv)):
-        grad[SELF][n] = tn(r.a1[...], right[...]).astype(BF16)
-    y_start(*SELF_UNITS)
-    up.pop(0)()
-    rs_start(
-        R_CHAIN, lambda at: nt(r.dq[at, :], w[SELF][0]) + nt(r.dk[at, :], w[SELF][1]) + nt(r.dv[at, :], w[SELF][2])
-    )
-    down.pop(0)()
-    up.pop(0)()
-    cross_out, cross = moved_steps(CROSS_OUT), unit_steps(*CROSS_UNITS)
-    self_out, selves = moved_steps(SELF_OUT), unit_steps(*SELF_UNITS)
-    up.pop(0)()
-    for ch in range(2):
-        rows = slice(ch * half, (ch + 1) * half)
+
+    def self_back():
+        ag_wait(G_DZ1, r.dz1)
+        grad[SELF_OUT][...] = tn(r.o[...], r.dz1[...]).astype(BF16)
+        f_start(SELF_OUT)
+        r.do[...] = nt(r.dz1[...], w[SELF_OUT][...]).astype(BF16)
+        attend_back(r.q, r.k, r.v, r.do, r.p, r.dq, r.dk, r.dv, True)
+        for n, right in enumerate((r.dq, r.dk, r.dv)):
+            grad[SELF][n] = tn(r.a1[...], right[...]).astype(BF16)
+        y_start(*SELF_UNITS)
+
+    def self_back_sum():
+        rs_sent(R_CHAIN)
+        rs_start(
+            R_CHAIN,
+            lambda at: nt(r.dq[at, :], w[SELF][0]) + nt(r.dk[at, :], w[SELF][1]) + nt(r.dv[at, :], w[SELF][2]),
+        )
+
+    def memory_sum():
+        ag_sent(G_A2, r.a2.at[own], r.a2)
+        rs_start(R_MEMORY, lambda at: nt(r.dkc[at, :], w[CROSS][1]) + nt(r.dvc[at, :], w[CROSS][2]))
+
+    @each_row_part
+    def input_add(ch, rows):
         back_term = norm_back(0, r.all_tokens[part_of(seq, ch), :].astype(F32), rs_wait(R_CHAIN, ch), ch)
         r.input_grad[rows, :] = r.dx1[rows, :] + back_term
-    r.small[1] = r.norm_terms[...]
-    small_start(1, 2)
-    ag_sent(G_DZ2, r.dz2.at[own], r.dz2)
-    rs_start(R_MIXED, lambda at: nn(r.g[at, :], w[DOWN][...]))
-    for step in cross_out[:-2]:
-        step()
-    for ch in range(2):
-        r.memory_grad[ch * half : (ch + 1) * half, :] = rs_wait(R_MEMORY, ch)
-    small_wait(1, 2)
-    small_start(1, 0)
-    cross.pop(0)()
-    up.pop(0)()
-    cross.pop(0)()
-    for step in cross_out[-2:]:
-        step()
-    cross.pop(0)()
-    small_wait(1, 0)
-    small_start(1, 1)
-    cross.pop(0)()
-    for step in self_out[:-2]:
-        step()
-    cross.pop(0)()
-    selves.pop(0)()
-    for step in self_out[-2:]:
-        step()
-    for ch in range(2):
-        rows = slice(ch * half, (ch + 1) * half)
+
+    def small_last():
+        r.small[1] = r.norm_terms[...]
+        small_start(1, 2)
+
+    def mixed_sum():
+        ag_sent(G_DZ2, r.dz2.at[own], r.dz2)
+        rs_start(R_MIXED, lambda at: nn(r.g[at, :], w[DOWN][...]))
+
+    @each_row_part
+    def memory_add(ch, rows):
+        r.memory_grad[rows, :] = rs_wait(R_MEMORY, ch)
+
+    @each_row_part
+    def mixed_add(ch, rows):
         live_row = (seq * Tl + ch * half + lax.broadcasted_iota(jnp.int32, (half, 1), 0)) < token_live
         r.mixed[rows, :] = jnp.where(live_row, r.x2[rows, :] + rs_wait(R_MIXED, ch), 0.0).astype(BF16)
-    selves.pop(0)()
-    selves.pop(0)()
-    small_wait(1, 1)
-    picked = lax.dot_general(
-        r.small[1],
-        placed.astype(F32),
-        (((1,), (1,)), ((), ())),
-        precision=lax.Precision.HIGHEST,
-        preferred_element_type=F32,
-    )
-    r.gains_grad[...] = picked[0:3]
-    r.biases_grad[...] = picked[3:6]
-    for g in MOVED:
-        s_wait(g)
-    for step in (*down, *up, *cross, *selves):
+
+    def norms_out():
+        small_wait(1, 0)
+        picked = lax.dot_general(
+            r.small[1],
+            placed.astype(F32),
+            (((1,), (1,)), ((), ())),
+            precision=lax.Precision.HIGHEST,
+            preferred_element_type=F32,
+        )
+        r.gains_grad[...] = picked[0:3]
+        r.biases_grad[...] = picked[3:6]
+
+    when(87, hidden_back)
+    when(91, hidden_sum)
+    if turned_back:
+        when(99, lambda: c_sum(0, UP_UNITS[3]))
+        when(102, lambda: c_sum(1, UP_UNITS[3]))
+        when(104, lambda: c_sum(2, UP_UNITS[3]))
+        when(110, lambda: c_total(UP_UNITS[3]))
+        when(138, lambda: c_end(UP_UNITS[3]))
+        g_moved(DOWN, 97, 7.2, 5.6, 5)
+        g_units(UP_UNITS[:3], 120.5, 4.5, 4.2, 7)
+    else:
+        g_moved(DOWN, 97, 7.2, 5.6, 0)
+        g_units(UP_UNITS, 120.5, 4.5, 5.6, 0)
+    when(102, hidden_add)
+    when(106.5, lambda: ag_forward(G_DZ2, r.dz2))
+    when(108.5, cross_back)
+    when(114, cross_back_sum)
+    when(116, cross_grad)
+    when(124, cross_back_add)
+    when(130, lambda: ag_forward(G_DZ1, r.dz1))
+    when(132, self_back)
+    when(137, self_back_sum)
+    g_moved(CROSS_OUT, 134, 3.2, 1.4, 6)
+    when(142, memory_sum)
+    g_units(CROSS_UNITS, 141.5, 6, 4.2, 4)
+    when(146, input_add)
+    when(147, small_last)
+    when(150, mixed_sum)
+    when(152, lambda: small_next(1, 2))
+    when(154, memory_add)
+    g_moved(SELF_OUT, 157, 3.2, 1.4, 2)
+    when(162, lambda: small_next(1, 1))
+    when(166, mixed_add)
+    g_units(SELF_UNITS, 168, 6, 4.2, 0)
+    when(177, lambda: s_wait(DOWN), lambda: s_wait(CROSS_OUT))
+    when(181, lambda: s_wait(SELF_OUT), norms_out)
+
+    for _, step in sorted(plan, key=lambda entry: entry[0]):
         step()
 
     for i in (R_CHAIN, R_MIXED, R_MEMORY):
@@ -934,6 +1086,12 @@
     dma = pltpu.SemaphoreType.DMA
     small_slots = S + A + B - 3
     units = len(UNITS)
+    pieces = [(shards[g][0], Fl // QUARTERS) if g == UP else shards[g][1:] for g, _ in UNITS]
+    turn = pieces[-1]
+    if B == 2:
+        pieces[-1] = (16, LANES)
+    else:
+        turn = (16, LANES)
     row_ref, wide_ref = V((T, D), BF16), V((T, Dl), BF16)
     own_ref, hidden_ref = V((Tl, D), F32), V((T, Fl), BF16)
     operands = dict(
@@ -960,8 +1118,11 @@
     scratch = dict(
         w=[V(s, BF16) for s in full],
         grad=[V(s, BF16) for s in full],
-        rb=[V((B - 1, A, *shards[g][-2:]), BF16) for g, _ in UNITS],
-        zz=[V((A + 1, *shards[g][-2:]), BF16) for g, _ in UNITS],
+        rb=[V((B - 1, A, *piece), BF16) for piece in pieces],
+        zz=[V((A + 1, *piece), BF16) for piece in pieces],
+        ta=V((2, A, *turn), BF16),
+        tz=V((2, A + 1, *turn), BF16),
+        tb=V(turn, BF16),
         fb=[V((B - 1, S, *shards[g]), BF16) for g in MOVED],
         vv=[V((2, S, *shards[g]), BF16) for g in MOVED],
         back=[V(shards[g], BF16) for g in MOVED],
@@ -984,6 +1145,8 @@
         dq=wide_ref,
         dk=wide_ref,
         dv=wide_ref,
+        dkc=wide_ref,
+        dvc=wide_ref,
         p=V((heads, T, T), BF16),
         pc=V((heads, T, T), BF16),
         g=hidden_ref,
@@ -1014,6 +1177,8 @@
         y_recv=dma((units, B - 1, A)),
         z_send=dma((units, A)),
         z_recv=dma((units, A + 1)),
+        tz_send=dma((2, A)),
+        tz_recv=dma((2, A + 1)),
         m_gave=dma((3,)),
         m_got=dma((3, S)),
         m_send=dma((3, S, B + 1)),

time: 236 us -> 214 us (0.907)
  Pallas kernels: 233 us -> 212 us
    pallas_call x1, Pallas kernels: 230 us -> 209 us  [layer_call(): pl.pallas_call(kernel, out_shape=out_shape, in_specs=in_specs, out_specs=...]
where the time goes in v5:
time: 214 us
  Pallas kernels  212 us (99%)
  between operations  2.15 us (1%)
    pallas_call x1, Pallas kernels, layer_call(): pl.pallas_call(kernel, out_shape=out_shape, in_specs=in_specs, out_specs=...  209 us

profile of v5, /device:TPU:0, one launch (start us, length us, event | category | flops | bytes accessed | tf_op | source)
XLA Modules:
  0.0 213.9 jit_solution(13203078703970001685)
XLA Ops:
  1.9 208.8 %layer.1 = (f32[3,32]{1,0:T(4,128)}, f32[3,32]{1,0:T(4,128)}, f32[128,1024]{1,0:T(8,128)}, f32[128,1024]{1,0:T(8,128)}, bf16[128,1024]{1,0:T(8,128)(2,1)}, /*ind...) custom-call(bf16[128,1024]{1,0:T(8,128)(2,1)} %bitcast.8, ...), custom_call_target="tpu_custom_call" | custom-call | tf_op jit(solution)/shard_map/layer/pallas_call | solution.py:1204
  210.7 3.0 %keep.1 = (bf16[1,128,1024]{2,1,0:T(8,128)(2,1)}, f32[1,128,1024]{2,1,0:T(8,128)}, f32[1,128,1024]{2,1,0:T(8,128)}, f32[3,128,256]{2,1,0:T(8,128)}, f32[128,256]...) custom-call(bf16[1,128,1024]{2,1,0:T(8,128)(2,1)} %bitcast.11, ...), custom_call_target="tpu_custom_call" | custom-call | tf_op jit(solution)/shard_map/keep/pallas_call | solution.py:1235

commit v6 on v5

--- a/solution.py
+++ b/solution.py
@@ -14,8 +14,8 @@
 SELF, SELF_OUT, CROSS, CROSS_OUT, UP, DOWN = range(6)
 MOVED = (SELF_OUT, CROSS_OUT, DOWN)
 QUARTERS = 4
-UNITS = tuple((g, n) for g, count in ((SELF, 3), (CROSS, 3), (UP, QUARTERS)) for n in range(count))
-SELF_UNITS, CROSS_UNITS, UP_UNITS = (0, 1, 2), (3, 4, 5), (6, 7, 8, 9)
+UNITS = ((SELF, 0), (SELF, 1), (SELF, 2), (CROSS, None), *((UP, n) for n in range(QUARTERS)))
+SELF_UNITS, CROSS_UNITS, UP_UNITS = (0, 1, 2), (3,), (4, 5, 6, 7)
 G_TOKENS, G_MEMORY, G_COT, G_A2, G_A3, G_DZ2, G_DZ1 = range(7)
 R_CHAIN, R_MIXED, R_MEMORY = range(3)
 LANES = 128
@@ -52,7 +52,7 @@
 def layer_kernel(A, B, S, r):
     r.dz1 = r.a3
     r.part = [r.chain_part, r.dz2, r.a2]
-    ins, w, grad, outs = r.ins, r.w, r.grad, r.outs
+    ins, w, grad, outs = r.ins, r.w, r.grad, r.sums
     page, seq = lax.axis_index("page"), lax.axis_index("seq")
     a, b = lax.div(page, B), lax.rem(page, B)
     R = A * B // S
@@ -200,8 +200,8 @@
             remote(
                 r.small.at[i],
                 r.small_got.at[i, base + k - 1],
-                r.sm_send.at[i, base + k - 1],
-                r.sm_recv.at[i, base + k - 1],
+                r.sm_send.at[base + k - 1],
+                r.sm_recv.at[base + k - 1],
                 device(k),
             )
             for k in range(1, count)
@@ -224,20 +224,33 @@
         g, n = UNITS[u]
         size = ins[g].shape[-2]
         at = rows_at(j * size, size)
-        return arrays[g].at[at, n * Fq : (n + 1) * Fq] if g == UP else arrays[g].at[n, at, :]
+        if g == UP:
+            return arrays[g].at[at, n * Fq : (n + 1) * Fq]
+        return arrays[g].at[:, at, :] if n is None else arrays[g].at[n, at, :]
 
     def whole_of(arrays, u):
         g, n = UNITS[u]
-        return arrays[g].at[:, n * Fq : (n + 1) * Fq] if g == UP else arrays[g].at[n]
+        if g == UP:
+            return arrays[g].at[:, n * Fq : (n + 1) * Fq]
+        return arrays[g] if n is None else arrays[g].at[n]
 
     turned = UP_UNITS[2:] if B == 2 else ()
     turned_back = UP_UNITS[3:] if B == 2 else ()
     beside = a * B + 1 - b
+    inside = (a > 0) & (a < A - 1)
+
+    def w_slot(u, j, way):
+        t, e = lax.div(j, B), lax.rem(j, B)
+        if way < 2:
+            side = jnp.where(e == b, 0, A + 1) if u in turned else 0
+            return r.w_send.at[u, side + jnp.where((t == a) & (way == 1), A, t)]
+        base = 2 * (A + 1)
+        return r.w_send.at[u, base + (t if B == 2 else jnp.where((e == b) & (way == 3), A * B + t, j))]
 
     def w_copy(u, j, way, src=None):
         place = rows_of(w, u, j)
         device = (page + (-B, B, -1, 1)[way], seq)
-        return remote(place if src is None else src, place, r.w_send.at[u, j, way], r.w_recv.at[u, j], device)
+        return remote(place if src is None else src, place, w_slot(u, j, way), r.w_recv.at[u, j], device)
 
     ways = (a > 0, a < A - 1, b > 0, b < B - 1)
 
@@ -261,10 +274,10 @@
             landed(rows_of(w, u, beside), r.w_recv.at[u, beside])
             w_forward(u, beside, (0, 1))
 
-    def w_step(d, *units):
+    def w_step(d, *units, on=True):
         for u in units:
             for sign, way in ((-1, 1), (1, 0)):
-                @pl.when((a + sign * d >= 0) & (a + sign * d < A))
+                @pl.when((a + sign * d >= 0) & (a + sign * d < A) & on)
                 def _():
                     for column in (page, beside) if u in turned else (page,):
                         j = column + sign * d * B
@@ -349,11 +362,10 @@
 
             m_forward(g, n)
 
-    inside = (a > 0) & (a < A - 1)
     hops = jnp.abs(a - a0)
 
-    def m_pass(g, n, hop):
-        @pl.when(holds & (hops == hop))
+    def m_pass(g, n, hop, where):
+        @pl.when(holds & (hops == hop) & where)
         def _():
             landed(block(w[g], g, mine, n), r.m_recv.at[MOVED.index(g), mine, n])
             m_forward(g, n)
@@ -526,14 +538,19 @@
             def _():
                 z_copy(u, t, jnp.where(t > a, 1, -1)).wait_send()
 
-    def f_copy(g, k, n):
+    def f_parts(g):
+        return max(QUARTERS // R, 1) if g == DOWN else 1
+
+    def f_copy(g, k, n, part):
         i = MOVED.index(g)
         other = lax.rem(b + k, B)
+        rows, cols = ins[g].shape
+        size = rows // f_parts(g)
         return remote(
-            block(grad[g], g, other - b0, n),
-            r.fb[i].at[B - 1 - k, n],
-            r.f_send.at[i, k - 1, n],
-            r.f_recv.at[i, B - 1 - k, n],
+            grad[g].at[rows_at((other - b0) * rows + part * size, size), rows_at(n * cols, cols)],
+            r.fb[i].at[B - 1 - k, n, part * size : (part + 1) * size, :],
+            r.f_send[i].at[k - 1, n, part],
+            r.f_recv[i].at[B - 1 - k, n, part],
             (a * B + other, seq),
         )
 
@@ -541,12 +558,13 @@
         shelf_of = lax.rem(b + k, B) - b0
         return (shelf_of >= 0) & (shelf_of < R)
 
-    def f_start(g):
+    def f_start(g, ready=lambda part: True):
         for n in range(S):
             for k in range(1, B):
-                @pl.when(wanted(k))
-                def _():
-                    f_copy(g, k, n).start()
+                for part in range(f_parts(g)):
+                    @pl.when(wanted(k) & ready((lax.rem(b + k, B) - b0) * f_parts(g) + part))
+                    def _():
+                        f_copy(g, k, n, part).start()
 
     inward = jnp.where(a > a0, -1, 1)
     from_out = holds & (a != a0) & inside
@@ -570,7 +588,8 @@
         def _():
             total = block(grad[g], g, mine, n)[...].astype(F32)
             for slot in range(B - 1):
-                landed(r.fb[i].at[slot, n], r.f_recv.at[i, slot, n])
+                for part in range(f_parts(g)):
+                    f_copy(g, B - 1 - slot, n, part).wait_recv()
                 total = total + r.fb[i][slot, n].astype(F32)
             r.fb[i][0, n] = total.astype(BF16)
 
@@ -626,9 +645,10 @@
     def v_sent(g):
         for n in range(S):
             for k in range(1, B):
-                @pl.when(wanted(k))
-                def _():
-                    f_copy(g, k, n).wait_send()
+                for part in range(f_parts(g)):
+                    @pl.when(wanted(k))
+                    def _():
+                        f_copy(g, k, n, part).wait_send()
 
             @pl.when(starts_line | from_out)
             def _():
@@ -717,13 +737,11 @@
     def norm_own(k, values, dst, ch):
         dst[part_of(seq, ch), :] = (normed(values)[0] * gains(k) + biases(k)).astype(BF16)
 
-    tile = min(256, Fl)
-    tiles = Fl // tile
-
     few = r.norm_gains.shape[1]
     at_feature = lax.broadcasted_iota(jnp.int32, (few, D), 1)
     placed = at_feature == lax.broadcasted_iota(jnp.int32, (few, D), 0) + (page * S + seq) * few
     plan = []
+    SLOW = 5
 
     def when(time, *steps):
         plan.extend((time, step) for step in steps)
@@ -735,19 +753,38 @@
 
         return run
 
-    def w_moved(g, first, hop_time, gap):
+    results = [
+        (r.own_mixed, r.mixed),
+        (r.own_input_grad, r.input_grad),
+        (r.own_memory_grad, r.memory_grad),
+        *((r.sums[g], r.outs[g]) for g in MOVED),
+        *((whole_of(r.sums, u), whole_of(r.outs, u)) for u in range(len(UNITS))),
+    ]
+    O_MIXED, O_INPUT, O_MEMORY, O_MOVED, O_UNITS = 0, 1, 2, 3, 6
+
+    def leave(n):
+        kept, out = results[n]
+        return pltpu.make_async_copy(kept, out, r.o_sem.at[n])
+
+    def w_moved(g, first, hop_time, gap, end_first, end_gap):
+        ends = jnp.logical_not(inside)
         for n in range(S):
             when(first + n * gap, lambda n=n: m_first(g, n))
             for hop in range(1, A):
-                when(first + n * gap + hop * hop_time, lambda n=n, hop=hop: m_pass(g, n, hop))
-
-    def g_moved(g, first, hop_time, gap, late):
+                time = first + n * gap + hop * hop_time
+                if hop < A - 1:
+                    when(time, lambda n=n, hop=hop: m_pass(g, n, hop, inside))
+                if hop > 1:
+                    time = end_first + n * end_gap + hop / 10
+                when(time, lambda n=n, hop=hop: m_pass(g, n, hop, ends))
+
+    def g_moved(g, first, hop_time, gap, late, last):
         for n in range(S):
             time = first + n * gap
             when(time, lambda n=n: f_sum(g, n))
             for hop in range(1, A - 1):
-                when(time + late + hop * hop_time, lambda n=n, hop=hop: v_sum(g, n, hop))
-            when(time + late + (A - 1) * hop_time, lambda n=n: v_total(g, n))
+                when(time + late + hop * hop_time + (hop - 1) * SLOW, lambda n=n, hop=hop: v_sum(g, n, hop))
+            when(last, lambda n=n: v_total(g, n))
 
     def g_units(units, first, hop_time, gap, late):
         for place, u in enumerate(units):
@@ -756,9 +793,9 @@
                 when(time + gap * m, lambda m=m, u=u: y_sum(m, u))
             for m in range(A - 2):
                 when(time + gap * m + late + hop_time, lambda m=m, u=u: z_sum(m, u))
-            after = time + late + 2 * hop_time
+            after = time + late + 2 * hop_time + SLOW
             when(max(after, time + gap * (A - 2)), lambda u=u: z_sum(A - 2, u))
-            when(max(after + gap, time + gap * (A - 1)), lambda u=u: z_total(u))
+            when(188, lambda u=u: z_total(u), lambda u=u: leave(O_UNITS + u).start())
 
     given = (
         (G_TOKENS, r.tokens, r.all_tokens), (G_MEMORY, r.memory, r.all_memory), (G_COT, r.cotangent, r.dyr)
@@ -771,6 +808,7 @@
         r.small[0, 3:6, :] = nn(r.norm_biases[...], placed.astype(F32).astype(BF16))
         small_start(0, 0)
         w_first(*SELF_UNITS)
+        w_first(*turned, along=(2, 3))
         m_collect(SELF_OUT)
         ag_begin(*given[0])
         for load in loads:
@@ -837,52 +875,79 @@
         norm_own(2, r.x2[rows, :], r.a3, ch)
         ag_start(G_A3, r.a3.at[own], r.a3, ch)
 
-    def hidden():
-        w_wait(*UP_UNITS)
-        ag_wait(G_A3, r.a3)
-
-        @pl.loop(0, tiles)
+    def hidden_units(lo, hi):
+        @pl.loop(lo, hi)
         def _(n):
-            cols = rows_at(far_first(n) * tile, tile)
+            cols = rows_at(n * Fq, Fq)
             out, slope = gelu_pair(nn(r.a3[...], w[UP][:, cols]))
             r.g[:, cols] = out.astype(BF16)
             r.slope[:, cols] = slope
+
+    def down_grad(lo, hi):
+        @pl.loop(lo, hi)
+        def _(n):
+            cols = rows_at(n * Fq, Fq)
             grad[DOWN][cols, :] = tn(r.g[:, cols], r.dyr[...]).astype(BF16)
 
-            @pl.when(n == tiles * (R - 1) // R - 1)
-            def _():
-                f_start(DOWN)
-
-    def far_first(n):
-        shelf_last = jnp.where(holds, mine + 1, 0) * (tiles // R)
-        return lax.rem(n + shelf_last, tiles)
+    def hidden_grad(lo, hi):
+        @pl.loop(lo, hi)
+        def _(n):
+            cols = rows_at(n * Fq, Fq)
+            r.du[:, cols] = (nt(r.dyr[...], w[DOWN][cols, :]) * r.slope[:, cols]).astype(BF16)
+
+    def up_grad(lo, hi):
+        if lo < hi:
+            @pl.loop(0, D // 256)
+            def _(n):
+                cols = rows_at(n * 256, 256)
+                grad[UP][cols, lo * Fq : hi * Fq] = tn(r.a3[:, cols], r.du[:, lo * Fq : hi * Fq]).astype(BF16)
+
+    ahead = QUARTERS - len(turned)
+
+    def hidden():
+        w_wait(*UP_UNITS[:ahead])
+        ag_wait(G_A3, r.a3)
+        hidden_units(0, ahead)
+        down_grad(0, ahead)
+
+    def hidden_rest():
+        if turned:
+            for d in range(1, A):
+                w_step(d, *turned, on=jnp.logical_not(inside))
+            w_wait(*turned)
+            f_start(DOWN, lambda part: part < ahead)
+            hidden_units(ahead, QUARTERS)
+            down_grad(ahead, QUARTERS)
+            f_start(DOWN, lambda part: part >= ahead)
+        else:
+            f_start(DOWN)
 
     straight = tuple(u for u in UP_UNITS if u not in turned)
     when(0, begin)
     when(6, lambda: w_step(1, *SELF_UNITS))
     when(8, lambda: small_next(0, 0), lambda: m_collect(CROSS_OUT), lambda: ag_begin(*given[1]), lambda: m_collect(DOWN))
     when(12, lambda: w_step(2, *SELF_UNITS))
-    w_moved(SELF_OUT, 13, 4, 0.1)
+    w_moved(SELF_OUT, 13, 4, 0.1, 25, 0.1)
     when(15, lambda: small_next(0, 1), lambda: ag_forward(G_TOKENS, r.all_tokens), lambda: ag_begin(*given[2]))
     when(16.5, lambda: w_step(3, *SELF_UNITS))
-    when(17.5, lambda: w_first(*CROSS_UNITS))
-    when(21, lambda: w_first(*turned, along=(2, 3)))
+    when(17.5, lambda: w_first(*CROSS_UNITS, along=(2, 3)))
+    when(17.5, lambda: w_first(*CROSS_UNITS, along=(0, 1)))
     when(22, lambda: w_first(*straight))
     when(23.5, lambda: w_step(1, *CROSS_UNITS))
     when(24.5, take_tokens)
     when(27, self_project)
     when(29, lambda: w_step(2, *CROSS_UNITS))
-    w_moved(CROSS_OUT, 30, 5, 0.1)
+    w_moved(CROSS_OUT, 30, 5, 0.1, 46, 0.1)
     when(31, lambda: ag_forward(G_MEMORY, r.all_memory))
     when(32, lambda: attend(r.q, r.k, r.v, r.o, r.p, token_live, True))
     when(34.5, lambda: w_step(3, *CROSS_UNITS))
     when(36, self_sum)
     when(37, lambda: w_step(1, *straight))
-    w_moved(DOWN, 37.5, 7.5, 4.5)
+    w_moved(DOWN, 37.5, 7.5, 3, 60, 5)
     when(42, lambda: ag_forward(G_COT, r.dyr))
     when(43, lambda: w_step(2, *straight))
     when(46, self_add)
-    when(47, lambda: w_first(*turned, along=(0, 1)))
+    when(51, lambda: w_first(*turned, along=(0, 1)))
     when(48, memory_project)
     when(49, lambda: w_step(3, *straight))
     when(50, lambda: w_turn(*turned))
@@ -890,41 +955,28 @@
     when(53.2, cross_project)
     when(54, lambda: attend(r.qc, r.kc, r.vc, r.oc, r.pc, patch_live, False))
     when(57, cross_sum)
-    when(58, lambda: w_step(1, *turned))
+    when(62, lambda: w_step(1, *turned, on=inside))
     when(61, take_cotangent)
     when(67, cross_add)
-    when(66, lambda: w_step(2, *turned))
-    when(73, lambda: w_step(3, *turned))
+    when(69, lambda: w_step(2, *turned, on=inside))
     when(75, lambda: ag_forward(G_A3, r.a3))
-    when(78, hidden)
+    when(76, hidden)
+    when(84, hidden_rest)
 
     def hidden_back():
         m_wait(DOWN)
-
-        @pl.loop(0, tiles)
-        def _(n):
-            cols = rows_at(n * tile, tile)
-            r.du[:, cols] = (nt(r.dyr[...], w[DOWN][cols, :]) * r.slope[:, cols]).astype(BF16)
-
-        straight_columns = (QUARTERS - len(turned_back)) * Fq
-        for part in (slice(straight_columns, Fl), slice(0, straight_columns)):
-            if part.start == part.stop:
-                continue
-
-            @pl.loop(0, D // 256)
-            def _(n):
-                cols = rows_at(n * 256, 256)
-                grad[UP][cols, part] = tn(r.a3[:, cols], r.du[:, part]).astype(BF16)
-
-            if part.start:
-                for u in turned_back:
-                    c_first(u)
-        y_start(*UP_UNITS[: QUARTERS - len(turned_back)])
-
-    def hidden_sum():
+        hidden_grad(QUARTERS - len(turned_back), QUARTERS)
+        up_grad(QUARTERS - len(turned_back), QUARTERS)
+        for u in turned_back:
+            c_first(u)
+        hidden_grad(0, QUARTERS - len(turned_back))
         ag_sent(G_A3, r.a3.at[own], r.a3)
         rs_sent(R_CHAIN)
         rs_start(R_CHAIN, lambda at: nt(r.du[at, :], w[UP][...]))
+
+    def up_grad_rest():
+        up_grad(0, QUARTERS - len(turned_back))
+        y_start(*UP_UNITS[: QUARTERS - len(turned_back)])
 
     @each_row_part
     def hidden_add(ch, rows):
@@ -979,7 +1031,7 @@
     @each_row_part
     def input_add(ch, rows):
         back_term = norm_back(0, r.all_tokens[part_of(seq, ch), :].astype(F32), rs_wait(R_CHAIN, ch), ch)
-        r.input_grad[rows, :] = r.dx1[rows, :] + back_term
+        r.own_input_grad[rows, :] = r.dx1[rows, :] + back_term
 
     def small_last():
         r.small[1] = r.norm_terms[...]
@@ -991,12 +1043,12 @@
 
     @each_row_part
     def memory_add(ch, rows):
-        r.memory_grad[rows, :] = rs_wait(R_MEMORY, ch)
+        r.own_memory_grad[rows, :] = rs_wait(R_MEMORY, ch)
 
     @each_row_part
     def mixed_add(ch, rows):
         live_row = (seq * Tl + ch * half + lax.broadcasted_iota(jnp.int32, (half, 1), 0)) < token_live
-        r.mixed[rows, :] = jnp.where(live_row, r.x2[rows, :] + rs_wait(R_MIXED, ch), 0.0).astype(BF16)
+        r.own_mixed[rows, :] = jnp.where(live_row, r.x2[rows, :] + rs_wait(R_MIXED, ch), 0.0).astype(BF16)
 
     def norms_out():
         small_wait(1, 0)
@@ -1011,45 +1063,48 @@
         r.biases_grad[...] = picked[3:6]
 
     when(87, hidden_back)
-    when(91, hidden_sum)
+    when(95, up_grad_rest)
     if turned_back:
         when(99, lambda: c_sum(0, UP_UNITS[3]))
         when(102, lambda: c_sum(1, UP_UNITS[3]))
-        when(104, lambda: c_sum(2, UP_UNITS[3]))
-        when(110, lambda: c_total(UP_UNITS[3]))
-        when(138, lambda: c_end(UP_UNITS[3]))
-        g_moved(DOWN, 97, 7.2, 5.6, 5)
-        g_units(UP_UNITS[:3], 120.5, 4.5, 4.2, 7)
+        when(105, lambda: c_sum(2, UP_UNITS[3]))
+        when(112, lambda: c_total(UP_UNITS[3]))
+        when(142, lambda: c_end(UP_UNITS[3]), lambda: leave(O_UNITS + UP_UNITS[3]).start())
+        g_moved(DOWN, 98, 7.2, 5.6, 4, 155)
+        g_units(UP_UNITS[:3], 121, 4.5, 4.2, 7)
     else:
-        g_moved(DOWN, 97, 7.2, 5.6, 0)
-        g_units(UP_UNITS, 120.5, 4.5, 5.6, 0)
-    when(102, hidden_add)
-    when(106.5, lambda: ag_forward(G_DZ2, r.dz2))
-    when(108.5, cross_back)
-    when(114, cross_back_sum)
-    when(116, cross_grad)
-    when(124, cross_back_add)
-    when(130, lambda: ag_forward(G_DZ1, r.dz1))
-    when(132, self_back)
-    when(137, self_back_sum)
-    g_moved(CROSS_OUT, 134, 3.2, 1.4, 6)
-    when(142, memory_sum)
-    g_units(CROSS_UNITS, 141.5, 6, 4.2, 4)
-    when(146, input_add)
-    when(147, small_last)
-    when(150, mixed_sum)
-    when(152, lambda: small_next(1, 2))
-    when(154, memory_add)
-    g_moved(SELF_OUT, 157, 3.2, 1.4, 2)
-    when(162, lambda: small_next(1, 1))
-    when(166, mixed_add)
-    g_units(SELF_UNITS, 168, 6, 4.2, 0)
-    when(177, lambda: s_wait(DOWN), lambda: s_wait(CROSS_OUT))
-    when(181, lambda: s_wait(SELF_OUT), norms_out)
+        g_moved(DOWN, 97, 7.2, 5.6, 0, 155)
+        g_units(UP_UNITS, 121, 4.5, 5.6, 0)
+    when(103, hidden_add)
+    when(109, lambda: ag_forward(G_DZ2, r.dz2))
+    when(111, cross_back)
+    when(117, cross_back_sum)
+    when(119, cross_grad)
+    when(126.5, cross_back_add)
+    when(132.5, lambda: ag_forward(G_DZ1, r.dz1))
+    when(134.5, self_back)
+    when(140.5, self_back_sum)
+    g_moved(CROSS_OUT, 138, 3.2, 1.4, 4, 172)
+    when(145, memory_sum)
+    g_units(CROSS_UNITS, 144, 6, 4.2, 4)
+    when(149, input_add, lambda: leave(O_INPUT).start())
+    when(150, small_last)
+    when(153, mixed_sum)
+    when(160, lambda: small_next(1, 2))
+    when(179, memory_add, lambda: leave(O_MEMORY).start())
+    g_moved(SELF_OUT, 159, 3.2, 1.4, 2, 182)
+    when(177, lambda: small_next(1, 1))
+    when(179, mixed_add, lambda: leave(O_MIXED).start())
+    g_units(SELF_UNITS, 166, 6, 4.2, 0)
+    for time, g in ((179, DOWN), (179, CROSS_OUT), (190, SELF_OUT)):
+        when(time, lambda g=g: s_wait(g), lambda g=g: leave(O_MOVED + MOVED.index(g)).start())
+    when(190, norms_out)
 
     for _, step in sorted(plan, key=lambda entry: entry[0]):
         step()
 
+    for n in range(len(results)):
+        leave(n).wait()
     for i in (R_CHAIN, R_MIXED, R_MEMORY):
         rs_sent(i)
     for i, piece, everyone in given[:2]:
@@ -1086,7 +1141,9 @@
     dma = pltpu.SemaphoreType.DMA
     small_slots = S + A + B - 3
     units = len(UNITS)
-    pieces = [(shards[g][0], Fl // QUARTERS) if g == UP else shards[g][1:] for g, _ in UNITS]
+    pieces = [
+        (shards[g][0], Fl // QUARTERS) if g == UP else shards[g] if n is None else shards[g][1:] for g, n in UNITS
+    ]
     turn = pieces[-1]
     if B == 2:
         pieces[-1] = (16, LANES)
@@ -1160,6 +1217,10 @@
         dv_sum=V((T, LANES), F32),
         chain_part=row_ref,
         got=[V((S - 1, Tl, D), BF16)] * 3,
+        own_mixed=V((Tl, D), BF16),
+        own_input_grad=own_ref,
+        own_memory_grad=own_ref,
+        sums=[V(s, F32) for s in shards],
         small=V((2, 8, D), F32),
         small_got=V((2, small_slots, 8, D), F32),
         norm_terms=V((8, D), F32),
@@ -1167,10 +1228,11 @@
         ag_recv=dma((7, 2, S)),
         rs_send=dma((3, 2, S - 1)),
         rs_recv=dma((3, 2, S - 1)),
-        sm_send=dma((2, small_slots)),
-        sm_recv=dma((2, small_slots)),
+        sm_send=dma((small_slots,)),
+        sm_recv=dma((small_slots,)),
         ld_sem=dma((3,)),
-        w_send=dma((units, pages, 4)),
+        o_sem=dma((units + 6,)),
+        w_send=dma((units, 2 * (A + 1) + (A if B == 2 else pages + A))),
         w_recv=dma((units, pages)),
         w_local=dma((units,)),
         y_send=dma((units, B - 1, A)),
@@ -1183,8 +1245,8 @@
         m_got=dma((3, S)),
         m_send=dma((3, S, B + 1)),
         m_recv=dma((3, R, S)),
-        f_send=dma((3, B - 1, S)),
-        f_recv=dma((3, B - 1, S)),
+        f_send=[dma((B - 1, S, max(QUARTERS // R, 1) if g == DOWN else 1)) for g in MOVED],
+        f_recv=[dma((B - 1, S, max(QUARTERS // R, 1) if g == DOWN else 1)) for g in MOVED],
         v_send=dma((3, S)),
         v_recv=dma((3, 2, S)),
         s_send=dma((3, S)),
@@ -1205,7 +1267,7 @@
         kernel,
         out_shape=out_shape,
         in_specs=in_specs,
-        out_specs=[vmem] * len(out_shape),
+        out_specs=[vmem if s.shape == norms[0].shape else hbm for s in out_shape],
         scratch_shapes=scratch_shapes,
         compiler_params=pltpu.CompilerParams(
             collective_id=0, has_side_effects=True, vmem_limit_bytes=62 * 2**20

time: 214 us -> 200 us (0.935); the launches traced: 214 us -> 197 us
  Pallas kernels: 212 us -> 195 us
    pallas_call x1, Pallas kernels: 209 us -> 192 us  [layer_call(): pl.pallas_call(kernel, out_shape=out_shape, in_specs=in_specs, out_specs=...]
where the time goes in v6:
time: 200 us; the launch traced here: 197 us
  Pallas kernels  195 us (98%)
  between operations  2.13 us (1%)
    pallas_call x1, Pallas kernels, layer_call(): pl.pallas_call(kernel, out_shape=out_shape, in_specs=in_specs, out_specs=...  192 us

profile of v6, /device:TPU:0, one launch (start us, length us, event | category | flops | bytes accessed | tf_op | source)
XLA Modules:
  0.0 197.0 jit_solution(1757051687103051303)
XLA Ops:
  1.9 191.8 %layer.1 = (f32[3,32]{1,0:T(4,128)}, f32[3,32]{1,0:T(4,128)}, f32[128,1024]{1,0:T(8,128)}, f32[128,1024]{1,0:T(8,128)}, bf16[128,1024]{1,0:T(8,128)(2,1)}, /*ind...) custom-call(bf16[128,1024]{1,0:T(8,128)(2,1)} %bitcast.8, ...), custom_call_target="tpu_custom_call" | custom-call | tf_op jit(solution)/shard_map/layer/pallas_call | solution.py:1266
  193.8 3.0 %keep.1 = (bf16[1,128,1024]{2,1,0:T(8,128)(2,1)}, f32[1,128,1024]{2,1,0:T(8,128)}, f32[1,128,1024]{2,1,0:T(8,128)}, f32[3,128,256]{2,1,0:T(8,128)}, f32[128,256]...) custom-call(bf16[1,128,1024]{2,1,0:T(8,128)(2,1)} %bitcast.11, ...), custom_call_target="tpu_custom_call" | custom-call | tf_op jit(solution)/shard_map/keep/pallas_call | solution.py:1297

commit v7 on v6

--- a/solution.py
+++ b/solution.py
@@ -14,8 +14,9 @@
 SELF, SELF_OUT, CROSS, CROSS_OUT, UP, DOWN = range(6)
 MOVED = (SELF_OUT, CROSS_OUT, DOWN)
 QUARTERS = 4
-UNITS = ((SELF, 0), (SELF, 1), (SELF, 2), (CROSS, None), *((UP, n) for n in range(QUARTERS)))
-SELF_UNITS, CROSS_UNITS, UP_UNITS = (0, 1, 2), (3,), (4, 5, 6, 7)
+UNITS = ((SELF, 0), (SELF, 1), (SELF, 2), (CROSS, None), (UP, (0, 2)), (UP, (2, 4)))
+BACK_UNITS = ((SELF, 0), (SELF, 1), (SELF, 2), (CROSS, None), (UP, (0, 3)), (UP, (3, 4)))
+SELF_UNITS, CROSS_UNITS, UP_UNITS = (0, 1, 2), (3,), (4, 5)
 G_TOKENS, G_MEMORY, G_COT, G_A2, G_A3, G_DZ2, G_DZ1 = range(7)
 R_CHAIN, R_MIXED, R_MEMORY = range(3)
 LANES = 128
@@ -95,43 +96,47 @@
     sibling = chip * 2 + 1 - core
     half = Tl // 2
 
-    def part_of(source, ch):
-        return rows_at(source * Tl + ch * half, half)
+    def part_of(source, ch, parts=2):
+        size = Tl // parts
+        return rows_at(source * Tl + ch * size, size)
+
+    def parts_of(i):
+        return 1 if i <= G_COT else 2
 
     def chip_at(dx):
         return lax.rem(chip + dx, X)
 
     def ag_copy(i, src, dst, ch, n):
         source = chip_at(2 * X - 1 - n) * 2 + core if n >= X else seq
-        mine = dst.at[part_of(source, ch)] if n >= X else src.at[rows_at(ch * half, half)]
+        parts = parts_of(i)
+        mine = dst.at[part_of(source, ch, parts)] if n >= X else src.at[rows_at(ch * (Tl // parts), Tl // parts)]
         to = chip_at(n) * 2 + core if 0 < n < X else sibling
-        return remote(
-            mine, dst.at[part_of(source, ch)], r.ag_send.at[i, ch, n], r.ag_recv.at[i, ch, source], (page, to)
-        )
+        place = dst.at[part_of(source, ch, parts)]
+        return remote(mine, place, r.ag_send[i].at[ch, n], r.ag_recv[i].at[ch, source], (page, to))
 
     def ag_start(i, src, dst, ch):
         for n in (*range(1, X), 0):
             ag_copy(i, src, dst, ch, n).start()
 
     def ag_begin(i, src, dst):
-        for ch in range(2):
+        for ch in range(parts_of(i)):
             ag_start(i, src, dst, ch)
 
     def ag_forward(i, dst):
-        for ch in range(2):
+        for ch in range(parts_of(i)):
             for n in range(X, 2 * X - 1):
                 source = chip_at(2 * X - 1 - n) * 2 + core
-                landed(dst.at[part_of(source, ch)], r.ag_recv.at[i, ch, source])
+                landed(dst.at[part_of(source, ch, parts_of(i))], r.ag_recv[i].at[ch, source])
                 ag_copy(i, None, dst, ch, n).start()
 
     def ag_wait(i, dst):
-        for ch in range(2):
+        for ch in range(parts_of(i)):
             for x in range(X):
                 source = 2 * x + 1 - core
-                landed(dst.at[part_of(source, ch)], r.ag_recv.at[i, ch, source])
+                landed(dst.at[part_of(source, ch, parts_of(i))], r.ag_recv[i].at[ch, source])
 
     def ag_sent(i, src, dst):
-        for ch in range(2):
+        for ch in range(parts_of(i)):
             for n in range(2 * X - 1):
                 ag_copy(i, src, dst, ch, n).wait_send()
 
@@ -220,32 +225,37 @@
             total = total + r.small_got[i, base + k]
         r.small[i] = total
 
+    def unit_of(arrays, u):
+        g, n = (UNITS if arrays is w or arrays is ins else BACK_UNITS)[u]
+        return g, slice(n[0] * Fq, n[1] * Fq) if g == UP else n
+
     def rows_of(arrays, u, j):
-        g, n = UNITS[u]
+        g, n = unit_of(arrays, u)
         size = ins[g].shape[-2]
         at = rows_at(j * size, size)
         if g == UP:
-            return arrays[g].at[at, n * Fq : (n + 1) * Fq]
+            return arrays[g].at[at, n]
         return arrays[g].at[:, at, :] if n is None else arrays[g].at[n, at, :]
 
     def whole_of(arrays, u):
-        g, n = UNITS[u]
+        g, n = unit_of(arrays, u)
         if g == UP:
-            return arrays[g].at[:, n * Fq : (n + 1) * Fq]
+            return arrays[g].at[:, n]
         return arrays[g] if n is None else arrays[g].at[n]
 
-    turned = UP_UNITS[2:] if B == 2 else ()
-    turned_back = UP_UNITS[3:] if B == 2 else ()
+    turned = turned_back = UP_UNITS[1:] if B == 2 else ()
     beside = a * B + 1 - b
     inside = (a > 0) & (a < A - 1)
 
     def w_slot(u, j, way):
         t, e = lax.div(j, B), lax.rem(j, B)
+        over = A if B == 2 else A * B + A
+        base = u * (A + 1 + over)
         if way < 2:
-            side = jnp.where(e == b, 0, A + 1) if u in turned else 0
-            return r.w_send.at[u, side + jnp.where((t == a) & (way == 1), A, t)]
-        base = 2 * (A + 1)
-        return r.w_send.at[u, base + (t if B == 2 else jnp.where((e == b) & (way == 3), A * B + t, j))]
+            if u in turned:
+                base = jnp.where(e == b, base, len(UNITS) * (A + 1 + over))
+            return r.w_send.at[base + jnp.where((t == a) & (way == 1), A, t)]
+        return r.w_send.at[base + A + 1 + (t if B == 2 else jnp.where((e == b) & (way == 3), A * B + t, j))]
 
     def w_copy(u, j, way, src=None):
         place = rows_of(w, u, j)
@@ -902,10 +912,12 @@
                 cols = rows_at(n * 256, 256)
                 grad[UP][cols, lo * Fq : hi * Fq] = tn(r.a3[:, cols], r.du[:, lo * Fq : hi * Fq]).astype(BF16)
 
-    ahead = QUARTERS - len(turned)
+    straight = tuple(u for u in UP_UNITS if u not in turned)
+    ahead = UNITS[UP_UNITS[1]][1][0] if turned else QUARTERS
+    back_from = BACK_UNITS[UP_UNITS[1]][1][0] if turned_back else QUARTERS
 
     def hidden():
-        w_wait(*UP_UNITS[:ahead])
+        w_wait(*straight)
         ag_wait(G_A3, r.a3)
         hidden_units(0, ahead)
         down_grad(0, ahead)
@@ -922,7 +934,6 @@
         else:
             f_start(DOWN)
 
-    straight = tuple(u for u in UP_UNITS if u not in turned)
     when(0, begin)
     when(6, lambda: w_step(1, *SELF_UNITS))
     when(8, lambda: small_next(0, 0), lambda: m_collect(CROSS_OUT), lambda: ag_begin(*given[1]), lambda: m_collect(DOWN))
@@ -965,18 +976,18 @@
 
     def hidden_back():
         m_wait(DOWN)
-        hidden_grad(QUARTERS - len(turned_back), QUARTERS)
-        up_grad(QUARTERS - len(turned_back), QUARTERS)
+        hidden_grad(back_from, QUARTERS)
+        up_grad(back_from, QUARTERS)
         for u in turned_back:
             c_first(u)
-        hidden_grad(0, QUARTERS - len(turned_back))
+        hidden_grad(0, back_from)
         ag_sent(G_A3, r.a3.at[own], r.a3)
         rs_sent(R_CHAIN)
         rs_start(R_CHAIN, lambda at: nt(r.du[at, :], w[UP][...]))
 
     def up_grad_rest():
-        up_grad(0, QUARTERS - len(turned_back))
-        y_start(*UP_UNITS[: QUARTERS - len(turned_back)])
+        up_grad(0, back_from)
+        y_start(*(u for u in UP_UNITS if u not in turned_back))
 
     @each_row_part
     def hidden_add(ch, rows):
@@ -1065,13 +1076,13 @@
     when(87, hidden_back)
     when(95, up_grad_rest)
     if turned_back:
-        when(99, lambda: c_sum(0, UP_UNITS[3]))
-        when(102, lambda: c_sum(1, UP_UNITS[3]))
-        when(105, lambda: c_sum(2, UP_UNITS[3]))
-        when(112, lambda: c_total(UP_UNITS[3]))
-        when(142, lambda: c_end(UP_UNITS[3]), lambda: leave(O_UNITS + UP_UNITS[3]).start())
+        when(99, lambda: c_sum(0, UP_UNITS[1]))
+        when(102, lambda: c_sum(1, UP_UNITS[1]))
+        when(105, lambda: c_sum(2, UP_UNITS[1]))
+        when(112, lambda: c_total(UP_UNITS[1]))
+        when(142, lambda: c_end(UP_UNITS[1]), lambda: leave(O_UNITS + UP_UNITS[1]).start())
         g_moved(DOWN, 98, 7.2, 5.6, 4, 155)
-        g_units(UP_UNITS[:3], 121, 4.5, 4.2, 7)
+        g_units(UP_UNITS[:1], 122, 6, 4.2, 5)
     else:
         g_moved(DOWN, 97, 7.2, 5.6, 0, 155)
         g_units(UP_UNITS, 121, 4.5, 5.6, 0)
@@ -1092,7 +1103,7 @@
     when(153, mixed_sum)
     when(160, lambda: small_next(1, 2))
     when(179, memory_add, lambda: leave(O_MEMORY).start())
-    g_moved(SELF_OUT, 159, 3.2, 1.4, 2, 182)
+    g_moved(SELF_OUT, 159, 3.2, 1.4, 4, 183)
     when(177, lambda: small_next(1, 1))
     when(179, mixed_add, lambda: leave(O_MIXED).start())
     g_units(SELF_UNITS, 166, 6, 4.2, 0)
@@ -1142,7 +1153,8 @@
     small_slots = S + A + B - 3
     units = len(UNITS)
     pieces = [
-        (shards[g][0], Fl // QUARTERS) if g == UP else shards[g] if n is None else shards[g][1:] for g, n in UNITS
+        (shards[g][0], (n[1] - n[0]) * Fl // QUARTERS) if g == UP else shards[g] if n is None else shards[g][1:]
+        for g, n in BACK_UNITS
     ]
     turn = pieces[-1]
     if B == 2:
@@ -1224,15 +1236,15 @@
         small=V((2, 8, D), F32),
         small_got=V((2, small_slots, 8, D), F32),
         norm_terms=V((8, D), F32),
-        ag_send=dma((7, 2, S - 1)),
-        ag_recv=dma((7, 2, S)),
+        ag_send=[dma((1 if i <= G_COT else 2, S - 1)) for i in range(7)],
+        ag_recv=[dma((1 if i <= G_COT else 2, S)) for i in range(7)],
         rs_send=dma((3, 2, S - 1)),
         rs_recv=dma((3, 2, S - 1)),
         sm_send=dma((small_slots,)),
         sm_recv=dma((small_slots,)),
         ld_sem=dma((3,)),
         o_sem=dma((units + 6,)),
-        w_send=dma((units, 2 * (A + 1) + (A if B == 2 else pages + A))),
+        w_send=dma((units * (A + 1 + (A if B == 2 else pages + A)) + A + 1,)),
         w_recv=dma((units, pages)),
         w_local=dma((units,)),
         y_send=dma((units, B - 1, A)),

time: 200 us -> 199 us (level)
  no operation moved by 1% of the time
where the time goes in v7:
time: 199 us; the launch traced here: 196 us
  Pallas kernels  194 us (97%)
  between operations  2.13 us (1%)
    pallas_call x1, Pallas kernels, layer_call(): pl.pallas_call(kernel, out_shape=out_shape, in_specs=in_specs, out_specs=...  191 us

profile of v7, /device:TPU:0, one launch (start us, length us, event | category | flops | bytes accessed | tf_op | source)
XLA Modules:
  0.0 196.3 jit_solution(11575613878743024154)
XLA Ops:
  1.9 191.2 %layer.1 = (f32[3,32]{1,0:T(4,128)}, f32[3,32]{1,0:T(4,128)}, f32[128,1024]{1,0:T(8,128)}, f32[128,1024]{1,0:T(8,128)}, bf16[128,1024]{1,0:T(8,128)(2,1)}, /*ind...) custom-call(bf16[128,1024]{1,0:T(8,128)(2,1)} %bitcast.8, ...), custom_call_target="tpu_custom_call" | custom-call | tf_op jit(solution)/shard_map/layer/pallas_call | solution.py:1278
  193.2 3.0 %keep.1 = (bf16[1,128,1024]{2,1,0:T(8,128)(2,1)}, f32[1,128,1024]{2,1,0:T(8,128)}, f32[1,128,1024]{2,1,0:T(8,128)}, f32[3,128,256]{2,1,0:T(8,128)}, f32[128,256]...) custom-call(bf16[1,128,1024]{2,1,0:T(8,128)(2,1)} %bitcast.11, ...), custom_call_target="tpu_custom_call" | custom-call | tf_op jit(solution)/shard_map/keep/pallas_call | solution.py:1309

commit v8 on v7

--- a/solution.py
+++ b/solution.py
@@ -140,12 +140,15 @@
             for n in range(2 * X - 1):
                 ag_copy(i, src, dst, ch, n).wait_send()
 
+    def rs_parts(i):
+        return 2 if i == R_CHAIN else 1
+
     def rs_copy(i, x, ch):
         return remote(
-            r.part[i].at[part_of(x * 2 + 1 - core, ch)],
-            r.got[i].at[x, rows_at(ch * half, half)],
-            r.rs_send.at[i, ch, x],
-            r.rs_recv.at[i, ch, x],
+            r.part[i].at[part_of(x * 2 + 1 - core, ch, rs_parts(i))],
+            r.got[i].at[x, rows_at(ch * (Tl // rs_parts(i)), Tl // rs_parts(i))],
+            r.rs_send[i].at[ch, x],
+            r.rs_recv[i].at[ch, x],
             (page, sibling),
         )
 
@@ -153,10 +156,10 @@
         to = chip_at(dx) * 2 + core
         slot = X + dx - 1
         return remote(
-            r.part[i].at[part_of(to, ch)],
-            r.got[i].at[slot, rows_at(ch * half, half)],
-            r.rs_send.at[i, ch, slot],
-            r.rs_recv.at[i, ch, slot],
+            r.part[i].at[part_of(to, ch, rs_parts(i))],
+            r.got[i].at[slot, rows_at(ch * (Tl // rs_parts(i)), Tl // rs_parts(i))],
+            r.rs_send[i].at[ch, slot],
+            r.rs_recv[i].at[ch, slot],
             (page, to),
         )
 
@@ -166,30 +169,33 @@
             x = chip_at(n)
             at = rows_at((x * 2 + 1 - core) * Tl, Tl)
             part[at, :] = term(at).astype(BF16)
-            for ch in range(2):
+            for ch in range(rs_parts(i)):
                 rs_copy(i, x, ch).start()
         for dx in range(1, X):
             x = chip_at(dx)
             at = rows_at((x * 2 + core) * Tl, Tl)
             mine = term(at)
-            for ch in range(2):
+            for ch in range(rs_parts(i)):
                 rs_copy(i, x, ch).wait_recv()
-                other = got[x, ch * half : (ch + 1) * half, :].astype(F32)
-                part[part_of(x * 2 + core, ch), :] = (mine[ch * half : (ch + 1) * half] + other).astype(BF16)
+                rows = slice(ch * (Tl // rs_parts(i)), (ch + 1) * (Tl // rs_parts(i)))
+                other = got[x, rows, :].astype(F32)
+                part[part_of(x * 2 + core, ch, rs_parts(i)), :] = (mine[rows] + other).astype(BF16)
                 rs_far(i, dx, ch).start()
         part[own, :] = term(own).astype(BF16)
 
     def rs_wait(i, ch):
         rows = slice(ch * half, (ch + 1) * half)
-        rs_copy(i, chip, ch).wait_recv()
+        if ch < rs_parts(i):
+            rs_copy(i, chip, ch).wait_recv()
         total = r.part[i][part_of(seq, ch), :].astype(F32) + r.got[i][chip, rows, :].astype(F32)
         for dx in range(1, X):
-            rs_far(i, dx, ch).wait_recv()
+            if ch < rs_parts(i):
+                rs_far(i, dx, ch).wait_recv()
             total = total + r.got[i][X + dx - 1, rows, :].astype(F32)
         return total
 
     def rs_sent(i):
-        for ch in range(2):
+        for ch in range(rs_parts(i)):
             for x in range(X):
                 rs_copy(i, x, ch).wait_send()
             for dx in range(1, X):
@@ -1103,7 +1109,7 @@
     when(153, mixed_sum)
     when(160, lambda: small_next(1, 2))
     when(179, memory_add, lambda: leave(O_MEMORY).start())
-    g_moved(SELF_OUT, 159, 3.2, 1.4, 4, 183)
+    g_moved(SELF_OUT, 159, 3.2, 1.4, 6, 184)
     when(177, lambda: small_next(1, 1))
     when(179, mixed_add, lambda: leave(O_MIXED).start())
     g_units(SELF_UNITS, 166, 6, 4.2, 0)
@@ -1238,8 +1244,8 @@
         norm_terms=V((8, D), F32),
         ag_send=[dma((1 if i <= G_COT else 2, S - 1)) for i in range(7)],
         ag_recv=[dma((1 if i <= G_COT else 2, S)) for i in range(7)],
-        rs_send=dma((3, 2, S - 1)),
-        rs_recv=dma((3, 2, S - 1)),
+        rs_send=[dma((2 if i == R_CHAIN else 1, S - 1)) for i in range(3)],
+        rs_recv=[dma((2 if i == R_CHAIN else 1, S - 1)) for i in range(3)],
         sm_send=dma((small_slots,)),
         sm_recv=dma((small_slots,)),
         ld_sem=dma((3,)),

time: 199 us -> 198 us (level)
  no operation moved by 1% of the time
where the time goes in v8:
time: 198 us; the launch traced here: 197 us
  Pallas kernels  195 us (98%)
  between operations  2.13 us (1%)
    pallas_call x1, Pallas kernels, layer_call(): pl.pallas_call(kernel, out_shape=out_shape, in_specs=in_specs, out_specs=...  192 us

profile of v8, /device:TPU:0, one launch (start us, length us, event | category | flops | bytes accessed | tf_op | source)
XLA Modules:
  0.0 197.1 jit_solution(18414448561492974063)
XLA Ops:
  1.9 192.0 %layer.1 = (f32[3,32]{1,0:T(4,128)}, f32[3,32]{1,0:T(4,128)}, f32[128,1024]{1,0:T(8,128)}, f32[128,1024]{1,0:T(8,128)}, bf16[128,1024]{1,0:T(8,128)(2,1)}, /*ind...) custom-call(bf16[128,1024]{1,0:T(8,128)(2,1)} %bitcast.8, ...), custom_call_target="tpu_custom_call" | custom-call | tf_op jit(solution)/shard_map/layer/pallas_call | solution.py:1284
  193.9 3.0 %keep.1 = (bf16[1,128,1024]{2,1,0:T(8,128)(2,1)}, f32[1,128,1024]{2,1,0:T(8,128)}, f32[1,128,1024]{2,1,0:T(8,128)}, f32[3,128,256]{2,1,0:T(8,128)}, f32[128,256]...) custom-call(bf16[1,128,1024]{2,1,0:T(8,128)(2,1)} %bitcast.11, ...), custom_call_target="tpu_custom_call" | custom-call | tf_op jit(solution)/shard_map/keep/pallas_call | solution.py:1315
